TPU v7x, 128 devices: a whole 4x4x4 slice. The times are simulated.
128 devices in a mesh: section: 2 (over core), seq: 8 (over y, x_lo), mp: 8 (over x_hi, z).
Axes of the slice: x: 4 (x_hi: 2, x_lo: 2; x = x_hi * 2 + x_lo), y: 4, z: 4, core: 2. Of those that a mesh axis runs over, the one named last changes fastest.
Arguments:
- bottleneck: bfloat16 [2, 1024, 4096], P('section', ('seq', 'mp')), may hold values from -6 to 6
- qkv_weight: bfloat16 [3, 4096, 4096], P(None, None, ('section', 'mp')), may hold values from -0.2 to 0.2
- out_weight: bfloat16 [4096, 4096], P(('section', 'mp')), may hold values from -0.5 to 0.5
- up_weight: bfloat16 [4096, 16384], P(None, ('section', 'mp')), may hold values from -0.09375 to 0.09375
- down_weight: bfloat16 [16384, 4096], P(('section', 'mp')), may hold values from -0.046875 to 0.046875
- cotangent: bfloat16 [2, 1024, 4096], P('section', ('seq', 'mp')), may hold values from -6 to 6
Outputs:
- block_out: bfloat16 [2, 1024, 4096], P('section', ('seq', 'mp'))
- grad_input: bfloat16 [2, 1024, 4096], P('section', ('seq', 'mp'))
All inputs are finite; a program needn't handle non-finite values.
Results may differ from a plain program's by a relative error of at most 0.025.
Values may be sent and summed in bfloat16 or wider, within the bound.
No kernel may reach another device: no remote copies, remote signals or barrier semaphores. Data moves between devices by JAX's collectives and lax.ppermute only.
A program may use at most 128 MiB of HBM per device.

v0:
```python
import math

import jax
import jax.numpy as jnp
from jax import lax
from jax.sharding import PartitionSpec as P

HD = 128


norm_eps = 1e-06


def layer_norm(inputs):
    row_mean = jnp.mean(inputs, axis=-1, keepdims=True)
    centered = inputs - row_mean
    inv_std = lax.rsqrt(jnp.mean(centered * centered, axis=-1, keepdims=True) + norm_eps)
    return (centered * inv_std, inv_std)


def norm_backward(normed, inv_std, grad_in):
    mean_grad = jnp.mean(grad_in, axis=-1, keepdims=True)
    mean_mix = jnp.mean(grad_in * normed, axis=-1, keepdims=True)
    return inv_std * (grad_in - mean_grad - normed * mean_mix)


def gelu_value(pre_act):
    return pre_act * 0.5 * (1.0 + lax.erf(pre_act * 0.7071067811865476))


def gelu_slope(pre_act):
    cumul = 0.5 * (1.0 + lax.erf(pre_act * 0.7071067811865476))
    return cumul + pre_act * jnp.exp(-0.5 * pre_act * pre_act) * 0.3989422804014327


def per_device(bottleneck, qkv_weight, out_weight, up_weight, down_weight, cotangent):
    row_count = bottleneck.shape[1]
    model_width = bottleneck.shape[2]
    group_size = lax.axis_size(("section", "mp"))
    images = lax.axis_size("section")
    own_start = lax.axis_index(("section", "mp")) * row_count
    total_rows = group_size * row_count
    block_rows = total_rows // images
    head_cols = qkv_weight.shape[2]
    head_count = head_cols // HD
    score_scale = 1.0 / math.sqrt(HD)
    gathered = lax.all_gather(bottleneck, ("section", "mp"), axis=0, tiled=True).reshape(
        total_rows, model_width
    )
    normed_one, inv_one = layer_norm(gathered.astype(jnp.float32))
    projected = jnp.einsum(
        "td,kdf->ktf",
        normed_one.astype(jnp.bfloat16),
        qkv_weight,
        preferred_element_type=jnp.float32,
    ).astype(jnp.bfloat16)
    queries = projected[0].reshape(images, block_rows, head_cols)
    own_keys = projected[1].reshape(images, block_rows, head_cols)
    own_values = projected[2].reshape(images, block_rows, head_cols)
    all_keys, all_values = (
        lax.all_gather(own_keys, "seq", axis=1, tiled=True),
        lax.all_gather(own_values, "seq", axis=1, tiled=True),
    )
    length = all_keys.shape[1]
    query_heads = queries.reshape(images, block_rows, head_count, HD)
    key_heads = all_keys.reshape(images, length, head_count, HD)
    value_heads = all_values.reshape(images, length, head_count, HD)
    scores = (
        jnp.einsum("ilhd,imhd->ihlm", query_heads, key_heads, preferred_element_type=jnp.float32)
        * score_scale
    )
    row_max = jnp.max(scores, axis=-1)
    weights = jnp.exp(scores - row_max[..., None])
    totals = jnp.sum(weights, axis=-1)
    log_total = row_max + jnp.log(totals)
    mixed_values = jnp.einsum(
        "ihlm,imhd->ilhd",
        weights.astype(jnp.bfloat16),
        value_heads,
        preferred_element_type=jnp.float32,
    )
    attended = (mixed_values / jnp.transpose(totals, (0, 2, 1))[..., None]).astype(jnp.bfloat16)
    attended_flat = attended.reshape(total_rows, head_cols)
    attn_own = lax.psum_scatter(
        jnp.dot(attended_flat, out_weight, preferred_element_type=jnp.float32).astype(jnp.bfloat16),
        ("section", "mp"),
        scatter_dimension=0,
        tiled=True,
    ).astype(jnp.float32)
    resid_own = (bottleneck[0].astype(jnp.float32) + attn_own).astype(jnp.bfloat16)
    resid_all = lax.all_gather(resid_own, ("section", "mp"), axis=0, tiled=True)
    normed_two, inv_two = layer_norm(resid_all.astype(jnp.float32))
    hidden_pre = jnp.dot(
        normed_two.astype(jnp.bfloat16), up_weight, preferred_element_type=jnp.float32
    )
    hidden = gelu_value(hidden_pre).astype(jnp.bfloat16)
    ffn_own = lax.psum_scatter(
        jnp.dot(hidden, down_weight, preferred_element_type=jnp.float32).astype(jnp.bfloat16),
        ("section", "mp"),
        scatter_dimension=0,
        tiled=True,
    ).astype(jnp.float32)
    block_out = (resid_own.astype(jnp.float32) + ffn_own).astype(jnp.bfloat16)
    grad_all = lax.all_gather(cotangent, ("section", "mp"), axis=0, tiled=True).reshape(
        total_rows, model_width
    )
    grad_act = jnp.einsum("td,fd->tf", grad_all, down_weight, preferred_element_type=jnp.float32)
    grad_hidden = (grad_act * gelu_slope(hidden_pre)).astype(jnp.bfloat16)
    grad_norm_two = lax.psum_scatter(
        jnp.einsum("tf,df->td", grad_hidden, up_weight, preferred_element_type=jnp.float32).astype(
            jnp.bfloat16
        ),
        ("section", "mp"),
        scatter_dimension=0,
        tiled=True,
    ).astype(jnp.float32)
    normed_two_own = lax.dynamic_slice_in_dim(normed_two, own_start, row_count, 0)
    inv_two_own = lax.dynamic_slice_in_dim(inv_two, own_start, row_count, 0)
    grad_resid = (
        cotangent[0].astype(jnp.float32) + norm_backward(normed_two_own, inv_two_own, grad_norm_two)
    ).astype(jnp.bfloat16)
    grad_resid_all = lax.all_gather(grad_resid, ("section", "mp"), axis=0, tiled=True)
    grad_attn = jnp.einsum(
        "td,fd->tf", grad_resid_all, out_weight, preferred_element_type=jnp.float32
    ).astype(jnp.bfloat16)
    grad_attn_heads = grad_attn.reshape(images, block_rows, head_count, HD)
    row_delta = jnp.sum(grad_attn_heads.astype(jnp.float32) * attended.astype(jnp.float32), axis=-1)
    prob_rows = jnp.exp(scores - log_total[..., None])
    grad_probs = jnp.einsum(
        "ilhd,imhd->ihlm", grad_attn_heads, value_heads, preferred_element_type=jnp.float32
    )
    grad_scores = (
        prob_rows * (grad_probs - jnp.transpose(row_delta, (0, 2, 1))[..., None]) * score_scale
    ).astype(jnp.bfloat16)
    grad_query = jnp.einsum(
        "ihlm,imhd->ilhd", grad_scores, key_heads, preferred_element_type=jnp.float32
    ).astype(jnp.bfloat16)
    key_terms = jnp.einsum(
        "ihlm,ilhd->imhd", grad_scores, query_heads, preferred_element_type=jnp.float32
    ).reshape(images, length, head_cols)
    value_terms = jnp.einsum(
        "ihlm,ilhd->imhd",
        prob_rows.astype(jnp.bfloat16),
        grad_attn_heads,
        preferred_element_type=jnp.float32,
    ).reshape(images, length, head_cols)
    key_sum, value_sum = (
        lax.psum_scatter(
            key_terms.astype(jnp.bfloat16), "seq", scatter_dimension=1, tiled=True
        ).astype(jnp.float32),
        lax.psum_scatter(
            value_terms.astype(jnp.bfloat16), "seq", scatter_dimension=1, tiled=True
        ).astype(jnp.float32),
    )
    grad_key = key_sum.astype(jnp.bfloat16)
    grad_value = value_sum.astype(jnp.bfloat16)
    grad_qkv = jnp.stack(
        [
            grad_query.reshape(total_rows, head_cols),
            grad_key.reshape(total_rows, head_cols),
            grad_value.reshape(total_rows, head_cols),
        ]
    )
    grad_norm_one = lax.psum_scatter(
        jnp.einsum("ktf,kdf->td", grad_qkv, qkv_weight, preferred_element_type=jnp.float32).astype(
            jnp.bfloat16
        ),
        ("section", "mp"),
        scatter_dimension=0,
        tiled=True,
    ).astype(jnp.float32)
    normed_one_own = lax.dynamic_slice_in_dim(normed_one, own_start, row_count, 0)
    inv_one_own = lax.dynamic_slice_in_dim(inv_one, own_start, row_count, 0)
    grad_input = (
        grad_resid.astype(jnp.float32) + norm_backward(normed_one_own, inv_one_own, grad_norm_one)
    ).astype(jnp.bfloat16)
    return (block_out[None], grad_input[None])


def solution(mesh):
    in_specs = (
        P("section", ("seq", "mp"), None),
        P(None, None, ("section", "mp")),
        P(("section", "mp"), None),
        P(None, ("section", "mp")),
        P(("section", "mp"), None),
        P("section", ("seq", "mp"), None),
    )
    out_specs = (P("section", ("seq", "mp"), None), P("section", ("seq", "mp"), None))
    return jax.shard_map(
        per_device, mesh=mesh, in_specs=in_specs, out_specs=out_specs, check_vma=False
    )
```

profile of v0, /device:TPU:0, one launch (start us, length us, event | category | flops | bytes accessed | tf_op | source)
XLA Modules:
  0.0 712.6 jit_solution(180392068172383027)
XLA Ops:
  8.0 52.6 %all-gather.7.cloned.1.call-done = bf16[16,16,4096]{2,1,0:T(8,128)(2,1)} async-done(((bf16[1,16,4096]{2,1,0:T(8,128)(2,1)}), bf16[16,16,4096]{2,1,0:T(8,128)(2,1)}) %all-gather.7.cloned.1.call-update) | async-done | bytes 2097168 | tf_op jit(solution)/shard_map/all_gather | solution.py:47
  65.0 2.5 fusion.4
  72.8 38.2 %all-gather.11.cloned.1.call-done = bf16[2,1024,256]{1,2,0:T(8,128)(2,1)} async-done(((bf16[2,128,256]{1,2,0:T(8,128)(2,1)}), bf16[2,1024,256]{1,2,0:T(8,128)(2,1)}) %all-gather.11.cloned.1.call-update) | async-done | bytes 1048592 | tf_op jit(solution)/shard_map/all_gather | solution.py:61
  114.7 39.9 %all-gather.9.cloned.1.call-done = bf16[2,1024,256]{2,1,0:T(8,128)(2,1)} async-done(((bf16[2,128,256]{2,1,0:T(8,128)(2,1)}), bf16[2,1024,256]{2,1,0:T(8,128)(2,1)}) %all-gather.9.cloned.1.call-update) | async-done | bytes 1048592 | tf_op jit(solution)/shard_map/all_gather | solution.py:62
  156.1 2.5 fusion.21
  160.9 70.8 %reduce-scatter.11.cloned.1.call-done = bf16[16,4096]{1,0:T(8,128)(2,1)} async-done(((bf16[256,4096]{1,0:T(8,128)(2,1)}), bf16[16,4096]{1,0:T(8,128)(2,1)}) %reduce-scatter.11.cloned.1.call-update) | async-done | bytes 131088 | tf_op jit(solution)/shard_map/reduce_scatter | solution.py:84
  234.1 47.4 %all-gather.13.cloned.1.call-done = bf16[256,4096]{1,0:T(8,128)(2,1)} async-done(((bf16[16,4096]{1,0:T(8,128)(2,1)}), bf16[256,4096]{1,0:T(8,128)(2,1)}) %all-gather.13.cloned.1.call-update) | async-done | bytes 2097168 | tf_op jit(solution)/shard_map/all_gather | solution.py:91
  284.4 6.8 fusion.7
  291.1 39.4 %all-gather.15.cloned.1.call-done = bf16[16,16,4096]{2,1,0:T(8,128)(2,1)} async-done(((bf16[1,16,4096]{2,1,0:T(8,128)(2,1)}), bf16[16,16,4096]{2,1,0:T(8,128)(2,1)}) %all-gather.15.cloned.1.call-update) | async-done | bytes 2097168 | tf_op jit(solution)/shard_map/all_gather | solution.py:104
  330.5 12.8 %convolution_convert_fusion = bf16[256,4096]{1,0:T(8,128)(2,1)} fusion(bf16[4096,1024]{1,0:T(8,128)(2,1)} %param.9, bf16[256,4096]{1,0:T(8,128)(2,1)} %bitcast.106, bf16[1024,4096]{1,0:T(8,128)(2,1)} %param.10, f32[256,1024]{1,0:T(8,128)} %fusion.7), kind=kOutput, calls=%fused_computation.3 | convolution fusion | flops 4298637312 | bytes 22020096 | tf_op jit(solution)/shard_map/tf,df->td/dot_general | solution.py:110
  343.4 4.4 fusion.1
  347.8 65.5 %reduce-scatter.15.cloned.1.call-done = bf16[16,4096]{1,0:T(8,128)(2,1)} async-done(((bf16[256,4096]{1,0:T(8,128)(2,1)}), bf16[16,4096]{1,0:T(8,128)(2,1)}) %reduce-scatter.15.cloned.1.call-update) | async-done | bytes 131088 | tf_op jit(solution)/shard_map/reduce_scatter | solution.py:109
  416.5 46.6 %all-gather.17.cloned.1.call-done = bf16[256,4096]{1,0:T(8,128)(2,1)} async-done(((bf16[16,4096]{1,0:T(8,128)(2,1)}), bf16[256,4096]{1,0:T(8,128)(2,1)}) %all-gather.17.cloned.1.call-update) | async-done | bytes 2097168 | tf_op jit(solution)/shard_map/all_gather | solution.py:122
  465.6 3.1 convolution_convert_fusion.3
  468.7 2.5 copy.46
  472.6 2.6 multiply_convert_fusion
  476.6 3.6 copy.44
  480.3 2.4 copy.51
  483.0 7.4 %convolution_convert_fusion.1 = bf16[256,4096]{1,0:T(8,128)(2,1)} fusion(bf16[1024,4096]{1,0:T(8,128)(2,1)} %param.10, f32[256,1024]{1,0:T(8,128)} %fusion.7), kind=kOutput, calls=%fused_computation.4 | convolution fusion | flops 2149842944 | bytes 11534336 | tf_op jit(solution)/shard_map/dot_general | solution.py:98
  492.4 20.2 %reduce-scatter.21.cloned.1.call-done = bf16[128,512]{1,0:T(8,128)(2,1)} async-done(((bf16[1024,512]{1,0:T(8,128)(2,1)}), bf16[128,512]{1,0:T(8,128)(2,1)}) %reduce-scatter.21.cloned.1.call-update) | async-done | bytes 131088
  513.5 41.1 %reduce-scatter.19.cloned.1.call-done = bf16[128,512]{1,0:T(8,128)(2,1)} async-done(((bf16[1024,512]{1,0:T(8,128)(2,1)}), bf16[128,512]{1,0:T(8,128)(2,1)}) %reduce-scatter.19.cloned.1.call-update) | async-done | bytes 131088
  555.6 6.0 fusion
  561.7 66.7 %reduce-scatter.13.cloned.1.call-done = bf16[16,4096]{1,0:T(8,128)(2,1)} async-done(((bf16[256,4096]{1,0:T(8,128)(2,1)}), bf16[16,4096]{1,0:T(8,128)(2,1)}) %reduce-scatter.13.cloned.1.call-update) | async-done | bytes 131088 | tf_op jit(solution)/shard_map/reduce_scatter | solution.py:97
  630.0 72.7 %reduce-scatter.17.cloned.1.call-done = bf16[16,4096]{1,0:T(8,128)(2,1)} async-done(((bf16[256,4096]{1,0:T(8,128)(2,1)}), bf16[16,4096]{1,0:T(8,128)(2,1)}) %reduce-scatter.17.cloned.1.call-update) | async-done | bytes 131088 | tf_op jit(solution)/shard_map/reduce_scatter | solution.py:164
  (94 shorter events, 40.4 us)
Async XLA Ops:
  7.2 151.6 %copy-start = (bf16[256,4096]{1,0:T(8,128)(2,1)S(1)}, bf16[256,4096]{1,0:T(8,128)(2,1)}, u32[]{:S(2)}) copy-start(bf16[256,4096]{1,0:T(8,128)(2,1)} %param.8) | copy-start | bytes 6291460
  7.2 53.4 %all-gather.7.cloned.1.call-start = ((), (), s32[]{:S(2)}) async-start(), calls=%async_computation.6 | async-start | bytes 2228224 | tf_op jit(solution)/shard_map/all_gather | solution.py:47
  7.9 103.1 %all-gather.11.cloned.1.call-start = ((), (), s32[]{:S(2)}) async-start(), calls=%async_computation.8 | async-start | bytes 1179648 | tf_op jit(solution)/shard_map/all_gather | solution.py:61
  65.0 3.4 copy-start.11
  68.4 1.9 copy-start.3
  71.8 82.8 %all-gather.9.cloned.1.call-start = ((), (), s32[]{:S(2)}) async-start(), calls=%async_computation.7 | async-start | bytes 1179648 | tf_op jit(solution)/shard_map/all_gather | solution.py:62
  72.6 159.1 %reduce-scatter.11.cloned.1.call-start = ((), (), s32[]{:S(2)}) async-start(), calls=%async_computation.9 | async-start | bytes 2228224 | tf_op jit(solution)/shard_map/reduce_scatter | solution.py:84
  112.8 1.4 copy-start.1
  114.7 43.9 %copy-start.9 = (f32[2,2,128]{2,1,0:T(2,128)}, f32[2,2,128]{2,1,0:T(2,128)S(1)}, u32[]{:S(2)}) copy-start(f32[2,2,128]{2,1,0:T(2,128)S(1)} %fusion.10) | copy-start | bytes 6148
  156.1 4.7 copy-start.4
  160.8 70.8 %copy-start.7 = (bf16[1,16,4096]{2,1,0:T(8,128)(2,1)S(1)}, bf16[1,16,4096]{2,1,0:T(8,128)(2,1)}, u32[]{:S(2)}) copy-start(bf16[1,16,4096]{2,1,0:T(8,128)(2,1)} %param.6) | copy-start | bytes 393220
  160.9 120.6 %all-gather.13.cloned.1.call-start = ((), (), s32[]{:S(2)}) async-start(), calls=%async_computation.10 | async-start | bytes 2228224 | tf_op jit(solution)/shard_map/all_gather | solution.py:91
  233.3 97.2 %all-gather.15.cloned.1.call-start = ((), (), s32[]{:S(2)}) async-start(), calls=%async_computation.12 | async-start | bytes 2228224 | tf_op jit(solution)/shard_map/all_gather | solution.py:104
  233.9 179.5 %reduce-scatter.15.cloned.1.call-start = ((), (), s32[]{:S(2)}) async-start(), calls=%async_computation.13 | async-start | bytes 2228224 | tf_op jit(solution)/shard_map/reduce_scatter | solution.py:109
  281.5 2.2 copy-start.2
  343.3 119.8 %all-gather.17.cloned.1.call-start = ((), (), s32[]{:S(2)}) async-start(), calls=%async_computation.14 | async-start | bytes 2228224 | tf_op jit(solution)/shard_map/all_gather | solution.py:122
  343.4 71.1 %copy-start.8 = (bf16[1,16,4096]{2,1,0:T(8,128)(2,1)S(1)}, bf16[1,16,4096]{2,1,0:T(8,128)(2,1)}, u32[]{:S(2)}) copy-start(bf16[1,16,4096]{2,1,0:T(8,128)(2,1)} %param.11) | copy-start | bytes 393220
  343.4 73.0 %copy-start.10 = (f32[2,2,128]{2,1,0:T(2,128)S(1)}, f32[2,2,128]{2,1,0:T(2,128)}, u32[]{:S(2)}) copy-start(f32[2,2,128]{2,1,0:T(2,128)} %copy-done.9) | copy-start | bytes 6148
  416.4 96.2 %reduce-scatter.21.cloned.1.call-start = ((), (), s32[]{:S(2)}) async-start(), calls=%async_computation.17 | async-start | bytes 1179648
  472.5 82.2 %reduce-scatter.19.cloned.1.call-start = ((), (), s32[]{:S(2)}) async-start(), calls=%async_computation.16 | async-start | bytes 1179648
  482.7 145.7 %reduce-scatter.13.cloned.1.call-start = ((), (), s32[]{:S(2)}) async-start(), calls=%async_computation.11 | async-start | bytes 2228224 | tf_op jit(solution)/shard_map/reduce_scatter | solution.py:97
  490.4 212.3 %reduce-scatter.17.cloned.1.call-start = ((), (), s32[]{:S(2)}) async-start(), calls=%async_computation.15 | async-start | bytes 2228224 | tf_op jit(solution)/shard_map/reduce_scatter | solution.py:164
  561.6 66.9 %copy-start.5 = (bf16[16,4096]{1,0:T(8,128)(2,1)S(1)}, bf16[16,4096]{1,0:T(8,128)(2,1)}, u32[]{:S(2)}) copy-start(bf16[16,4096]{1,0:T(8,128)(2,1)} %fusion.50) | copy-start | bytes 393220
  561.6 142.4 %copy-start.6 = (bf16[16,4096]{1,0:T(8,128)(2,1)S(1)}, bf16[16,4096]{1,0:T(8,128)(2,1)}, u32[]{:S(2)}) copy-start(bf16[16,4096]{1,0:T(8,128)(2,1)} %fusion.43) | copy-start | bytes 393220
Sparse Core Ops, SparseCore 0:
  10.5 50.0 all-gather.6
  71.9 39.0 all-gather.10
  113.3 41.2 all-gather.8
  161.0 70.6 reduce-scatter.10
  234.9 46.5 all-gather.12
  284.1 46.3 all-gather.14
  343.4 69.8 reduce-scatter.14
  416.5 46.5 all-gather.16
  472.6 39.9 reduce-scatter.20
  514.8 39.8 reduce-scatter.18
  558.5 69.8 reduce-scatter.12
  632.7 70.0 reduce-scatter.16
where the time goes:
time: 713 us
  waiting for transfers between devices  603 us (85%)
  matrix products  52.2 us (7%)
  other arithmetic  23.6 us (3%)
  local copies, waits for them, and re-layouts  18.3 us (3%)
  between operations  14.4 us (2%)
    reduce_scatter x1, waiting for transfers between devices, per_device(): lax.psum_scatter(jnp.einsum('ktf,kdf->td', grad_qkv, qkv_weight, preferre...  72.7 us
    reduce_scatter x1, waiting for transfers between devices, per_device(): lax.psum_scatter(jnp.dot(attended_flat, out_weight, preferred_element_typ...  70.8 us
    reduce_scatter x1, waiting for transfers between devices, per_device(): lax.psum_scatter(jnp.dot(hidden, down_weight, preferred_element_type=jnp....  66.7 us
    reduce_scatter x1, waiting for transfers between devices, per_device(): lax.psum_scatter(jnp.einsum('tf,df->td', grad_hidden, up_weight, preferre...  65.5 us
    unnamed x14, waiting for transfers between devices  63.3 us
    all_gather x1, waiting for transfers between devices, per_device(): lax.all_gather(bottleneck, ('section', 'mp'), axis=0, tiled=True)  52.6 us
    all_gather x1, waiting for transfers between devices, per_device(): resid_all = lax.all_gather(resid_own, ('section', 'mp'), axis=0, tiled=True)  47.4 us
    all_gather x1, waiting for transfers between devices, per_device(): lax.all_gather(grad_resid, ('section', 'mp'), axis=0, tiled=True)  46.6 us
  transfers between devices with their start and end apart: 12, of which 12 were waited for; matrix products, arithmetic and copies ran while one was open for 6% of the time, Pallas kernels for 0%

commit v1 on v0

v1 whole, which is shorter than its diff:
```python
import math

import jax
import jax.numpy as jnp
from jax import lax
from jax.sharding import PartitionSpec as P

HD = 128


norm_eps = 1e-06


def layer_norm(inputs):
    row_mean = jnp.mean(inputs, axis=-1, keepdims=True)
    centered = inputs - row_mean
    inv_std = lax.rsqrt(jnp.mean(centered * centered, axis=-1, keepdims=True) + norm_eps)
    return (centered * inv_std, inv_std)


def norm_backward(normed, inv_std, grad_in):
    mean_grad = jnp.mean(grad_in, axis=-1, keepdims=True)
    mean_mix = jnp.mean(grad_in * normed, axis=-1, keepdims=True)
    return inv_std * (grad_in - mean_grad - normed * mean_mix)


def gelu_value(pre_act):
    return pre_act * 0.5 * (1.0 + lax.erf(pre_act * 0.7071067811865476))


def gelu_slope(pre_act):
    cumul = 0.5 * (1.0 + lax.erf(pre_act * 0.7071067811865476))
    return cumul + pre_act * jnp.exp(-0.5 * pre_act * pre_act) * 0.3989422804014327


def swap_section(data):
    return lax.ppermute(data, "section", [(0, 1), (1, 0)])


def spread(own, axis):
    size = lax.axis_size(axis)
    copies = jnp.broadcast_to(own[None], (size,) + own.shape)
    return lax.all_to_all(copies, axis, 0, 0)


def gather_rows(own):
    mine = spread(own, "mp").reshape(-1, own.shape[-1])
    return jnp.concatenate([mine, swap_section(mine)], axis=0)


def scatter_rows(partial):
    half = partial.shape[0] // 2
    width = partial.shape[1]
    other = swap_section(partial[half:].astype(jnp.bfloat16))
    pair = (partial[:half] + other.astype(jnp.float32)).astype(jnp.bfloat16)
    size = lax.axis_size("mp")
    parts = lax.all_to_all(pair.reshape(size, half // size, width), "mp", 0, 0)
    return jnp.sum(parts.astype(jnp.float32), axis=0)


def scatter_rows_later(partial):
    half = partial.shape[0] // 2
    other = swap_section(partial[half:].astype(jnp.bfloat16))
    pair = (partial[:half] + other.astype(jnp.float32)).astype(jnp.bfloat16)
    return lax.psum_scatter(pair, "mp", scatter_dimension=0, tiled=True).astype(jnp.float32)


def gather_rows_early(own):
    mine = lax.all_gather(own, "mp", axis=0, tiled=True)
    return jnp.concatenate([mine, swap_section(mine)], axis=0)


def dot_f32(lhs, rhs):
    return jnp.dot(lhs, rhs, preferred_element_type=jnp.float32)


def dot_nt(lhs, rhs):
    return jnp.einsum("tf,df->td", lhs, rhs, preferred_element_type=jnp.float32)


def per_device(bottleneck, qkv_weight, out_weight, up_weight, down_weight, cotangent):
    own_in = bottleneck[0].astype(jnp.float32)
    own_cot = cotangent[0]
    images = 2
    head_cols = qkv_weight.shape[2]
    head_count = head_cols // HD
    score_scale = 1.0 / math.sqrt(HD)

    cot_all = gather_rows_early(own_cot)
    normed_one, inv_one = layer_norm(own_in)
    normed_all = gather_rows(normed_one.astype(jnp.bfloat16))
    total_rows = normed_all.shape[0]
    block_rows = total_rows // images
    projected = jnp.einsum(
        "td,kdf->ktf", normed_all, qkv_weight, preferred_element_type=jnp.float32
    ).astype(jnp.bfloat16)
    query_heads = projected[0].reshape(images, block_rows, head_count, HD)
    pairs = spread(projected[1:].reshape(2, images, block_rows, head_cols), "seq")
    seq_size = pairs.shape[0]
    length = seq_size * block_rows
    heads = jnp.transpose(pairs, (1, 2, 0, 3, 4)).reshape(2, images, length, head_count, HD)
    key_heads, value_heads = heads[0], heads[1]

    scores = (
        jnp.einsum("ilhd,imhd->ihlm", query_heads, key_heads, preferred_element_type=jnp.float32)
        * score_scale
    )
    row_max = jnp.max(scores, axis=-1)
    weights = jnp.exp(scores - row_max[..., None])
    totals = jnp.sum(weights, axis=-1)
    log_total = row_max + jnp.log(totals)
    mixed_values = jnp.einsum(
        "ihlm,imhd->ilhd",
        weights.astype(jnp.bfloat16),
        value_heads,
        preferred_element_type=jnp.float32,
    )
    attended = (mixed_values / jnp.transpose(totals, (0, 2, 1))[..., None]).astype(jnp.bfloat16)
    attn_own = scatter_rows(dot_f32(attended.reshape(total_rows, head_cols), out_weight))
    resid = (own_in + attn_own).astype(jnp.bfloat16)
    normed_two, inv_two = layer_norm(resid.astype(jnp.float32))
    normed_two_all = gather_rows(normed_two.astype(jnp.bfloat16))
    hidden_pre = dot_f32(normed_two_all, up_weight)
    hidden = gelu_value(hidden_pre).astype(jnp.bfloat16)
    grad_act = dot_nt(cot_all, down_weight)
    grad_hidden = (grad_act * gelu_slope(hidden_pre)).astype(jnp.bfloat16)
    grad_norm_two = scatter_rows(dot_nt(grad_hidden, up_weight))
    ffn_own = scatter_rows_later(dot_f32(hidden, down_weight))
    block_out = (resid.astype(jnp.float32) + ffn_own).astype(jnp.bfloat16)

    grad_resid = (
        own_cot.astype(jnp.float32) + norm_backward(normed_two, inv_two, grad_norm_two)
    ).astype(jnp.bfloat16)
    grad_resid_all = gather_rows(grad_resid)
    grad_attn = dot_nt(grad_resid_all, out_weight).astype(jnp.bfloat16)
    grad_attn_heads = grad_attn.reshape(images, block_rows, head_count, HD)
    row_delta = jnp.sum(grad_attn_heads.astype(jnp.float32) * attended.astype(jnp.float32), axis=-1)
    prob_rows = jnp.exp(scores - log_total[..., None])
    grad_probs = jnp.einsum(
        "ilhd,imhd->ihlm", grad_attn_heads, value_heads, preferred_element_type=jnp.float32
    )
    grad_scores = (
        prob_rows * (grad_probs - jnp.transpose(row_delta, (0, 2, 1))[..., None]) * score_scale
    ).astype(jnp.bfloat16)
    grad_query = jnp.einsum(
        "ihlm,imhd->ilhd", grad_scores, key_heads, preferred_element_type=jnp.float32
    ).astype(jnp.bfloat16)
    key_terms = jnp.einsum(
        "ihlm,ilhd->imhd", grad_scores, query_heads, preferred_element_type=jnp.float32
    ).astype(jnp.bfloat16)
    value_terms = jnp.einsum(
        "ihlm,ilhd->imhd",
        prob_rows.astype(jnp.bfloat16),
        grad_attn_heads,
        preferred_element_type=jnp.float32,
    ).astype(jnp.bfloat16)
    terms = jnp.stack([key_terms, value_terms]).reshape(
        2, images, seq_size, block_rows, head_cols
    )
    terms = lax.all_to_all(jnp.transpose(terms, (2, 0, 1, 3, 4)), "seq", 0, 0)
    grad_kv = jnp.sum(terms.astype(jnp.float32), axis=0).astype(jnp.bfloat16)
    grad_qkv = jnp.concatenate(
        [grad_query.reshape(1, total_rows, head_cols), grad_kv.reshape(2, total_rows, head_cols)]
    )
    grad_norm_one = scatter_rows(
        jnp.einsum("ktf,kdf->td", grad_qkv, qkv_weight, preferred_element_type=jnp.float32)
    )
    grad_input = (
        grad_resid.astype(jnp.float32) + norm_backward(normed_one, inv_one, grad_norm_one)
    ).astype(jnp.bfloat16)
    return (block_out[None], grad_input[None])


def solution(mesh):
    in_specs = (
        P("section", ("seq", "mp"), None),
        P(None, None, ("section", "mp")),
        P(("section", "mp"), None),
        P(None, ("section", "mp")),
        P(("section", "mp"), None),
        P("section", ("seq", "mp"), None),
    )
    out_specs = (P("section", ("seq", "mp"), None), P("section", ("seq", "mp"), None))
    return jax.shard_map(
        per_device, mesh=mesh, in_specs=in_specs, out_specs=out_specs, check_vma=False
    )
```

time: 713 us -> 380 us (0.53)
  waiting for transfers between devices: 603 us -> 161 us
  blocking collectives: 0 us -> 108 us
  starting transfers between devices: 0.89 us -> 14.4 us
  matrix products: 52.2 us -> 40.4 us
    all_gather x6 -> x1, waiting for transfers between devices: 264 us -> 35 us  [gather_rows_early(): mine = lax.all_gather(own, 'mp', axis=0, tiled=True)]
    reduce_scatter x4 -> x1, waiting for transfers between devices: 276 us -> 48.2 us  [scatter_rows_later(): lax.psum_scatter(pair, 'mp', scatter_dimension=0, tiled=True)]
    all_to_all x0 -> x5, blocking collectives: none -> 108 us  [the longest x3 63.3 us: scatter_rows(): parts = lax.all_to_all(pair.reshape(size, half // size, width), 'mp', 0, 0)]
    all_to_all x0 -> x3, waiting for transfers between devices: none -> 66.6 us  [the longest x2 41 us: spread(): return lax.all_to_all(copies, axis, 0, 0)]
    unnamed x14 -> x2, waiting for transfers between devices: 63.3 us -> 0.7 us
    all_to_all x0 -> x3, starting transfers between devices: none -> 13.2 us  [the longest x2 8.84 us: spread(): return lax.all_to_all(copies, axis, 0, 0)]
    slice x1 -> x9, local copies, waits for them, and re-layouts: 0.68 us -> 11.7 us  [the longest x3 7.63 us: per_device(): key_heads, value_heads = (heads[0], heads[1])]
    unnamed x30 -> x28, local copies, waits for them, and re-layouts: 14.3 us -> 3.45 us
  transfers between devices with their start and end apart: 12 -> 13, of which waited for: 12 -> 9; matrix products, arithmetic and copies ran while one was open for 6% -> 9% of each run, Pallas kernels for 0% -> 0%
where the time goes in v1:
time: 380 us; the launch traced here: 379 us
  waiting for transfers between devices  161 us (42%)
  blocking collectives  108 us (28%)
  matrix products  40.4 us (11%)
  local copies, waits for them, and re-layouts  23.5 us (6%)
  other arithmetic  17.3 us (5%)
  between operations  14.5 us (4%)
  starting transfers between devices  14.4 us (4%)
    all_to_all x3, blocking collectives, scatter_rows(): parts = lax.all_to_all(pair.reshape(size, half // size, width), 'mp', 0, 0)  63.3 us
    reduce_scatter x1, waiting for transfers between devices, scatter_rows_later(): lax.psum_scatter(pair, 'mp', scatter_dimension=0, tiled=True)  48.2 us
    all_to_all x2, blocking collectives, spread(): return lax.all_to_all(copies, axis, 0, 0)  44.6 us
    all_to_all x2, waiting for transfers between devices, spread(): return lax.all_to_all(copies, axis, 0, 0)  41 us
    all_gather x1, waiting for transfers between devices, gather_rows_early(): mine = lax.all_gather(own, 'mp', axis=0, tiled=True)  35 us
    all_to_all x1, waiting for transfers between devices, per_device(): terms = lax.all_to_all(jnp.transpose(terms, (2, 0, 1, 3, 4)), 'seq', 0, 0)  25.7 us
    dot_general x2, matrix products, dot_nt(): return jnp.einsum('tf,df->td', lhs, rhs, preferred_element_type=jnp.float32)  14.2 us
    ppermute x8, waiting for transfers between devices, swap_section(): return lax.ppermute(data, 'section', [(0, 1), (1, 0)])  10.6 us
  transfers between devices with their start and end apart: 13, of which 9 were waited for; matrix products, arithmetic and copies ran while one was open for 9% of the time, Pallas kernels for 0%

profile of v1, /device:TPU:0, one launch (start us, length us, event | category | flops | bytes accessed | tf_op | source)
XLA Modules:
  0.0 379.1 jit_solution(5679118020968333429)
XLA Ops:
  10.6 24.8 %all_to_all.40 = bf16[8,16,4096]{2,1,0:T(8,128)(2,1)S(1)} all-to-all(bf16[8,16,4096]{2,1,0:T(8,128)(2,1)S(1)} %broadcast_in_dim.19), channel_id=1, replica_groups=mesh['section'=2,'seq'=8,'mp'=8] {'mp'}, dimensions={0} | all-to-all | bytes 2097152 | tf_op jit(solution)/shard_map/all_to_all | solution.py:43
  35.4 2.7 collective-permute-done
  38.1 4.6 %fusion.29 = bf16[3,256,256]{2,1,0:T(8,128)(2,1)S(1)} fusion(bf16[3,4096,256]{2,1,0:T(8,128)(2,1)} %param.7, bf16[128,4096]{1,0:T(8,128)(2,1)S(1)} %collective-permute-done, bf16[128,4096]{1,0:T(8,128)(2,1)S(1)} %bitcast.138), kind=kOutput, calls=%fused_computation.48 | convolution fusion | flops 1615003648 | bytes 8781824 | tf_op jit(solution)/shard_map/td,kdf->ktf/dot_general | solution.py:94
  44.7 4.6 %all-to-all-start.1 = ((bf16[8,2,2,128,256]{3,4,2,1,0:T(8,128)(2,1)}), bf16[8,2,2,128,256]{3,4,2,1,0:T(8,128)(2,1)}, u32[]{:S(2)}, u32[]{:S(2)}) async-start(bf16[8,2,2,128,256]{3,4,2,1,0:T(8,128)(2,1)} %broadcast_in_dim.21), calls=%async_computation.1 | async-start | bytes 4194304 | tf_op jit(solution)/shard_map/all_to_all | solution.py:43
  49.5 27.2 %all-to-all-done.1 = bf16[8,2,2,128,256]{3,4,2,1,0:T(8,128)(2,1)} async-done(((bf16[8,2,2,128,256]{3,4,2,1,0:T(8,128)(2,1)}), bf16[8,2,2,128,256]{3,4,2,1,0:T(8,128)(2,1)}, u32[]{:S(2)}, u32[]{:S(2)}) %all-to-all-start.1) | async-done | bytes 2097184 | tf_op jit(solution)/shard_map/all_to_all | solution.py:43
  76.6 2.7 fusion.99
  82.5 3.3 copy.25
  91.8 2.6 collective-permute-done.1
  94.6 20.7 %all_to_all.41 = bf16[8,16,4096]{2,1,0:T(8,128)(2,1)S(1)} all-to-all(bf16[8,16,4096]{2,1,0:T(8,128)(2,1)S(1)} %bitcast.130), channel_id=1, replica_groups=mesh['section'=2,'seq'=8,'mp'=8] {'mp'}, dimensions={0} | all-to-all | bytes 2097152 | tf_op jit(solution)/shard_map/all_to_all | solution.py:57
  117.1 4.2 %all-to-all-start.3 = ((bf16[8,16,4096]{2,1,0:T(8,128)(2,1)}), bf16[8,16,4096]{2,1,0:T(8,128)(2,1)}, u32[]{:S(2)}, u32[]{:S(2)}) async-start(bf16[8,16,4096]{2,1,0:T(8,128)(2,1)} %broadcast_in_dim.23), calls=%async_computation.3 | async-start | bytes 2097152 | tf_op jit(solution)/shard_map/all_to_all | solution.py:43
  122.1 13.8 %all-to-all-done.3 = bf16[8,16,4096]{2,1,0:T(8,128)(2,1)} async-done(((bf16[8,16,4096]{2,1,0:T(8,128)(2,1)}), bf16[8,16,4096]{2,1,0:T(8,128)(2,1)}, u32[]{:S(2)}, u32[]{:S(2)}) %all-to-all-start.3) | async-done | bytes 1048608 | tf_op jit(solution)/shard_map/all_to_all | solution.py:43
  135.9 35.0 %all-gather.3.cloned.1.call-done = bf16[1,128,4096]{2,1,0:T(8,128)(2,1)} async-done(((bf16[1,16,4096]{2,1,0:T(8,128)(2,1)}), bf16[1,128,4096]{2,1,0:T(8,128)(2,1)}) %all-gather.3.cloned.1.call-update) | async-done | bytes 1048592 | tf_op jit(solution)/shard_map/all_gather | solution.py:69
  170.9 6.5 %fusion.7 = f32[256,1024]{1,0:T(8,128)S(1)} fusion(bf16[4096,1024]{1,0:T(8,128)(2,1)} %param.9, bf16[128,4096]{1,0:T(8,128)(2,1)} %collective-permute-done.2, bf16[128,4096]{1,0:T(8,128)(2,1)} %bitcast.12), kind=kOutput, calls=%fused_computation.21 | convolution fusion | flops 2151677952 | bytes 11534336 | tf_op jit(solution)/shard_map/dot_general | solution.py:74
  183.9 13.4 %fusion.45 = f32[256,4096]{1,0:T(8,128)} fusion(bf16[4096,1024]{1,0:T(8,128)(2,1)} %param.9, bf16[1024,4096]{1,0:T(8,128)(2,1)} %param.10, bf16[128,4096]{1,0:T(8,128)(2,1)} %collective-permute-done.4, bf16[128,4096]{1,0:T(8,128)(2,1)} %bitcast.146, f32[256,1024]{1,0:T(8,128)} %copy-done.10), kind=kOutput, calls=%fused_computation.63 | convolution fusion | flops 4301783040 | bytes 24117248 | tf_op jit(solution)/shard_map/tf,df->td/dot_general | solution.py:78
  197.3 2.7 slice.83
  200.0 3.1 fusion.2
  205.2 22.3 %all_to_all.42 = bf16[8,16,4096]{2,1,0:T(8,128)(2,1)S(1)} all-to-all(bf16[8,16,4096]{2,1,0:T(8,128)(2,1)S(1)} %bitcast.131), channel_id=1, replica_groups=mesh['section'=2,'seq'=8,'mp'=8] {'mp'}, dimensions={0} | all-to-all | bytes 2097152 | tf_op jit(solution)/shard_map/all_to_all | solution.py:57
  227.9 48.2 %reduce-scatter.2.cloned.1.call-done = bf16[16,4096]{1,0:T(8,128)(2,1)} async-done(((bf16[128,4096]{1,0:T(8,128)(2,1)}), bf16[16,4096]{1,0:T(8,128)(2,1)}) %reduce-scatter.2.cloned.1.call-update) | async-done | bytes 131088 | tf_op jit(solution)/shard_map/reduce_scatter | solution.py:65
  278.1 19.8 %all_to_all.43 = bf16[8,16,4096]{2,1,0:T(8,128)(2,1)S(1)} all-to-all(bf16[8,16,4096]{2,1,0:T(8,128)(2,1)S(1)} %broadcast_in_dim.26), channel_id=1, replica_groups=mesh['section'=2,'seq'=8,'mp'=8] {'mp'}, dimensions={0} | all-to-all | bytes 2097152 | tf_op jit(solution)/shard_map/all_to_all | solution.py:43
  297.9 2.6 collective-permute-done.6
  308.7 4.3 %all-to-all-start.6 = ((bf16[8,2,2,128,256]{3,4,2,1,0:T(8,128)(2,1)}), bf16[8,2,2,128,256]{3,4,2,1,0:T(8,128)(2,1)}, u32[]{:S(2)}, u32[]{:S(2)}) async-start(bf16[8,2,2,128,256]{3,4,2,1,0:T(8,128)(2,1)} %maximum_bitcast_fusion.2), calls=%async_computation.7 | async-start | bytes 4194304 | tf_op jit(solution)/shard_map/all_to_all | solution.py:160
  315.0 25.7 %all-to-all-done.6 = bf16[8,2,2,128,256]{3,4,2,1,0:T(8,128)(2,1)} async-done(((bf16[8,2,2,128,256]{3,4,2,1,0:T(8,128)(2,1)}), bf16[8,2,2,128,256]{3,4,2,1,0:T(8,128)(2,1)}, u32[]{:S(2)}, u32[]{:S(2)}) %all-to-all-start.6) | async-done | bytes 2097184 | tf_op jit(solution)/shard_map/all_to_all | solution.py:160
  342.7 4.6 %convolution_bitcast_fusion = f32[256,4096]{1,0:T(8,128)S(1)} fusion(bf16[3,4096,256]{2,1,0:T(8,128)(2,1)} %param.7, bf16[2,256,256]{2,1,0:T(8,128)(2,1)S(1)} %bitcast.134, bf16[1,256,256]{2,1,0:T(8,128)(2,1)S(1)} %reshape.277), kind=kOutput, calls=%fused_computation | convolution fusion | flops 1610809344 | bytes 10878976 | tf_op jit(solution)/shard_map/ktf,kdf->td/dot_general | solution.py:166
  350.4 20.3 %all_to_all.44 = bf16[8,16,4096]{2,1,0:T(8,128)(2,1)S(1)} all-to-all(bf16[8,16,4096]{2,1,0:T(8,128)(2,1)S(1)} %bitcast.132), channel_id=1, replica_groups=mesh['section'=2,'seq'=8,'mp'=8] {'mp'}, dimensions={0} | all-to-all | bytes 2097152 | tf_op jit(solution)/shard_map/all_to_all | solution.py:57
  (106 shorter events, 44.9 us)
Async XLA Ops:
  7.2 83.7 %copy-start = (bf16[256,4096]{1,0:T(8,128)(2,1)S(1)}, bf16[256,4096]{1,0:T(8,128)(2,1)}, u32[]{:S(2)}) copy-start(bf16[256,4096]{1,0:T(8,128)(2,1)} %param.8) | copy-start | bytes 6291460
  35.4 2.7 collective-permute-start
  44.7 32.0 %all-to-all-start.1 = ((bf16[8,2,2,128,256]{3,4,2,1,0:T(8,128)(2,1)}), bf16[8,2,2,128,256]{3,4,2,1,0:T(8,128)(2,1)}, u32[]{:S(2)}, u32[]{:S(2)}) async-start(bf16[8,2,2,128,256]{3,4,2,1,0:T(8,128)(2,1)} %broadcast_in_dim.21), calls=%async_computation.1 | async-start | bytes 4194304 | tf_op jit(solution)/shard_map/all_to_all | solution.py:43
  49.4 38.7 %copy-start.7 = (bf16[2,128,2,128]{1,3,2,0:T(8,128)(2,1)}, bf16[2,128,2,128]{1,3,2,0:T(8,128)(2,1)S(1)}, u32[]{:S(2)}) copy-start(bf16[2,128,2,128]{1,3,2,0:T(8,128)(2,1)S(1)} %copy.34) | copy-start | bytes 393220
  82.5 5.6 %copy-start.3 = (bf16[2,1024,2,128]{1,3,2,0:T(8,128)(2,1)}, bf16[2,1024,2,128]{1,3,2,0:T(8,128)(2,1)S(1)}, u32[]{:S(2)}) copy-start(bf16[2,1024,2,128]{1,3,2,0:T(8,128)(2,1)S(1)} %squeeze.11) | copy-start | bytes 3145732
  88.1 2.0 copy-start.5
  91.7 2.7 collective-permute-start.1
  94.6 20.8 %copy-start.4 = (bf16[1,16,4096]{2,1,0:T(8,128)(2,1)S(1)}, bf16[1,16,4096]{2,1,0:T(8,128)(2,1)}, u32[]{:S(2)}) copy-start(bf16[1,16,4096]{2,1,0:T(8,128)(2,1)} %param.6) | copy-start | bytes 393220
  117.1 18.8 %all-to-all-start.3 = ((bf16[8,16,4096]{2,1,0:T(8,128)(2,1)}), bf16[8,16,4096]{2,1,0:T(8,128)(2,1)}, u32[]{:S(2)}, u32[]{:S(2)}) async-start(bf16[8,16,4096]{2,1,0:T(8,128)(2,1)} %broadcast_in_dim.23), calls=%async_computation.3 | async-start | bytes 2097152 | tf_op jit(solution)/shard_map/all_to_all | solution.py:43
  121.3 49.6 %all-gather.3.cloned.1.call-start = ((), (), s32[]{:S(2)}) async-start(), calls=%async_computation.10 | async-start | bytes 1179648 | tf_op jit(solution)/shard_map/all_gather | solution.py:69
  122.1 154.0 %reduce-scatter.2.cloned.1.call-start = ((), (), s32[]{:S(2)}) async-start(), calls=%async_computation.9 | async-start | bytes 1179648 | tf_op jit(solution)/shard_map/reduce_scatter | solution.py:65
  135.9 35.1 %collective-permute-start.2 = (bf16[128,4096]{1,0:T(8,128)(2,1)}, bf16[128,4096]{1,0:T(8,128)(2,1)}, u32[]{:S(2)}, u32[]{:S(2)}) collective-permute-start(bf16[128,4096]{1,0:T(8,128)(2,1)} %bitcast.12), channel_id=1, source_target_pairs={{0,64},{64,0},{1,65},{65,1},{2,66},{66,2},{3,67},{67,3},{4,68},{68... | collective-permute-start | bytes 3145736 | tf_op jit(solution)/shard_map/ppermute | solution.py:37
  170.9 6.5 %slice-start = ((s8[8388608]{0:T(1024)(128)(4,1)}), s8[4194304]{0:T(1024)(128)(4,1)S(1)}, s32[]{:S(2)}) async-start(s8[8388608]{0:T(1024)(128)(4,1)} %bitcast.143), calls=%async_computation.11 | async-start | bytes 8388608
  170.9 6.5 %slice-start.1 = ((s8[8388608]{0:T(1024)(128)(4,1)}), s8[4194304]{0:T(1024)(128)(4,1)S(1)}, s32[]{:S(2)}) async-start(s8[8388608]{0:T(1024)(128)(4,1)} %bitcast.143), calls=%async_computation.12 | async-start | bytes 8388608
  170.9 12.9 %collective-permute-start.4 = (bf16[128,4096]{1,0:T(8,128)(2,1)}, bf16[128,4096]{1,0:T(8,128)(2,1)}, u32[]{:S(2)}, u32[]{:S(2)}) collective-permute-start(bf16[128,4096]{1,0:T(8,128)(2,1)} %bitcast.145), channel_id=1, source_target_pairs={{0,64},{64,0},{1,65},{65,1},{2,66},{66,2},{3,67},{67,3},{4,68},{68... | collective-permute-start | bytes 3145736 | tf_op jit(solution)/shard_map/ppermute | solution.py:37
  177.5 2.4 copy-start.10
  182.9 17.1 %collective-permute-start.3 = (bf16[128,4096]{1,0:T(8,128)(2,1)}, bf16[128,4096]{1,0:T(8,128)(2,1)}, u32[]{:S(2)}, u32[]{:S(2)}) collective-permute-start(bf16[128,4096]{1,0:T(8,128)(2,1)} %slice.84), channel_id=1, source_target_pairs={{0,64},{64,0},{1,65},{65,1},{2,66},{66,2},{3,67},{67,3},{4,68},{68... | collective-permute-start | bytes 3145736 | tf_op jit(solution)/shard_map/ppermute | solution.py:37
  200.0 3.1 collective-permute-start.5
  205.2 72.7 %copy-start.9 = (bf16[1,16,4096]{2,1,0:T(8,128)(2,1)S(1)}, bf16[1,16,4096]{2,1,0:T(8,128)(2,1)}, u32[]{:S(2)}) copy-start(bf16[1,16,4096]{2,1,0:T(8,128)(2,1)} %param.11) | copy-start | bytes 393220
  297.9 2.7 collective-permute-start.6
  301.4 2.3 copy-start.2
  303.8 2.0 copy-start.8
  308.7 31.9 %all-to-all-start.6 = ((bf16[8,2,2,128,256]{3,4,2,1,0:T(8,128)(2,1)}), bf16[8,2,2,128,256]{3,4,2,1,0:T(8,128)(2,1)}, u32[]{:S(2)}, u32[]{:S(2)}) async-start(bf16[8,2,2,128,256]{3,4,2,1,0:T(8,128)(2,1)} %maximum_bitcast_fusion.2), calls=%async_computation.7 | async-start | bytes 4194304 | tf_op jit(solution)/shard_map/all_to_all | solution.py:160
  347.5 2.7 collective-permute-start.7
  (2 other events, 3.4 us)
Sparse Core Ops, SparseCore 0:
  124.5 46.3 all-gather.2
  203.2 72.8 reduce-scatter.1

commit v2 on v1

v2 whole, which is shorter than its diff:
```python
import math

import jax
import jax.numpy as jnp
from jax import lax
from jax.experimental import pallas as pl
from jax.experimental.pallas import tpu as pltpu
from jax.sharding import PartitionSpec as P

HD = 128
norm_eps = 1e-06
F32 = jnp.float32
BF16 = jnp.bfloat16
NT = (((1,), (1,)), ((), ()))
NN = (((1,), (0,)), ((), ()))
TN = (((0,), (0,)), ((), ()))


def dot(lhs, rhs, dims=NN):
    return lax.dot_general(lhs, rhs, dims, preferred_element_type=F32)


def whole(shape):
    rank = len(shape)
    return pl.BlockSpec(shape, lambda *ids: (0,) * rank)


def kernel_call(body, name, grid, ins, outs, scratch=(), after=(), flops=0, nbytes=0):
    count = len(ins)

    def run(*refs):
        body(*refs[:count], *refs[count + len(after) :])

    in_specs = [whole(arr.shape) if spec is None else spec for arr, spec in ins]
    in_specs += [pl.BlockSpec(memory_space=pl.ANY)] * len(after)
    out_specs = [whole(shape) if spec is None else spec for shape, _, spec in outs]
    return pl.pallas_call(
        run,
        name=name,
        grid=grid,
        in_specs=in_specs,
        out_specs=out_specs,
        out_shape=[jax.ShapeDtypeStruct(shape, dtype) for shape, dtype, _ in outs],
        scratch_shapes=list(scratch),
        compiler_params=pltpu.CompilerParams(vmem_limit_bytes=16 * 1024 * 1024),
        cost_estimate=pl.CostEstimate(flops=flops, bytes_accessed=nbytes, transcendentals=0),
    )(*[arr for arr, _ in ins], *after)


def hbm(array):
    return pltpu.with_memory_space_constraint(array, pltpu.HBM)


def fetch_body(src_ref, after_ref, dst_ref):
    pltpu.sync_copy(src_ref, dst_ref)


def fetch(weight, after, name):
    return pl.pallas_call(
        fetch_body,
        name=name,
        in_specs=[pl.BlockSpec(memory_space=pltpu.HBM), pl.BlockSpec(memory_space=pl.ANY)],
        out_specs=pl.BlockSpec(memory_space=pltpu.VMEM),
        out_shape=pltpu.VMEM(weight.shape, weight.dtype),
        compiler_params=pltpu.CompilerParams(vmem_limit_bytes=1024 * 1024),
        cost_estimate=pl.CostEstimate(flops=0, bytes_accessed=2 * weight.size, transcendentals=0),
    )(hbm(weight), after)


def local_call(body, name, ins, outs, scratch=(), after=(), flops=0, nbytes=0):
    vmem = pl.BlockSpec(memory_space=pltpu.VMEM)
    count = len(ins)

    def run(*refs):
        body(*refs[:count], *refs[count + len(after) :])

    return pl.pallas_call(
        run,
        name=name,
        in_specs=[vmem] * count + [pl.BlockSpec(memory_space=pl.ANY)] * len(after),
        out_specs=[vmem] * len(outs),
        out_shape=[jax.ShapeDtypeStruct(shape, dtype) for shape, dtype in outs],
        scratch_shapes=list(scratch),
        compiler_params=pltpu.CompilerParams(vmem_limit_bytes=16 * 1024 * 1024),
        cost_estimate=pl.CostEstimate(flops=flops, bytes_accessed=nbytes, transcendentals=0),
    )(*ins, *after)


def row_norm(rows):
    mean = jnp.mean(rows, axis=-1, keepdims=True)
    centered = rows - mean
    inv_std = lax.rsqrt(jnp.mean(centered * centered, axis=-1, keepdims=True) + norm_eps)
    return centered * inv_std, inv_std


def row_norm_backward(normed, inv_std, grad):
    mean_grad = jnp.mean(grad, axis=-1, keepdims=True)
    mean_mix = jnp.mean(grad * normed, axis=-1, keepdims=True)
    return inv_std * (grad - mean_grad - normed * mean_mix)


def add_parts(parts_ref):
    total = parts_ref[0].astype(F32)
    for index in range(1, parts_ref.shape[0]):
        total = total + parts_ref[index].astype(F32)
    return total


def fill_copies(copies_ref, rows):
    for index in range(copies_ref.shape[0]):
        copies_ref[index] = rows


def first_norm_body(in_ref, copies_ref):
    normed, _ = row_norm(in_ref[...].astype(F32))
    fill_copies(copies_ref, normed.astype(BF16))


def second_norm_body(parts_ref, in_ref, resid_ref, copies_ref):
    resid = (in_ref[...].astype(F32) + add_parts(parts_ref)).astype(BF16)
    resid_ref[...] = resid
    normed, _ = row_norm(resid.astype(F32))
    fill_copies(copies_ref, normed.astype(BF16))


def resid_grad_body(parts_ref, resid_ref, cot_ref, grad_ref, copies_ref, mark_ref):
    mark_ref[...] = jnp.zeros_like(mark_ref)
    normed, inv_std = row_norm(resid_ref[...].astype(F32))
    grad = row_norm_backward(normed, inv_std, add_parts(parts_ref))
    grad = (cot_ref[...].astype(F32) + grad).astype(BF16)
    grad_ref[...] = grad
    fill_copies(copies_ref, grad)


def input_grad_body(parts_ref, in_ref, grad_ref, resid_ref, ffn_ref, out_ref, block_ref):
    block_ref[...] = (resid_ref[...].astype(F32) + ffn_ref[...].astype(F32)).astype(BF16)
    normed, inv_std = row_norm(in_ref[...].astype(F32))
    grad = row_norm_backward(normed, inv_std, add_parts(parts_ref))
    out_ref[...] = (grad_ref[...].astype(F32) + grad).astype(BF16)


def pack_place(slot, half_rows):
    image, head, half = slot // 4, (slot // 2) % 2, slot % 2
    row = image * 2 * half_rows
    return row, row + half * half_rows, head * HD


def join_halves(mine_ref, other_ref, rows_ref):
    half = mine_ref.shape[0]
    rows_ref[:half] = mine_ref[...]
    rows_ref[half:] = other_ref[...]


def qkv_body(mine_ref, other_ref, w_ref, pack_ref, rows_ref):
    join_halves(mine_ref, other_ref, rows_ref)
    half_rows = pack_ref.shape[1] // 5
    for part in range(3):
        acc = dot(rows_ref[...], w_ref[part]).astype(BF16)
        for slot in range(8):
            image_row, row, col = pack_place(slot, half_rows)
            if part == 0:
                pack_ref[slot, :half_rows] = acc[row : row + half_rows, col : col + HD]
            else:
                start = half_rows * (2 * part - 1)
                pack_ref[slot, start : start + 2 * half_rows] = acc[
                    image_row : image_row + 2 * half_rows, col : col + HD
                ]


def attention_body(pack_ref, att_ref, lse_ref):
    half_rows = att_ref.shape[1]
    keys = pack_ref[:, half_rows : 3 * half_rows, :].reshape(-1, HD)
    values = pack_ref[:, 3 * half_rows :, :].reshape(-1, HD)
    scale = 1.0 / math.sqrt(HD)
    for chunk in range(4):
        queries = pack_ref[2 * chunk : 2 * chunk + 2, :half_rows, :].reshape(-1, HD)
        scores = dot(keys, queries, NT) * scale
        row_max = jnp.max(scores, axis=0, keepdims=True)
        weights = jnp.exp(scores - row_max)
        total = jnp.sum(weights, axis=0, keepdims=True)
        lse_ref[chunk] = row_max + jnp.log(total)
        mixed = dot(values, weights.astype(BF16), TN) / total
        att_ref[2 * chunk : 2 * chunk + 2] = mixed.T.astype(BF16).reshape(2, half_rows, HD)


def attention_grad_body(pack_ref, att_ref, lse_ref, grad_ref, out_ref):
    half_rows = att_ref.shape[1]
    scale = 1.0 / math.sqrt(HD)
    queries = pack_ref[:, :half_rows, :].reshape(-1, HD)
    grads = grad_ref[...].reshape(-1, HD)
    mix = grads.astype(F32) * att_ref[...].reshape(-1, HD).astype(F32)
    delta = jnp.sum(mix.T, axis=0, keepdims=True)
    lse = jnp.concatenate([lse_ref[chunk] for chunk in range(4)], axis=1)
    query_total = None
    for slot in range(8):
        keys = pack_ref[slot, half_rows : 3 * half_rows, :]
        values = pack_ref[slot, 3 * half_rows :, :]
        probs = jnp.exp(dot(keys, queries, NT) * scale - lse)
        grad_probs = dot(values, grads, NT)
        grad_scores = (probs * (grad_probs - delta) * scale).astype(BF16)
        out_ref[slot, half_rows : 3 * half_rows] = dot(grad_scores, queries).astype(BF16)
        out_ref[slot, 3 * half_rows :] = dot(probs.astype(BF16), grads).astype(BF16)
        term = dot(keys, grad_scores, TN)
        query_total = term if query_total is None else query_total + term
    out_ref[:, :half_rows] = query_total.T.astype(BF16).reshape(8, half_rows, HD)


def put_halves(own_ref, other_ref, cols, total):
    half = own_ref.shape[0]
    own_ref[:, cols] = total[:half]
    other_ref[:, cols] = total[half:].astype(BF16)


def blocks(count, size):
    def run(body):
        @pl.loop(0, count)
        def _(index):
            body(pl.ds(pl.multiple_of(index * size, size), size))

    return run


def out_body(att_ref, w_ref, own_ref, other_ref, rows_ref):
    half_rows = att_ref.shape[1]
    for slot in range(8):
        _, row, col = pack_place(slot, half_rows)
        rows_ref[row : row + half_rows, col : col + HD] = att_ref[slot]

    @blocks(w_ref.shape[1] // 512, 512)
    def _(cols):
        put_halves(own_ref, other_ref, cols, dot(rows_ref[...], w_ref[:, cols]))


def grad_act_body(all_ref, w_ref, out_ref, rows_ref):
    half = all_ref.shape[0] // 2
    section = lax.axis_index("section")

    @pl.when(pl.program_id(0) == 0)
    def _():
        rows_ref[:half] = all_ref[pl.ds(section * half, half)]
        rows_ref[half:] = all_ref[pl.ds((1 - section) * half, half)]

    out_ref[...] = dot(rows_ref[...], w_ref[...], NT)


def hidden_body(mine_ref, other_ref, w_ref, act_ref, hidden_ref, grad_ref, rows_ref):
    join_halves(mine_ref, other_ref, rows_ref)

    @blocks(w_ref.shape[1] // 256, 256)
    def _(cols):
        pre = dot(rows_ref[...], w_ref[:, cols])
        cumul = 0.5 * (1.0 + lax.erf(pre * 0.7071067811865476))
        hidden_ref[:, cols] = (pre * cumul).astype(BF16)
        slope = cumul + pre * jnp.exp(-0.5 * pre * pre) * 0.3989422804014327
        grad_ref[:, cols] = (act_ref[:, cols] * slope).astype(BF16)


def grad_norm_body(rows_ref, w_ref, own_ref, other_ref):
    @blocks(w_ref.shape[0] // 512, 512)
    def _(cols):
        put_halves(own_ref, other_ref, cols, dot(rows_ref[...], w_ref[cols, :], NT))


def down_body(rows_ref, w_ref, own_ref, other_ref):
    put_halves(own_ref, other_ref, slice(None), dot(rows_ref[...], w_ref[...]))


def out_grad_body(mine_ref, other_ref, w_ref, pack_ref):
    half_rows = pack_ref.shape[1]
    for image, rows_ref in enumerate((mine_ref, other_ref)):
        grad = dot(rows_ref[...], w_ref[...], NT).astype(BF16)
        for slot in range(4):
            _, row, col = pack_place(slot, half_rows)
            pack_ref[4 * image + slot] = grad[row : row + half_rows, col : col + HD]


def qkv_grad_body(pack_ref, w_ref, own_ref, other_ref, rows_ref):
    half_rows = pack_ref.shape[1] // 5

    @pl.when(pl.program_id(0) == 0)
    def _():
        for slot in range(8):
            _, row, col = pack_place(slot, half_rows)
            rows_ref[0, row : row + half_rows, col : col + HD] = pack_ref[slot, :half_rows]
        for slot in range(0, 8, 2):
            row, _, col = pack_place(slot, half_rows)
            for part in (1, 2):
                start = half_rows * (2 * part - 1)
                both = pack_ref[slot, start : start + 2 * half_rows].astype(F32) + pack_ref[
                    slot + 1, start : start + 2 * half_rows
                ].astype(F32)
                rows_ref[part, row : row + 2 * half_rows, col : col + HD] = both.astype(BF16)

    total = dot(rows_ref[0], w_ref[0], NT)
    for part in (1, 2):
        total = total + dot(rows_ref[part], w_ref[part], NT)
    put_halves(own_ref, other_ref, slice(None), total)


def swap_section(data):
    return lax.ppermute(data, "section", [(0, 1), (1, 0)])


def exchange(data, axis):
    return lax.all_to_all(data, axis, 0, 0)


def pair_sum(own, other):
    return (own + swap_section(other).astype(F32)).astype(BF16)


def high_groups():
    size = lax.axis_size("mp")
    return [[i, i + size // 2] for i in range(size // 2)]


def low_groups():
    size = lax.axis_size("mp")
    return [list(range(size // 2)), list(range(size // 2, size))]


def per_device(bottleneck, qkv_weight, out_weight, up_weight, down_weight, cotangent):
    own_in = bottleneck[0]
    own_cot = cotangent[0]
    rows, width = own_in.shape
    group = lax.axis_size("mp")
    seq_size = lax.axis_size("seq")
    half = rows * group
    total_rows = 2 * half
    half_rows = half // 2
    head_cols = qkv_weight.shape[2]
    units = up_weight.shape[1]
    assert (total_rows // half) * (head_cols // HD) * 2 == seq_size == 8
    copies = ((group, rows, width), BF16)
    row_out = ((rows, width), BF16)
    halves = [((half, width), F32), ((half, width), BF16)]
    att_shape = ((seq_size, half_rows, HD), BF16)
    pack_shape = ((seq_size, 5 * half_rows, HD), BF16)
    big = 2 * total_rows * width * units
    joined = pltpu.VMEM((total_rows, width), BF16)

    cot_all = lax.all_gather(own_cot, ("section", "mp"), axis=0, tiled=True)

    (send,) = local_call(first_norm_body, "first_norm", [own_in], [copies])
    weight = fetch(qkv_weight, send, "fetch_qkv")
    mine = exchange(send, "mp").reshape(half, width)
    (send,) = local_call(
        qkv_body,
        "qkv",
        [mine, swap_section(mine), weight],
        [pack_shape],
        [joined],
        flops=2 * total_rows * width * 3 * head_cols,
    )
    pack = exchange(send, "seq")
    att, lse = local_call(
        attention_body,
        "attention",
        [pack],
        [att_shape, ((4, 1, 2 * half_rows), F32)],
        flops=4 * half * half * 8 * HD,
    )
    weight = fetch(out_weight, att, "fetch_out")
    got = exchange(att, "seq")
    own, other = local_call(
        out_body,
        "attn_out",
        [got, weight],
        halves,
        [pltpu.VMEM((total_rows, head_cols), BF16)],
        after=[hbm(cot_all)],
        flops=2 * total_rows * width * head_cols,
    )
    send = pair_sum(own, other).reshape(group, rows, width)
    unit_block = units // 4
    unit_spec = pl.BlockSpec((total_rows, unit_block), lambda j: (0, j))
    (grad_act,) = kernel_call(
        grad_act_body,
        "grad_act",
        (4,),
        [
            (hbm(cot_all), None),
            (hbm(down_weight), pl.BlockSpec((unit_block, width), lambda j: (j, 0))),
        ],
        [((total_rows, units), F32, unit_spec)],
        [joined],
        after=[send],
        flops=big,
        nbytes=2 * width * units,
    )
    parts = exchange(send, "mp")
    resid, send = local_call(
        second_norm_body, "second_norm", [parts, own_in], [row_out, copies], after=[grad_act]
    )
    weight = fetch(up_weight, send, "fetch_up")
    mine = exchange(send, "mp").reshape(half, width)
    hidden, grad_hidden = local_call(
        hidden_body,
        "hidden",
        [mine, swap_section(mine), weight, grad_act],
        [((total_rows, units), BF16)] * 2,
        [joined],
        flops=big,
    )
    own, other = local_call(
        grad_norm_body, "grad_norm_two", [grad_hidden, weight], halves, flops=big
    )
    send = pair_sum(own, other).reshape(group, rows, width)
    block = width // 8
    block_spec = pl.BlockSpec((half, block), lambda j: (0, j))
    own, other = kernel_call(
        down_body,
        "down",
        (8,),
        [(hidden, None), (hbm(down_weight), pl.BlockSpec((units, block), lambda j: (0, j)))],
        [(shape, dtype, block_spec) for shape, dtype in halves],
        after=[send],
        flops=big,
        nbytes=2 * width * units,
    )
    parts = exchange(send, "mp")
    grad_resid, send, mark = local_call(
        resid_grad_body,
        "resid_grad",
        [parts, resid, own_cot],
        [row_out, copies, ((8, 128), F32)],
        after=[own],
    )
    weight = fetch(out_weight, send, "fetch_out_again")
    other, mark = lax.optimization_barrier((other, mark))
    mine = exchange(send, "mp").reshape(half, width)
    pair = pair_sum(own, other)
    ffn_high = lax.psum_scatter(
        pair, "mp", scatter_dimension=0, axis_index_groups=high_groups(), tiled=True
    )
    ffn_own = lax.psum_scatter(
        ffn_high, "mp", scatter_dimension=0, axis_index_groups=low_groups(), tiled=True
    )
    (send,) = local_call(
        out_grad_body,
        "attn_out_grad",
        [mine, swap_section(mine), weight],
        [att_shape],
        after=[mark],
        flops=2 * total_rows * width * head_cols,
    )
    grad_att = exchange(send, "seq")
    (send,) = local_call(
        attention_grad_body,
        "attention_grad",
        [pack, att, lse, grad_att],
        [pack_shape],
        after=[ffn_high],
        flops=10 * half * half * 8 * HD,
    )
    got = exchange(send, "seq")
    own, other = kernel_call(
        qkv_grad_body,
        "qkv_grad",
        (8,),
        [
            (got, None),
            (hbm(qkv_weight), pl.BlockSpec((3, block, head_cols), lambda j: (0, j, 0))),
        ],
        [(shape, dtype, block_spec) for shape, dtype in halves],
        [pltpu.VMEM((3, total_rows, head_cols), BF16)],
        flops=2 * total_rows * width * 3 * head_cols,
        nbytes=2 * width * 3 * head_cols,
    )
    parts = exchange(pair_sum(own, other).reshape(group, rows, width), "mp")
    grad_input, block_out = local_call(
        input_grad_body,
        "input_grad",
        [parts, own_in, grad_resid, resid, ffn_own],
        [row_out, row_out],
    )
    return (block_out[None], grad_input[None])


def solution(mesh):
    in_specs = (
        P("section", ("seq", "mp"), None),
        P(None, None, ("section", "mp")),
        P(("section", "mp"), None),
        P(None, ("section", "mp")),
        P(("section", "mp"), None),
        P("section", ("seq", "mp"), None),
    )
    out_specs = (P("section", ("seq", "mp"), None), P("section", ("seq", "mp"), None))
    return jax.shard_map(
        per_device, mesh=mesh, in_specs=in_specs, out_specs=out_specs, check_vma=False
    )
```

time: 380 us -> 260 us (0.68)
  waiting for transfers between devices: 161 us -> 62.2 us
  Pallas kernels: 0 us -> 54.8 us
  matrix products: 40.4 us -> 0 us
  local copies, waits for them, and re-layouts: 23.5 us -> 5.95 us
  blocking collectives: 108 us -> 93 us
  other arithmetic: 17.3 us -> 7.23 us
  starting transfers between devices: 14.4 us -> 21.7 us
    pallas_call x0 -> x18, Pallas kernels: none -> 54.8 us  [the longest x3 22.7 us: kernel_call(): pl.pallas_call(run, name=name, grid=grid, in_specs=in_specs, out_specs=ou...]
    dot_general x13 -> x0, matrix products: 40.4 us -> none  [the longest x2 14.2 us: dot_nt(): return jnp.einsum('tf,df->td', lhs, rhs, preferred_element_type=jnp.float32)]
    all_gather x1, waiting for transfers between devices: 35 us -> 0.01 us  [per_device(): cot_all = lax.all_gather(own_cot, ('section', 'mp'), axis=0, tiled=True)]
    reduce_scatter x1 -> x2, waiting for transfers between devices: 48.2 us -> 17 us  [the longest x1 17 us: per_device(): lax.psum_scatter(ffn_high, 'mp', scatter_dimension=0, axis_index_groups=l...]
    all_to_all x3 -> x5, waiting for transfers between devices: 66.6 us -> 36.5 us  [exchange(): return lax.all_to_all(data, axis, 0, 0)]
    all_to_all x5, blocking collectives: 108 us -> 93 us  [exchange(): return lax.all_to_all(data, axis, 0, 0)]
    slice x9 -> x0, local copies, waits for them, and re-layouts: 11.7 us -> none  [the longest x3 7.63 us: per_device(): key_heads, value_heads = (heads[0], heads[1])]
    reduce_sum x12 -> x0, other arithmetic: 8.18 us -> none  [the longest x2 1.93 us: norm_backward(): mean_mix = jnp.mean(grad_in * normed, axis=-1, keepdims=True)]
  transfers between devices with their start and end apart: 13 -> 15, of which waited for: 9 -> 8; matrix products, arithmetic and copies ran while one was open for 9% -> 2% of each run, Pallas kernels for 0% -> 12%
where the time goes in v2:
time: 260 us; the launch traced here: 259 us
  blocking collectives  93 us (36%)
  waiting for transfers between devices  62.2 us (24%)
  Pallas kernels  54.8 us (21%)
  starting transfers between devices  21.7 us (8%)
  between operations  13.9 us (5%)
  other arithmetic  7.23 us (3%)
  local copies, waits for them, and re-layouts  5.95 us (2%)
    all_to_all x5, blocking collectives, exchange(): return lax.all_to_all(data, axis, 0, 0)  93 us
    all_to_all x5, waiting for transfers between devices, exchange(): return lax.all_to_all(data, axis, 0, 0)  36.5 us
    pallas_call x3, Pallas kernels, kernel_call(): pl.pallas_call(run, name=name, grid=grid, in_specs=in_specs, out_specs=ou...  22.7 us
    pallas_call x11, Pallas kernels, local_call(): pl.pallas_call(run, name=name, in_specs=[vmem] * count + [pl.BlockSpec(me...  22.7 us
    all_to_all x5, starting transfers between devices, exchange(): return lax.all_to_all(data, axis, 0, 0)  20.9 us
    reduce_scatter x1, waiting for transfers between devices, per_device(): lax.psum_scatter(ffn_high, 'mp', scatter_dimension=0, axis_index_groups=l...  17 us
    pallas_call x4, Pallas kernels, fetch(): pl.pallas_call(fetch_body, name=name, in_specs=[pl.BlockSpec(memory_space...  9.37 us
    ppermute x7, waiting for transfers between devices, swap_section(): return lax.ppermute(data, 'section', [(0, 1), (1, 0)])  7.96 us
  transfers between devices with their start and end apart: 15, of which 8 were waited for; matrix products, arithmetic and copies ran while one was open for 2% of the time, Pallas kernels for 12%

profile of v2, /device:TPU:0, one launch (start us, length us, event | category | flops | bytes accessed | tf_op | source)
XLA Modules:
  0.0 258.7 jit_solution(9480377321957321325)
XLA Ops:
  9.1 26.2 %all_to_all.50 = bf16[8,16,4096]{2,1,0:T(8,128)(2,1)S(1)} all-to-all(bf16[8,16,4096]{2,1,0:T(8,128)(2,1)S(1)} %first_norm.1.after_ref), channel_id=1, replica_groups=mesh['section'=2,'seq'=8,'mp'=8] {'mp'}, dimensions={0} | all-to-all | bytes 2097152 | tf_op jit(solution)/shard_map/all_to_all | solution.py:305
  35.3 2.8 %fetch_qkv.1.refs_2_ = bf16[3,4096,256]{2,1,0:T(8,128)(2,1)S(1)} custom-call(bf16[3,4096,256]{2,1,0:T(8,128)(2,1)} %refs_1_.5, bf16[8,16,4096]{2,1,0:T(8,128)(2,1)S(1)} %first_norm.1.after_ref), custom_call_target="tpu_custom_call" | custom-call | bytes 6291456 | tf_op jit(solution)/shard_map/fetch_qkv/pallas_call | solution.py:59
  39.9 22.1 %all_to_all.51.refs_0_ = bf16[8,320,128]{2,1,0:T(8,128)(2,1)S(1)} all-to-all(bf16[8,320,128]{2,1,0:T(8,128)(2,1)S(1)} %qkv.1), channel_id=1, replica_groups=mesh['section'=2,'seq'=8,'mp'=8] {'seq'}, dimensions={0} | all-to-all | bytes 1310720 | tf_op jit(solution)/shard_map/all_to_all | solution.py:305
  64.1 3.4 %all-to-all-start.2 = ((bf16[8,64,128]{2,1,0:T(8,128)(2,1)}), bf16[8,64,128]{2,1,0:T(8,128)(2,1)S(1)}, u32[]{:S(2)}, u32[]{:S(2)}) async-start(bf16[8,64,128]{2,1,0:T(8,128)(2,1)} %get-tuple-element.23.after_ref.refs_1_), calls=%async_computation.2 | async-start | bytes 262144 | tf_op jit(solution)/shard_map/all_to_all | solution.py:305
  69.1 5.0 %all-to-all-done.2.refs_0_ = bf16[8,64,128]{2,1,0:T(8,128)(2,1)S(1)} async-done(((bf16[8,64,128]{2,1,0:T(8,128)(2,1)}), bf16[8,64,128]{2,1,0:T(8,128)(2,1)S(1)}, u32[]{:S(2)}, u32[]{:S(2)}) %all-to-all-start.2) | async-done | bytes 131104 | tf_op jit(solution)/shard_map/all_to_all | solution.py:305
  80.0 3.6 %all-to-all-start.3 = ((bf16[8,16,4096]{2,1,0:T(8,128)(2,1)}), bf16[8,16,4096]{2,1,0:T(8,128)(2,1)S(1)}, u32[]{:S(2)}, u32[]{:S(2)}) async-start(bf16[8,16,4096]{2,1,0:T(8,128)(2,1)} %bitcast.3.refs_2_), calls=%async_computation.3 | async-start | bytes 2097152 | tf_op jit(solution)/shard_map/all_to_all | solution.py:305
  83.6 6.4 %grad_act.1.refs_2_.refs_3_ = f32[256,1024]{1,0:T(8,128)S(1)} custom-call(bf16[256,4096]{1,0:T(8,128)(2,1)} %bitcast.20, bf16[1024,4096]{1,0:T(8,128)(2,1)} %refs_1_.4, bf16[8,16,4096]{2,1,0:T(8,128)(2,1)} %bitcast.3.refs_2_), custom_call_target="tpu_custom_call" | custom-call | flops 2147483648 | bytes 8388608 | tf_op jit(solution)/shard_map/grad_act/pallas_call | solution.py:37
  90.1 9.3 %all-to-all-done.3.refs_0_ = bf16[8,16,4096]{2,1,0:T(8,128)(2,1)S(1)} async-done(((bf16[8,16,4096]{2,1,0:T(8,128)(2,1)}), bf16[8,16,4096]{2,1,0:T(8,128)(2,1)S(1)}, u32[]{:S(2)}, u32[]{:S(2)}) %all-to-all-start.3) | async-done | bytes 1048608 | tf_op jit(solution)/shard_map/all_to_all | solution.py:305
  99.8 21.8 %all_to_all.52 = bf16[8,16,4096]{2,1,0:T(8,128)(2,1)S(1)} all-to-all(bf16[8,16,4096]{2,1,0:T(8,128)(2,1)S(1)} %get-tuple-element.27.after_ref), channel_id=1, replica_groups=mesh['section'=2,'seq'=8,'mp'=8] {'mp'}, dimensions={0} | all-to-all | bytes 2097152 | tf_op jit(solution)/shard_map/all_to_all | solution.py:305
  121.6 3.4 %fetch_up.1.refs_2_.refs_1_ = bf16[4096,1024]{1,0:T(8,128)(2,1)S(1)} custom-call(bf16[4096,1024]{1,0:T(8,128)(2,1)} %src_ref.6, bf16[8,16,4096]{2,1,0:T(8,128)(2,1)S(1)} %get-tuple-element.27.after_ref), custom_call_target="tpu_custom_call" | custom-call | bytes 8388608 | tf_op jit(solution)/shard_map/fetch_up/pallas_call | solution.py:59
  125.0 3.4 %hidden.1 = (bf16[256,1024]{1,0:T(8,128)(2,1)S(1)}, bf16[256,1024]{1,0:T(8,128)(2,1)S(1)}) custom-call(bf16[128,4096]{1,0:T(8,128)(2,1)S(1)} %bitcast.14, bf16[128,4096]{1,0:T(8,128)(2,1)S(1)} %collective-permute-done.2.refs_1_, bf16[4096,1024]{1,0:T(8,128)(2,1)S(1)} %fetch_up.1.refs_2_.refs_1_, f32[256,1024]{1,0:T(8,128)S(1)} %grad_act.1.refs_2_.refs_3_), custom_call_target="tpu_custom_call" | custom-call | flops 2147483648 | tf_op jit(solution)/shard_map/hidden/pallas_call | solution.py:77
  128.4 3.8 %grad_norm_two.1 = (f32[128,4096]{1,0:T(8,128)S(1)}, bf16[128,4096]{1,0:T(8,128)(2,1)S(1)}) custom-call(bf16[256,1024]{1,0:T(8,128)(2,1)S(1)} %get-tuple-element.28.refs_0_, bf16[4096,1024]{1,0:T(8,128)(2,1)S(1)} %fetch_up.1.refs_2_.refs_1_), custom_call_target="tpu_custom_call" | custom-call | flops 2147483648 | tf_op jit(solution)/shard_map/grad_norm_two/pallas_call | solution.py:77
  136.3 4.2 %all-to-all-start.5 = ((bf16[8,16,4096]{2,1,0:T(8,128)(2,1)}), bf16[8,16,4096]{2,1,0:T(8,128)(2,1)}, u32[]{:S(2)}, u32[]{:S(2)}) async-start(bf16[8,16,4096]{2,1,0:T(8,128)(2,1)} %bitcast.5.refs_2_), calls=%async_computation.5 | async-start | bytes 2097152 | tf_op jit(solution)/shard_map/all_to_all | solution.py:305
  140.5 8.4 %down.1 = (f32[128,4096]{1,0:T(8,128)S(1)}, bf16[128,4096]{1,0:T(8,128)(2,1)}) custom-call(bf16[256,1024]{1,0:T(8,128)(2,1)S(1)} %get-tuple-element.32.refs_0_, bf16[1024,4096]{1,0:T(8,128)(2,1)} %refs_1_.4, bf16[8,16,4096]{2,1,0:T(8,128)(2,1)} %bitcast.5.refs_2_), custom_call_target="tpu_custom_call" | custom-call | flops 2147483648 | bytes 8388608 | tf_op jit(solution)/shard_map/down/pallas_call | solution.py:37
  148.9 7.6 %all-to-all-done.5.refs_0_ = bf16[8,16,4096]{2,1,0:T(8,128)(2,1)} async-done(((bf16[8,16,4096]{2,1,0:T(8,128)(2,1)}), bf16[8,16,4096]{2,1,0:T(8,128)(2,1)}, u32[]{:S(2)}, u32[]{:S(2)}) %all-to-all-start.5) | async-done | bytes 1048608 | tf_op jit(solution)/shard_map/all_to_all | solution.py:305
  160.1 4.8 %all-to-all-start.6 = ((bf16[8,16,4096]{2,1,0:T(8,128)(2,1)}), bf16[8,16,4096]{2,1,0:T(8,128)(2,1)}, u32[]{:S(2)}, u32[]{:S(2)}) async-start(bf16[8,16,4096]{2,1,0:T(8,128)(2,1)} %copy-done), calls=%async_computation.6 | async-start | bytes 2097152 | tf_op jit(solution)/shard_map/all_to_all | solution.py:305
  167.4 14.6 %all-to-all-done.6 = bf16[8,16,4096]{2,1,0:T(8,128)(2,1)} async-done(((bf16[8,16,4096]{2,1,0:T(8,128)(2,1)}), bf16[8,16,4096]{2,1,0:T(8,128)(2,1)}, u32[]{:S(2)}, u32[]{:S(2)}) %all-to-all-start.6) | async-done | bytes 1048608 | tf_op jit(solution)/shard_map/all_to_all | solution.py:305
  187.6 9.4 %all_to_all.53.refs_3_ = bf16[8,64,128]{2,1,0:T(8,128)(2,1)S(1)} all-to-all(bf16[8,64,128]{2,1,0:T(8,128)(2,1)S(1)} %attn_out_grad.1), channel_id=1, replica_groups=mesh['section'=2,'seq'=8,'mp'=8] {'seq'}, dimensions={0} | all-to-all | bytes 262144 | tf_op jit(solution)/shard_map/all_to_all | solution.py:305
  198.0 3.4 %attention_grad.1 = bf16[8,320,128]{2,1,0:T(8,128)(2,1)S(1)} custom-call(bf16[8,320,128]{2,1,0:T(8,128)(2,1)S(1)} %all_to_all.51.refs_0_, bf16[8,64,128]{2,1,0:T(8,128)(2,1)} %get-tuple-element.23.after_ref.refs_1_, f32[4,1,128]{2,1,0:T(1,128)S(1)} %get-tuple-element.24.refs_2_, bf16[8,64,128]{2,1,0:T(8,128)(2,1)S(1)} %all_to_all.53.refs_3_, ...), custom_call_target="tpu_custom_call" | custom-call | flops 167772160 | tf_op jit(solution)/shard_map/attention_grad/pallas_call | solution.py:77
  201.4 13.5 %all_to_all.54.refs_0_ = bf16[8,320,128]{2,1,0:T(8,128)(2,1)S(1)} all-to-all(bf16[8,320,128]{2,1,0:T(8,128)(2,1)S(1)} %attention_grad.1), channel_id=1, replica_groups=mesh['section'=2,'seq'=8,'mp'=8] {'seq'}, dimensions={0} | all-to-all | bytes 1310720 | tf_op jit(solution)/shard_map/all_to_all | solution.py:305
  215.0 7.9 %qkv_grad.1 = (f32[128,4096]{1,0:T(8,128)S(1)}, bf16[128,4096]{1,0:T(8,128)(2,1)}) custom-call(bf16[8,320,128]{2,1,0:T(8,128)(2,1)S(1)} %all_to_all.54.refs_0_, bf16[3,4096,256]{2,1,0:T(8,128)(2,1)} %refs_1_.5), custom_call_target="tpu_custom_call" | custom-call | flops 1610612736 | bytes 6291456 | tf_op jit(solution)/shard_map/qkv_grad/pallas_call | solution.py:37
  222.9 3.0 %collective-permute-done.6 = bf16[128,4096]{1,0:T(8,128)(2,1)} collective-permute-done((bf16[128,4096]{1,0:T(8,128)(2,1)}, bf16[128,4096]{1,0:T(8,128)(2,1)}, u32[]{:S(2)}, u32[]{:S(2)}) %collective-permute-start.6) | collective-permute-done | bytes 1048608 | tf_op jit(solution)/shard_map/ppermute | solution.py:301
  228.3 4.9 %all-to-all-start.9 = ((bf16[8,16,4096]{2,1,0:T(8,128)(2,1)}), bf16[8,16,4096]{2,1,0:T(8,128)(2,1)S(1)}, u32[]{:S(2)}, u32[]{:S(2)}) async-start(bf16[8,16,4096]{2,1,0:T(8,128)(2,1)} %bitcast.21), calls=%async_computation.10 | async-start | bytes 2097152 | tf_op jit(solution)/shard_map/all_to_all | solution.py:305
  233.2 17.0 %reduce-scatter.5.cloned.1.call-done.refs_4_ = bf16[16,4096]{1,0:T(8,128)(2,1)} async-done(((bf16[64,4096]{1,0:T(8,128)(2,1)}), bf16[16,4096]{1,0:T(8,128)(2,1)}) %reduce-scatter.5.cloned.1.call-update) | async-done | bytes 131088 | tf_op jit(solution)/shard_map/reduce_scatter | solution.py:436
  (50 shorter events, 35.0 us)
Async XLA Ops:
  7.2 67.0 %all-gather.3.cloned.1.call-start = ((), (), s32[]{:S(2)}) async-start(), calls=%async_computation.14 | async-start | bytes 2228224 | tf_op jit(solution)/shard_map/all_gather | solution.py:342
  7.9 0.9 copy-start.3
  35.3 2.8 %collective-permute-start = (bf16[128,4096]{1,0:T(8,128)(2,1)S(1)}, bf16[128,4096]{1,0:T(8,128)(2,1)S(1)}, u32[]{:S(2)}, u32[]{:S(2)}) collective-permute-start(bf16[128,4096]{1,0:T(8,128)(2,1)S(1)} %bitcast.11), channel_id=1, source_target_pairs={{0,64},{64,0},{1,65},{65,1},{2,66},{66,2},{3,67},{67,3},{4,68},{68... | collective-permute-start | bytes 3145736 | tf_op jit(solution)/shard_map/ppermute | solution.py:301
  64.1 10.0 %all-to-all-start.2 = ((bf16[8,64,128]{2,1,0:T(8,128)(2,1)}), bf16[8,64,128]{2,1,0:T(8,128)(2,1)S(1)}, u32[]{:S(2)}, u32[]{:S(2)}) async-start(bf16[8,64,128]{2,1,0:T(8,128)(2,1)} %get-tuple-element.23.after_ref.refs_1_), calls=%async_computation.2 | async-start | bytes 262144 | tf_op jit(solution)/shard_map/all_to_all | solution.py:305
  76.0 2.7 %collective-permute-start.1 = (bf16[128,4096]{1,0:T(8,128)(2,1)S(1)}, bf16[128,4096]{1,0:T(8,128)(2,1)S(1)}, u32[]{:S(2)}, u32[]{:S(2)}) collective-permute-start(bf16[128,4096]{1,0:T(8,128)(2,1)S(1)} %get-tuple-element.26), channel_id=1, source_target_pairs={{0,64},{64,0},{1,65},{65,1},{2,66},{66,2},{3,67},{67,3},{4,68},{68... | collective-permute-start | bytes 3145736 | tf_op jit(solution)/shard_map/ppermute | solution.py:301
  80.0 19.3 %all-to-all-start.3 = ((bf16[8,16,4096]{2,1,0:T(8,128)(2,1)}), bf16[8,16,4096]{2,1,0:T(8,128)(2,1)S(1)}, u32[]{:S(2)}, u32[]{:S(2)}) async-start(bf16[8,16,4096]{2,1,0:T(8,128)(2,1)} %bitcast.3.refs_2_), calls=%async_computation.3 | async-start | bytes 2097152 | tf_op jit(solution)/shard_map/all_to_all | solution.py:305
  83.6 15.8 %copy-start.4 = (bf16[1,16,4096]{2,1,0:T(8,128)(2,1)S(1)}, bf16[1,16,4096]{2,1,0:T(8,128)(2,1)}, u32[]{:S(2)}) copy-start(bf16[1,16,4096]{2,1,0:T(8,128)(2,1)} %param.6) | copy-start | bytes 393220
  121.6 3.4 %collective-permute-start.2 = (bf16[128,4096]{1,0:T(8,128)(2,1)S(1)}, bf16[128,4096]{1,0:T(8,128)(2,1)S(1)}, u32[]{:S(2)}, u32[]{:S(2)}) collective-permute-start(bf16[128,4096]{1,0:T(8,128)(2,1)S(1)} %bitcast.13), channel_id=1, source_target_pairs={{0,64},{64,0},{1,65},{65,1},{2,66},{66,2},{3,67},{67,3},{4,68},{68... | collective-permute-start | bytes 3145736 | tf_op jit(solution)/shard_map/ppermute | solution.py:301
  132.2 2.9 %collective-permute-start.3 = (bf16[128,4096]{1,0:T(8,128)(2,1)S(1)}, bf16[128,4096]{1,0:T(8,128)(2,1)S(1)}, u32[]{:S(2)}, u32[]{:S(2)}) collective-permute-start(bf16[128,4096]{1,0:T(8,128)(2,1)S(1)} %get-tuple-element.30), channel_id=1, source_target_pairs={{0,64},{64,0},{1,65},{65,1},{2,66},{66,2},{3,67},{67,3},{4,68},{68... | collective-permute-start | bytes 3145736 | tf_op jit(solution)/shard_map/ppermute | solution.py:301
  136.3 20.2 %all-to-all-start.5 = ((bf16[8,16,4096]{2,1,0:T(8,128)(2,1)}), bf16[8,16,4096]{2,1,0:T(8,128)(2,1)}, u32[]{:S(2)}, u32[]{:S(2)}) async-start(bf16[8,16,4096]{2,1,0:T(8,128)(2,1)} %bitcast.5.refs_2_), calls=%async_computation.5 | async-start | bytes 2097152 | tf_op jit(solution)/shard_map/all_to_all | solution.py:305
  156.5 0.9 copy-start.5
  159.1 1.0 copy-start
  160.1 4.8 %collective-permute-start.5 = (bf16[128,4096]{1,0:T(8,128)(2,1)}, bf16[128,4096]{1,0:T(8,128)(2,1)}, u32[]{:S(2)}, u32[]{:S(2)}) collective-permute-start(bf16[128,4096]{1,0:T(8,128)(2,1)} %get-tuple-element.38), channel_id=1, source_target_pairs={{0,64},{64,0},{1,65},{65,1},{2,66},{66,2},{3,67},{67,3},{4,68},{68... | collective-permute-start | bytes 3145736 | tf_op jit(solution)/shard_map/ppermute | solution.py:301
  160.1 21.9 %all-to-all-start.6 = ((bf16[8,16,4096]{2,1,0:T(8,128)(2,1)}), bf16[8,16,4096]{2,1,0:T(8,128)(2,1)}, u32[]{:S(2)}, u32[]{:S(2)}) async-start(bf16[8,16,4096]{2,1,0:T(8,128)(2,1)} %copy-done), calls=%async_computation.6 | async-start | bytes 2097152 | tf_op jit(solution)/shard_map/all_to_all | solution.py:305
  164.9 32.1 %reduce-scatter.3.cloned.1.call-start = ((), (), s32[]{:S(2)}) async-start(), calls=%async_computation.12 | async-start | bytes 1572864 | tf_op jit(solution)/shard_map/reduce_scatter | solution.py:433
  167.4 82.8 %reduce-scatter.5.cloned.1.call-start = ((), (), s32[]{:S(2)}) async-start(), calls=%async_computation.13 | async-start | bytes 655360 | tf_op jit(solution)/shard_map/reduce_scatter | solution.py:436
  182.0 2.9 %collective-permute-start.4 = (bf16[128,4096]{1,0:T(8,128)(2,1)}, bf16[128,4096]{1,0:T(8,128)(2,1)S(1)}, u32[]{:S(2)}, u32[]{:S(2)}) collective-permute-start(bf16[128,4096]{1,0:T(8,128)(2,1)} %bitcast.7.refs_0_), channel_id=1, source_target_pairs={{0,64},{64,0},{1,65},{65,1},{2,66},{66,2},{3,67},{67,3},{4,68},{68... | collective-permute-start | bytes 3145736 | tf_op jit(solution)/shard_map/ppermute | solution.py:301
  182.0 1.2 copy-start.1
  197.0 1.0 copy-start.2
  222.9 3.0 %collective-permute-start.6 = (bf16[128,4096]{1,0:T(8,128)(2,1)}, bf16[128,4096]{1,0:T(8,128)(2,1)}, u32[]{:S(2)}, u32[]{:S(2)}) collective-permute-start(bf16[128,4096]{1,0:T(8,128)(2,1)} %get-tuple-element.40), channel_id=1, source_target_pairs={{0,64},{64,0},{1,65},{65,1},{2,66},{66,2},{3,67},{67,3},{4,68},{68... | collective-permute-start | bytes 3145736 | tf_op jit(solution)/shard_map/ppermute | solution.py:301
  228.3 21.9 %all-to-all-start.9 = ((bf16[8,16,4096]{2,1,0:T(8,128)(2,1)}), bf16[8,16,4096]{2,1,0:T(8,128)(2,1)S(1)}, u32[]{:S(2)}, u32[]{:S(2)}) async-start(bf16[8,16,4096]{2,1,0:T(8,128)(2,1)} %bitcast.21), calls=%async_computation.10 | async-start | bytes 2097152 | tf_op jit(solution)/shard_map/all_to_all | solution.py:305
  250.2 0.9 copy-start.6
Sparse Core Ops, SparseCore 0:
  10.5 54.6 all-gather.2
  168.1 24.8 reduce-scatter.2
  223.0 27.0 reduce-scatter.4

commit v3 on v2

--- a/solution.py
+++ b/solution.py
@@ -1,3 +1,4 @@
+import functools
 import math
 
 import jax
@@ -51,39 +52,66 @@
     return pltpu.with_memory_space_constraint(array, pltpu.HBM)
 
 
-def fetch_body(src_ref, after_ref, dst_ref):
-    pltpu.sync_copy(src_ref, dst_ref)
-
-
-def fetch(weight, after, name):
+def fetch(weight, after, name, part=0, parts=1):
+    rows = weight.shape[0] // parts
+
+    def fetch_body(src_ref, after_ref, dst_ref):
+        pltpu.sync_copy(src_ref.at[pl.ds(part * rows, rows)], dst_ref)
+
     return pl.pallas_call(
         fetch_body,
         name=name,
         in_specs=[pl.BlockSpec(memory_space=pltpu.HBM), pl.BlockSpec(memory_space=pl.ANY)],
         out_specs=pl.BlockSpec(memory_space=pltpu.VMEM),
-        out_shape=pltpu.VMEM(weight.shape, weight.dtype),
+        out_shape=pltpu.VMEM((rows,) + weight.shape[1:], weight.dtype),
         compiler_params=pltpu.CompilerParams(vmem_limit_bytes=1024 * 1024),
-        cost_estimate=pl.CostEstimate(flops=0, bytes_accessed=2 * weight.size, transcendentals=0),
+        cost_estimate=pl.CostEstimate(
+            flops=0, bytes_accessed=2 * weight.size // parts, transcendentals=0
+        ),
     )(hbm(weight), after)
 
 
-def local_call(body, name, ins, outs, scratch=(), after=(), flops=0, nbytes=0):
+def local_call(
+    body, name, ins, outs, scratch=(), after=(), late=(), aliases=None, flops=0, nbytes=0
+):
     vmem = pl.BlockSpec(memory_space=pltpu.VMEM)
-    count = len(ins)
+    count, extra = len(ins), len(late)
 
     def run(*refs):
-        body(*refs[:count], *refs[count + len(after) :])
-
+        sources = refs[count : count + extra]
+        rest = refs[count + extra + len(after) :]
+        if not extra:
+            body(*refs[:count], *rest)
+            return
+        buffers, sems = rest[-1 - extra : -1], rest[-1]
+        moves = [
+            pltpu.make_async_copy(source, buffer, sems.at[index])
+            for index, (source, buffer) in enumerate(zip(sources, buffers))
+        ]
+        for move in moves:
+            move.start()
+
+        def wait():
+            for move in moves:
+                move.wait()
+
+        body(*refs[:count], *buffers, *rest[: -1 - extra], wait)
+
+    scratch = list(scratch)
+    if extra:
+        scratch += [pltpu.VMEM(arr.shape, arr.dtype) for arr in late]
+        scratch.append(pltpu.SemaphoreType.DMA((extra,)))
     return pl.pallas_call(
         run,
         name=name,
-        in_specs=[vmem] * count + [pl.BlockSpec(memory_space=pl.ANY)] * len(after),
+        in_specs=[vmem] * count + [pl.BlockSpec(memory_space=pl.ANY)] * (extra + len(after)),
         out_specs=[vmem] * len(outs),
         out_shape=[jax.ShapeDtypeStruct(shape, dtype) for shape, dtype in outs],
-        scratch_shapes=list(scratch),
+        scratch_shapes=scratch,
+        input_output_aliases=aliases or {},
         compiler_params=pltpu.CompilerParams(vmem_limit_bytes=16 * 1024 * 1024),
         cost_estimate=pl.CostEstimate(flops=flops, bytes_accessed=nbytes, transcendentals=0),
-    )(*ins, *after)
+    )(*ins, *late, *after)
 
 
 def row_norm(rows):
@@ -117,7 +145,8 @@
 
 
 def second_norm_body(parts_ref, in_ref, resid_ref, copies_ref):
-    resid = (in_ref[...].astype(F32) + add_parts(parts_ref)).astype(BF16)
+    total = add_parts(parts_ref)
+    resid = (in_ref[...].astype(F32) + total).astype(BF16)
     resid_ref[...] = resid
     normed, _ = row_norm(resid.astype(F32))
     fill_copies(copies_ref, normed.astype(BF16))
@@ -125,17 +154,23 @@
 
 def resid_grad_body(parts_ref, resid_ref, cot_ref, grad_ref, copies_ref, mark_ref):
     mark_ref[...] = jnp.zeros_like(mark_ref)
+    total = add_parts(parts_ref)
     normed, inv_std = row_norm(resid_ref[...].astype(F32))
-    grad = row_norm_backward(normed, inv_std, add_parts(parts_ref))
+    grad = row_norm_backward(normed, inv_std, total)
     grad = (cot_ref[...].astype(F32) + grad).astype(BF16)
     grad_ref[...] = grad
     fill_copies(copies_ref, grad)
 
 
-def input_grad_body(parts_ref, in_ref, grad_ref, resid_ref, ffn_ref, out_ref, block_ref):
-    block_ref[...] = (resid_ref[...].astype(F32) + ffn_ref[...].astype(F32)).astype(BF16)
+def input_grad_body(
+    parts_ref, in_ref, grad_ref, resid_ref, near_ref, far_ref, out_ref, block_ref, wait
+):
+    total = add_parts(parts_ref)
+    wait()
+    ffn = near_ref[...].astype(F32) + far_ref[...].astype(F32)
+    block_ref[...] = (resid_ref[...].astype(F32) + ffn).astype(BF16)
     normed, inv_std = row_norm(in_ref[...].astype(F32))
-    grad = row_norm_backward(normed, inv_std, add_parts(parts_ref))
+    grad = row_norm_backward(normed, inv_std, total)
     out_ref[...] = (grad_ref[...].astype(F32) + grad).astype(BF16)
 
 
@@ -151,7 +186,9 @@
     rows_ref[half:] = other_ref[...]
 
 
-def qkv_body(mine_ref, other_ref, w_ref, pack_ref, rows_ref):
+def qkv_body(
+    mine_ref, other_ref, w_ref, pack_ref, rows_ref
+):
     join_halves(mine_ref, other_ref, rows_ref)
     half_rows = pack_ref.shape[1] // 5
     for part in range(3):
@@ -207,47 +244,72 @@
 
 def put_halves(own_ref, other_ref, cols, total):
     half = own_ref.shape[0]
-    own_ref[:, cols] = total[:half]
+    own_ref[:, cols] = total[:half].astype(BF16)
     other_ref[:, cols] = total[half:].astype(BF16)
 
 
-def blocks(count, size):
-    def run(body):
-        @pl.loop(0, count)
-        def _(index):
-            body(pl.ds(pl.multiple_of(index * size, size), size))
-
-    return run
-
-
-def out_body(att_ref, w_ref, own_ref, other_ref, rows_ref):
+def out_body(start, att_ref, w_ref, own_ref, other_ref, rows_ref):
     half_rows = att_ref.shape[1]
     for slot in range(8):
         _, row, col = pack_place(slot, half_rows)
         rows_ref[row : row + half_rows, col : col + HD] = att_ref[slot]
-
-    @blocks(w_ref.shape[1] // 512, 512)
-    def _(cols):
-        put_halves(own_ref, other_ref, cols, dot(rows_ref[...], w_ref[:, cols]))
-
-
-def grad_act_body(all_ref, w_ref, out_ref, rows_ref):
-    half = all_ref.shape[0] // 2
-    section = lax.axis_index("section")
-
+    size = 512
+    for step in range(own_ref.shape[1] // size):
+        cols = slice(start + step * size, start + (step + 1) * size)
+        total = dot(rows_ref[...], w_ref[:, cols])
+        put_halves(own_ref, other_ref, slice(step * size, (step + 1) * size), total)
+
+
+def join_low_body(*refs):
+    out_ref = refs[-1]
+    count = len(refs) - 1
+    low = lax.rem(lax.axis_index("mp"), count)
+    high = lax.axis_index("mp") // count
+    rows = refs[0].shape[1]
+    for step in range(count):
+        source = lax.rem(low + count - step, count)
+        for side, place in ((0, high), (1, 1 - high)):
+            start = pl.multiple_of((place * count + source) * rows, rows)
+            out_ref[pl.ds(start, rows)] = refs[step][side]
+
+
+def split_low_body(own_ref, other_ref, *out_refs):
+    count = len(out_refs)
+    low = lax.rem(lax.axis_index("mp"), count)
+    high = lax.axis_index("mp") // count
+    rows = out_refs[0].shape[1]
+    for step in range(count):
+        target = lax.rem(low + step, count)
+        for side, place in ((0, high), (1, 1 - high)):
+            start = pl.multiple_of((place * count + target) * rows, rows)
+            total = own_ref[pl.ds(start, rows)].astype(F32) + other_ref[pl.ds(start, rows)].astype(F32)
+            out_refs[step][side] = total.astype(BF16)
+
+
+def sum_low_body(*refs):
+    near_ref, far_ref = refs[-2:]
+    for side, out_ref in enumerate((near_ref, far_ref)):
+        total = refs[0][side].astype(F32)
+        for ref in refs[1:-2]:
+            total = total + ref[side].astype(F32)
+        out_ref[...] = total.astype(BF16)
+
+
+def grad_act_body(mine_ref, other_ref, w_ref, out_ref, rows_ref):
     @pl.when(pl.program_id(0) == 0)
     def _():
-        rows_ref[:half] = all_ref[pl.ds(section * half, half)]
-        rows_ref[half:] = all_ref[pl.ds((1 - section) * half, half)]
+        join_halves(mine_ref, other_ref, rows_ref)
 
     out_ref[...] = dot(rows_ref[...], w_ref[...], NT)
 
 
-def hidden_body(mine_ref, other_ref, w_ref, act_ref, hidden_ref, grad_ref, rows_ref):
+def hidden_body(
+    mine_ref, other_ref, w_ref, act_ref, hidden_ref, grad_ref, rows_ref
+):
     join_halves(mine_ref, other_ref, rows_ref)
 
-    @blocks(w_ref.shape[1] // 256, 256)
-    def _(cols):
+    for step in range(w_ref.shape[1] // 256):
+        cols = slice(step * 256, (step + 1) * 256)
         pre = dot(rows_ref[...], w_ref[:, cols])
         cumul = 0.5 * (1.0 + lax.erf(pre * 0.7071067811865476))
         hidden_ref[:, cols] = (pre * cumul).astype(BF16)
@@ -255,46 +317,67 @@
         grad_ref[:, cols] = (act_ref[:, cols] * slope).astype(BF16)
 
 
-def grad_norm_body(rows_ref, w_ref, own_ref, other_ref):
-    @blocks(w_ref.shape[0] // 512, 512)
-    def _(cols):
-        put_halves(own_ref, other_ref, cols, dot(rows_ref[...], w_ref[cols, :], NT))
+def grad_norm_body(start, rows_ref, w_ref, own_ref, other_ref):
+    size = 512
+    for step in range(own_ref.shape[1] // size):
+        source = slice(start + step * size, start + (step + 1) * size)
+        total = dot(rows_ref[...], w_ref[source, :], NT)
+        put_halves(own_ref, other_ref, slice(step * size, (step + 1) * size), total)
+
+
+def pair_body(*refs):
+    out_ref = refs[-1]
+    size = refs[0].shape[1]
+    for index in range(2):
+        total = refs[2 * index][...].astype(F32) + refs[2 * index + 1][...].astype(F32)
+        out_ref[:, index * size : (index + 1) * size] = total.astype(BF16)
 
 
 def down_body(rows_ref, w_ref, own_ref, other_ref):
     put_halves(own_ref, other_ref, slice(None), dot(rows_ref[...], w_ref[...]))
 
 
-def out_grad_body(mine_ref, other_ref, w_ref, pack_ref):
+def out_grad_body(mine_ref, other_ref, w_ref, pack_ref, rows_ref):
+    join_halves(mine_ref, other_ref, rows_ref)
     half_rows = pack_ref.shape[1]
-    for image, rows_ref in enumerate((mine_ref, other_ref)):
-        grad = dot(rows_ref[...], w_ref[...], NT).astype(BF16)
-        for slot in range(4):
-            _, row, col = pack_place(slot, half_rows)
-            pack_ref[4 * image + slot] = grad[row : row + half_rows, col : col + HD]
-
-
-def qkv_grad_body(pack_ref, w_ref, own_ref, other_ref, rows_ref):
+    grad = dot(rows_ref[...], w_ref[...], NT).astype(BF16)
+    for slot in range(8):
+        _, row, col = pack_place(slot, half_rows)
+        pack_ref[slot] = grad[row : row + half_rows, col : col + HD]
+
+
+def qkv_grad_body(base, pack_ref, w_ref, *refs):
+    own_ref, other_ref, rows_ref, w_buf, sems = refs[-5:]
     half_rows = pack_ref.shape[1] // 5
-
-    @pl.when(pl.program_id(0) == 0)
-    def _():
-        for slot in range(8):
-            _, row, col = pack_place(slot, half_rows)
-            rows_ref[0, row : row + half_rows, col : col + HD] = pack_ref[slot, :half_rows]
-        for slot in range(0, 8, 2):
-            row, _, col = pack_place(slot, half_rows)
-            for part in (1, 2):
-                start = half_rows * (2 * part - 1)
-                both = pack_ref[slot, start : start + 2 * half_rows].astype(F32) + pack_ref[
-                    slot + 1, start : start + 2 * half_rows
-                ].astype(F32)
-                rows_ref[part, row : row + 2 * half_rows, col : col + HD] = both.astype(BF16)
-
-    total = dot(rows_ref[0], w_ref[0], NT)
-    for part in (1, 2):
-        total = total + dot(rows_ref[part], w_ref[part], NT)
-    put_halves(own_ref, other_ref, slice(None), total)
+    steps = sems.shape[0]
+    size = w_buf.shape[1] // steps
+
+    def move(step):
+        source = pl.ds(base + step * size, size)
+        cols = pl.ds(step * size, size)
+        return pltpu.make_async_copy(w_ref.at[:, source, :], w_buf.at[:, cols, :], sems.at[step])
+
+    for step in range(steps):
+        move(step).start()
+    for slot in range(8):
+        _, row, col = pack_place(slot, half_rows)
+        rows_ref[0, row : row + half_rows, col : col + HD] = pack_ref[slot, :half_rows]
+    for slot in range(0, 8, 2):
+        row, _, col = pack_place(slot, half_rows)
+        for part in (1, 2):
+            start = half_rows * (2 * part - 1)
+            both = pack_ref[slot, start : start + 2 * half_rows].astype(F32) + pack_ref[
+                slot + 1, start : start + 2 * half_rows
+            ].astype(F32)
+            rows_ref[part, row : row + 2 * half_rows, col : col + HD] = both.astype(BF16)
+
+    for step in range(steps):
+        move(step).wait()
+        cols = slice(step * size, (step + 1) * size)
+        total = dot(rows_ref[0], w_buf[0, cols, :], NT)
+        for part in (1, 2):
+            total = total + dot(rows_ref[part], w_buf[part, cols, :], NT)
+        put_halves(own_ref, other_ref, cols, total)
 
 
 def swap_section(data):
@@ -305,18 +388,28 @@
     return lax.all_to_all(data, axis, 0, 0)
 
 
+def by_columns(partial, half, width, after=()):
+    sides = [partial(start) for start in (0, width // 2)]
+    ins = []
+    for own, other in sides:
+        ins += [own, swap_section(other)]
+    (total,) = local_call(pair_body, "pair", ins, [((half, width), BF16)], after=after)
+    return total
+
+
 def pair_sum(own, other):
-    return (own + swap_section(other).astype(F32)).astype(BF16)
-
-
-def high_groups():
+    return (own.astype(F32) + swap_section(other).astype(F32)).astype(BF16)
+
+
+def shift_high(data):
     size = lax.axis_size("mp")
-    return [[i, i + size // 2] for i in range(size // 2)]
-
-
-def low_groups():
-    size = lax.axis_size("mp")
-    return [list(range(size // 2)), list(range(size // 2, size))]
+    return lax.ppermute(data, "mp", [(i, (i + size // 2) % size) for i in range(size)])
+
+
+def shift_low(data, step):
+    size = lax.axis_size("mp") // 2
+    pairs = [(h * size + i, h * size + (i + step) % size) for h in range(2) for i in range(size)]
+    return lax.ppermute(data, "mp", pairs)
 
 
 def per_device(bottleneck, qkv_weight, out_weight, up_weight, down_weight, cotangent):
@@ -333,17 +426,20 @@
     assert (total_rows // half) * (head_cols // HD) * 2 == seq_size == 8
     copies = ((group, rows, width), BF16)
     row_out = ((rows, width), BF16)
-    halves = [((half, width), F32), ((half, width), BF16)]
+    halves = [((half, width), BF16)] * 2
+    column_halves = [((half, width // 2), BF16)] * 2
     att_shape = ((seq_size, half_rows, HD), BF16)
     pack_shape = ((seq_size, 5 * half_rows, HD), BF16)
     big = 2 * total_rows * width * units
     joined = pltpu.VMEM((total_rows, width), BF16)
 
-    cot_all = lax.all_gather(own_cot, ("section", "mp"), axis=0, tiled=True)
-
     (send,) = local_call(first_norm_body, "first_norm", [own_in], [copies])
+    send, cot_near = lax.optimization_barrier((send, own_cot))
+    cot_far = shift_high(cot_near)
     weight = fetch(qkv_weight, send, "fetch_qkv")
-    mine = exchange(send, "mp").reshape(half, width)
+    mine, cot_far = lax.optimization_barrier((exchange(send, "mp"), cot_far))
+    mine = mine.reshape(half, width)
+    cot_two = jnp.stack([cot_near, cot_far])
     (send,) = local_call(
         qkv_body,
         "qkv",
@@ -352,7 +448,9 @@
         [joined],
         flops=2 * total_rows * width * 3 * head_cols,
     )
+    send, cot_two = lax.optimization_barrier((send, cot_two))
     pack = exchange(send, "seq")
+    cot_shifted = [shift_low(cot_two, step) for step in range(1, group // 2)]
     att, lse = local_call(
         attention_body,
         "attention",
@@ -362,16 +460,26 @@
     )
     weight = fetch(out_weight, att, "fetch_out")
     got = exchange(att, "seq")
-    own, other = local_call(
-        out_body,
-        "attn_out",
-        [got, weight],
-        halves,
-        [pltpu.VMEM((total_rows, head_cols), BF16)],
-        after=[hbm(cot_all)],
-        flops=2 * total_rows * width * head_cols,
-    )
-    send = pair_sum(own, other).reshape(group, rows, width)
+    (cot_mine,) = local_call(
+        join_low_body,
+        "join_cotangent",
+        [cot_two, *cot_shifted],
+        [((half, width), BF16)],
+        after=[att],
+    )
+    cots = [cot_mine, swap_section(cot_mine)]
+
+    def attn_out(start):
+        return local_call(
+            functools.partial(out_body, start),
+            "attn_out",
+            [got, weight],
+            column_halves,
+            [pltpu.VMEM((total_rows, head_cols), BF16)],
+            after=[cot_mine],
+        )
+
+    send = by_columns(attn_out, half, width).reshape(group, rows, width)
     unit_block = units // 4
     unit_spec = pl.BlockSpec((total_rows, unit_block), lambda j: (0, j))
     (grad_act,) = kernel_call(
@@ -379,7 +487,7 @@
         "grad_act",
         (4,),
         [
-            (hbm(cot_all), None),
+            *[(cot, None) for cot in cots],
             (hbm(down_weight), pl.BlockSpec((unit_block, width), lambda j: (j, 0))),
         ],
         [((total_rows, units), F32, unit_spec)],
@@ -392,8 +500,8 @@
     resid, send = local_call(
         second_norm_body, "second_norm", [parts, own_in], [row_out, copies], after=[grad_act]
     )
+    mine = exchange(send, "mp").reshape(half, width)
     weight = fetch(up_weight, send, "fetch_up")
-    mine = exchange(send, "mp").reshape(half, width)
     hidden, grad_hidden = local_call(
         hidden_body,
         "hidden",
@@ -402,10 +510,16 @@
         [joined],
         flops=big,
     )
-    own, other = local_call(
-        grad_norm_body, "grad_norm_two", [grad_hidden, weight], halves, flops=big
-    )
-    send = pair_sum(own, other).reshape(group, rows, width)
+
+    def grad_norm_two(start):
+        return local_call(
+            functools.partial(grad_norm_body, start),
+            "grad_norm_two",
+            [grad_hidden, weight],
+            column_halves,
+        )
+
+    send = by_columns(grad_norm_two, half, width).reshape(group, rows, width)
     block = width // 8
     block_spec = pl.BlockSpec((half, block), lambda j: (0, j))
     own, other = kernel_call(
@@ -428,19 +542,20 @@
     )
     weight = fetch(out_weight, send, "fetch_out_again")
     other, mark = lax.optimization_barrier((other, mark))
-    mine = exchange(send, "mp").reshape(half, width)
-    pair = pair_sum(own, other)
-    ffn_high = lax.psum_scatter(
-        pair, "mp", scatter_dimension=0, axis_index_groups=high_groups(), tiled=True
-    )
-    ffn_own = lax.psum_scatter(
-        ffn_high, "mp", scatter_dimension=0, axis_index_groups=low_groups(), tiled=True
-    )
+    sums_low = local_call(
+        split_low_body,
+        "split_sums",
+        [own, swap_section(other)],
+        [((2, rows, width), BF16)] * (group // 2),
+    )
+    mine, *sums_low = lax.optimization_barrier((exchange(send, "mp"), *sums_low))
+    mine = mine.reshape(half, width)
     (send,) = local_call(
         out_grad_body,
         "attn_out_grad",
         [mine, swap_section(mine), weight],
         [att_shape],
+        [joined],
         after=[mark],
         flops=2 * total_rows * width * head_cols,
     )
@@ -450,29 +565,42 @@
         "attention_grad",
         [pack, att, lse, grad_att],
         [pack_shape],
-        after=[ffn_high],
         flops=10 * half * half * 8 * HD,
     )
+    send, *sums_low = lax.optimization_barrier((send, *sums_low))
+    shifted = [shift_low(sums_low[step], step) for step in range(1, group // 2)]
+    sum_near, sum_far = local_call(
+        sum_low_body, "join_sums", [sums_low[0], *shifted], [row_out] * 2
+    )
+    sum_far = shift_high(sum_far)
     got = exchange(send, "seq")
-    own, other = kernel_call(
-        qkv_grad_body,
-        "qkv_grad",
-        (8,),
-        [
-            (got, None),
-            (hbm(qkv_weight), pl.BlockSpec((3, block, head_cols), lambda j: (0, j, 0))),
-        ],
-        [(shape, dtype, block_spec) for shape, dtype in halves],
-        [pltpu.VMEM((3, total_rows, head_cols), BF16)],
-        flops=2 * total_rows * width * 3 * head_cols,
-        nbytes=2 * width * 3 * head_cols,
-    )
-    parts = exchange(pair_sum(own, other).reshape(group, rows, width), "mp")
+    vmem = pl.BlockSpec(memory_space=pltpu.VMEM)
+
+    def qkv_grad(start):
+        after = shifted if start == 0 else [sum_near]
+        return pl.pallas_call(
+            functools.partial(qkv_grad_body, start),
+            name="qkv_grad",
+            in_specs=[vmem, pl.BlockSpec(memory_space=pltpu.HBM)]
+            + [pl.BlockSpec(memory_space=pl.ANY)] * len(after),
+            out_specs=[vmem] * 2,
+            out_shape=[jax.ShapeDtypeStruct(shape, dtype) for shape, dtype in column_halves],
+            scratch_shapes=[
+                pltpu.VMEM((3, total_rows, head_cols), BF16),
+                pltpu.VMEM((3, width // 2, head_cols), BF16),
+                pltpu.SemaphoreType.DMA((4,)),
+            ],
+            compiler_params=pltpu.CompilerParams(vmem_limit_bytes=16 * 1024 * 1024),
+            cost_estimate=pl.CostEstimate(flops=0, bytes_accessed=0, transcendentals=0),
+        )(got, hbm(qkv_weight), *after)
+
+    parts = exchange(by_columns(qkv_grad, half, width, [sum_far]).reshape(group, rows, width), "mp")
     grad_input, block_out = local_call(
         input_grad_body,
         "input_grad",
-        [parts, own_in, grad_resid, resid, ffn_own],
+        [parts],
         [row_out, row_out],
+        late=[hbm(own_in), grad_resid, resid, sum_near, sum_far],
     )
     return (block_out[None], grad_input[None])
 

time: 260 us -> 243 us (0.935)
  blocking collectives: 93 us -> 56 us
  starting transfers between devices: 21.7 us -> 50.7 us
  between operations: 13.9 us -> 1.08 us
  other arithmetic: 7.23 us -> 0.03 us
  waiting for transfers between devices: 62.2 us -> 69.1 us
  local copies, waits for them, and re-layouts: 5.95 us -> 10.5 us
    all_to_all x5 -> x3, blocking collectives: 93 us -> 56 us  [exchange(): return lax.all_to_all(data, axis, 0, 0)]
    ppermute x0 -> x8, waiting for transfers between devices: none -> 28.3 us  [the longest x2 18.9 us: shift_high(): lax.ppermute(data, 'mp', [(i, (i + size // 2) % size) for i in range(size)])]
    reduce_scatter x2 -> x0, waiting for transfers between devices: 17 us -> none  [the longest x1 17 us: per_device(): lax.psum_scatter(ffn_high, 'mp', scatter_dimension=0, axis_index_groups=l...]
    ppermute x0 -> x8, starting transfers between devices: none -> 15.8 us  [the longest x6 9.76 us: shift_low(): return lax.ppermute(data, 'mp', pairs)]
    all_to_all x5 -> x7, starting transfers between devices: 20.9 us -> 32.6 us  [exchange(): return lax.all_to_all(data, axis, 0, 0)]
    pallas_call x3 -> x2, Pallas kernels: 22.7 us -> 13.2 us  [kernel_call(): pl.pallas_call(run, name=name, grid=grid, in_specs=in_specs, out_specs=ou...]
    convert_element_type x4 -> x0, other arithmetic: 7.23 us -> none  [pair_sum(): return (own + swap_section(other).astype(F32)).astype(BF16)]
    pallas_call x0 -> x2, Pallas kernels: none -> 5.57 us  [qkv_grad(): pl.pallas_call(functools.partial(qkv_grad_body, start), name='qkv_grad',...]
  transfers between devices with their start and end apart: 15 -> 26, of which waited for: 8 -> 13; matrix products, arithmetic and copies ran while one was open for 2% -> 0% of each run, Pallas kernels for 12% -> 13%
where the time goes in v3:
time: 243 us; the launch traced here: 242 us
  waiting for transfers between devices  69.1 us (28%)
  blocking collectives  56 us (23%)
  Pallas kernels  54.1 us (22%)
  starting transfers between devices  50.7 us (21%)
  local copies, waits for them, and re-layouts  10.5 us (4%)
    all_to_all x3, blocking collectives, exchange(): return lax.all_to_all(data, axis, 0, 0)  56 us
    all_to_all x7, waiting for transfers between devices, exchange(): return lax.all_to_all(data, axis, 0, 0)  36 us
    all_to_all x7, starting transfers between devices, exchange(): return lax.all_to_all(data, axis, 0, 0)  32.6 us
    pallas_call x19, Pallas kernels, local_call(): pl.pallas_call(run, name=name, in_specs=[vmem] * count + [pl.BlockSpec(me...  25.9 us
    ppermute x2, waiting for transfers between devices, shift_high(): lax.ppermute(data, 'mp', [(i, (i + size // 2) % size) for i in range(size)])  18.9 us
    pallas_call x2, Pallas kernels, kernel_call(): pl.pallas_call(run, name=name, grid=grid, in_specs=in_specs, out_specs=ou...  13.2 us
    unnamed x34, local copies, waits for them, and re-layouts  10.5 us
    ppermute x6, starting transfers between devices, shift_low(): return lax.ppermute(data, 'mp', pairs)  9.76 us
  transfers between devices with their start and end apart: 26, of which 13 were waited for; matrix products, arithmetic and copies ran while one was open for 0% of the time, Pallas kernels for 13%

profile of v3, /device:TPU:0, one launch (start us, length us, event | category | flops | bytes accessed | tf_op | source)
XLA Modules:
  0.0 241.5 jit_solution(5562142520187980887)
XLA Ops:
  2.9 7.9 %all-to-all-start = ((bf16[8,16,4096]{2,1,0:T(8,128)(2,1)}), bf16[8,16,4096]{2,1,0:T(8,128)(2,1)S(1)}, u32[]{:S(2)}, u32[]{:S(2)}) async-start(bf16[8,16,4096]{2,1,0:T(8,128)(2,1)} %first_norm.1.after_ref), calls=%async_computation | async-start | bytes 2097152 | tf_op jit(solution)/shard_map/all_to_all | solution.py:388
  10.7 3.5 %collective-permute-start = (bf16[16,4096]{1,0:T(8,128)(2,1)}, bf16[16,4096]{1,0:T(8,128)(2,1)S(1)}, u32[]{:S(2)}, u32[]{:S(2)}) collective-permute-start(bf16[16,4096]{1,0:T(8,128)(2,1)} %bitcast.22), channel_id=1, source_target_pairs={{0,4},{1,5},{2,6},{3,7},{4,0},{5,1},{6,2},{7,3},{8,12},{9,13},{10,... | collective-permute-start | bytes 393224 | tf_op jit(solution)/shard_map/ppermute | solution.py:406
  14.3 14.4 %collective-permute-done = bf16[16,4096]{1,0:T(8,128)(2,1)S(1)} collective-permute-done((bf16[16,4096]{1,0:T(8,128)(2,1)}, bf16[16,4096]{1,0:T(8,128)(2,1)S(1)}, u32[]{:S(2)}, u32[]{:S(2)}) %collective-permute-start) | collective-permute-done | bytes 131104 | tf_op jit(solution)/shard_map/ppermute | solution.py:406
  34.2 4.8 %all-to-all-start.1 = ((bf16[8,320,128]{2,1,0:T(8,128)(2,1)}), bf16[8,320,128]{2,1,0:T(8,128)(2,1)S(1)}, u32[]{:S(2)}, u32[]{:S(2)}) async-start(bf16[8,320,128]{2,1,0:T(8,128)(2,1)} %qkv.1), calls=%async_computation.1 | async-start | bytes 1310720 | tf_op jit(solution)/shard_map/all_to_all | solution.py:388
  43.2 7.8 %all-to-all-done.1.refs_0_ = bf16[8,320,128]{2,1,0:T(8,128)(2,1)S(1)} async-done(((bf16[8,320,128]{2,1,0:T(8,128)(2,1)}), bf16[8,320,128]{2,1,0:T(8,128)(2,1)S(1)}, u32[]{:S(2)}, u32[]{:S(2)}) %all-to-all-start.1) | async-done | bytes 655392 | tf_op jit(solution)/shard_map/all_to_all | solution.py:388
  53.2 3.4 %all-to-all-start.2 = ((bf16[8,64,128]{2,1,0:T(8,128)(2,1)}), bf16[8,64,128]{2,1,0:T(8,128)(2,1)S(1)}, u32[]{:S(2)}, u32[]{:S(2)}) async-start(bf16[8,64,128]{2,1,0:T(8,128)(2,1)} %get-tuple-element.56.after_ref.refs_4_.refs_1_), calls=%async_computation.2 | async-start | bytes 262144 | tf_op jit(solution)/shard_map/all_to_all | solution.py:388
  67.8 4.6 %all-to-all-start.3 = ((bf16[8,16,4096]{2,1,0:T(8,128)(2,1)}), bf16[8,16,4096]{2,1,0:T(8,128)(2,1)S(1)}, u32[]{:S(2)}, u32[]{:S(2)}) async-start(bf16[8,16,4096]{2,1,0:T(8,128)(2,1)} %bitcast.5.refs_3_), calls=%async_computation.3 | async-start | bytes 2097152 | tf_op jit(solution)/shard_map/all_to_all | solution.py:388
  74.6 5.7 %grad_act.1.refs_2_.refs_3_ = f32[256,1024]{1,0:T(8,128)S(1)} custom-call(bf16[128,4096]{1,0:T(8,128)(2,1)S(1)} %join_cotangent.1.refs_2_.refs_0_, bf16[128,4096]{1,0:T(8,128)(2,1)S(1)} %copy-done.5, bf16[1024,4096]{1,0:T(8,128)(2,1)} %refs_1_.1, bf16[8,16,4096]{2,1,0:T(8,128)(2,1)} %bitcast.5.refs_3_), custom_call_target="tpu_custom_call" | custom-call | flops 2147483648 | bytes 8388608 | tf_op jit(solution)/shard_map/grad_act/pallas_call | solution.py:38
  80.3 7.9 %all-to-all-done.3.refs_0_ = bf16[8,16,4096]{2,1,0:T(8,128)(2,1)S(1)} async-done(((bf16[8,16,4096]{2,1,0:T(8,128)(2,1)}), bf16[8,16,4096]{2,1,0:T(8,128)(2,1)S(1)}, u32[]{:S(2)}, u32[]{:S(2)}) %all-to-all-start.3) | async-done | bytes 1048608 | tf_op jit(solution)/shard_map/all_to_all | solution.py:388
  88.7 21.7 %all_to_all.50 = bf16[8,16,4096]{2,1,0:T(8,128)(2,1)S(1)} all-to-all(bf16[8,16,4096]{2,1,0:T(8,128)(2,1)S(1)} %get-tuple-element.63.after_ref), channel_id=1, replica_groups=mesh['section'=2,'seq'=8,'mp'=8] {'mp'}, dimensions={0} | all-to-all | bytes 2097152 | tf_op jit(solution)/shard_map/all_to_all | solution.py:388
  110.4 3.4 %fetch_up.1.refs_2_.refs_1_ = bf16[4096,1024]{1,0:T(8,128)(2,1)S(1)} custom-call(bf16[4096,1024]{1,0:T(8,128)(2,1)} %src_ref.6, bf16[8,16,4096]{2,1,0:T(8,128)(2,1)S(1)} %get-tuple-element.63.after_ref), custom_call_target="tpu_custom_call" | custom-call | bytes 8388608 | tf_op jit(solution)/shard_map/fetch_up/pallas_call | solution.py:61
  123.3 3.7 %all-to-all-start.5 = ((bf16[8,16,4096]{2,1,0:T(8,128)(2,1)}), bf16[8,16,4096]{2,1,0:T(8,128)(2,1)S(1)}, u32[]{:S(2)}, u32[]{:S(2)}) async-start(bf16[8,16,4096]{2,1,0:T(8,128)(2,1)} %bitcast.7.refs_2_), calls=%async_computation.5 | async-start | bytes 2097152 | tf_op jit(solution)/shard_map/all_to_all | solution.py:388
  127.0 7.4 %down.1 = (bf16[128,4096]{1,0:T(8,128)(2,1)S(1)}, bf16[128,4096]{1,0:T(8,128)(2,1)S(1)}) custom-call(bf16[256,1024]{1,0:T(8,128)(2,1)S(1)} %get-tuple-element.70.refs_0_, bf16[1024,4096]{1,0:T(8,128)(2,1)} %refs_1_.1, bf16[8,16,4096]{2,1,0:T(8,128)(2,1)} %bitcast.7.refs_2_), custom_call_target="tpu_custom_call" | custom-call | flops 2147483648 | bytes 8388608 | tf_op jit(solution)/shard_map/down/pallas_call | solution.py:38
  135.4 7.5 %all-to-all-done.5.refs_0_ = bf16[8,16,4096]{2,1,0:T(8,128)(2,1)S(1)} async-done(((bf16[8,16,4096]{2,1,0:T(8,128)(2,1)}), bf16[8,16,4096]{2,1,0:T(8,128)(2,1)S(1)}, u32[]{:S(2)}, u32[]{:S(2)}) %all-to-all-start.5) | async-done | bytes 1048608 | tf_op jit(solution)/shard_map/all_to_all | solution.py:388
  144.5 4.8 %all-to-all-start.6 = ((bf16[8,16,4096]{2,1,0:T(8,128)(2,1)}), bf16[8,16,4096]{2,1,0:T(8,128)(2,1)S(1)}, u32[]{:S(2)}, u32[]{:S(2)}) async-start(bf16[8,16,4096]{2,1,0:T(8,128)(2,1)} %get-tuple-element.72.after_ref), calls=%async_computation.6 | async-start | bytes 2097152 | tf_op jit(solution)/shard_map/all_to_all | solution.py:388
  152.2 12.8 %all-to-all-done.6 = bf16[8,16,4096]{2,1,0:T(8,128)(2,1)S(1)} async-done(((bf16[8,16,4096]{2,1,0:T(8,128)(2,1)}), bf16[8,16,4096]{2,1,0:T(8,128)(2,1)S(1)}, u32[]{:S(2)}, u32[]{:S(2)}) %all-to-all-start.6) | async-done | bytes 1048608 | tf_op jit(solution)/shard_map/all_to_all | solution.py:388
  168.5 12.2 %all_to_all.51.refs_3_ = bf16[8,64,128]{2,1,0:T(8,128)(2,1)S(1)} all-to-all(bf16[8,64,128]{2,1,0:T(8,128)(2,1)S(1)} %attn_out_grad.1), channel_id=1, replica_groups=mesh['section'=2,'seq'=8,'mp'=8] {'seq'}, dimensions={0} | all-to-all | bytes 262144 | tf_op jit(solution)/shard_map/all_to_all | solution.py:388
  180.7 4.3 %attention_grad.1 = bf16[8,320,128]{2,1,0:T(8,128)(2,1)} custom-call(bf16[8,320,128]{2,1,0:T(8,128)(2,1)S(1)} %copy-done.1, bf16[8,64,128]{2,1,0:T(8,128)(2,1)} %get-tuple-element.56.after_ref.refs_4_.refs_1_, f32[4,1,128]{2,1,0:T(1,128)S(1)} %get-tuple-element.57.refs_2_, bf16[8,64,128]{2,1,0:T(8,128)(2,1)S(1)} %all_to_all.51.refs_3_), custom_call_target="tpu_custom_call" | custom-call | flops 167772160 | tf_op jit(solution)/shard_map/attention_grad/pallas_call | solution.py:104
  184.9 3.5 %all-to-all-start.8 = ((bf16[8,320,128]{2,1,0:T(8,128)(2,1)}), bf16[8,320,128]{2,1,0:T(8,128)(2,1)S(1)}, u32[]{:S(2)}, u32[]{:S(2)}) async-start(bf16[8,320,128]{2,1,0:T(8,128)(2,1)} %attention_grad.1), calls=%async_computation.8 | async-start | bytes 1310720 | tf_op jit(solution)/shard_map/all_to_all | solution.py:388
  189.7 2.9 %collective-permute-start.14 = (bf16[2,16,4096]{2,1,0:T(8,128)(2,1)}, bf16[2,16,4096]{2,1,0:T(8,128)(2,1)S(1)}, u32[]{:S(2)}, u32[]{:S(2)}) collective-permute-start(bf16[2,16,4096]{2,1,0:T(8,128)(2,1)} %copy-done.15), channel_id=1, source_target_pairs={{0,2},{1,3},{2,0},{3,1},{4,6},{5,7},{6,4},{7,5},{8,10},{9,11},{10,... | collective-permute-start | bytes 786440 | tf_op jit(solution)/shard_map/ppermute | solution.py:412
  193.9 4.4 %collective-permute-done.13.refs_0_.refs_1_ = bf16[2,16,4096]{2,1,0:T(8,128)(2,1)S(1)} collective-permute-done((bf16[2,16,4096]{2,1,0:T(8,128)(2,1)}, bf16[2,16,4096]{2,1,0:T(8,128)(2,1)S(1)}, u32[]{:S(2)}, u32[]{:S(2)}) %collective-permute-start.13) | collective-permute-done | bytes 262176 | tf_op jit(solution)/shard_map/ppermute | solution.py:412
  198.4 5.0 %collective-permute-done.14.refs_1_.refs_2_ = bf16[2,16,4096]{2,1,0:T(8,128)(2,1)S(1)} collective-permute-done((bf16[2,16,4096]{2,1,0:T(8,128)(2,1)}, bf16[2,16,4096]{2,1,0:T(8,128)(2,1)S(1)}, u32[]{:S(2)}, u32[]{:S(2)}) %collective-permute-start.14) | collective-permute-done | bytes 262176 | tf_op jit(solution)/shard_map/ppermute | solution.py:412
  212.5 4.5 %collective-permute-done.18.refs_4_.refs_5_ = bf16[16,4096]{1,0:T(8,128)(2,1)S(1)} collective-permute-done((bf16[16,4096]{1,0:T(8,128)(2,1)S(1)}, bf16[16,4096]{1,0:T(8,128)(2,1)S(1)}, u32[]{:S(2)}, u32[]{:S(2)}) %collective-permute-start.18) | collective-permute-done | bytes 131104 | tf_op jit(solution)/shard_map/ppermute | solution.py:406
  217.2 22.1 %all_to_all.52.refs_0_ = bf16[8,16,4096]{2,1,0:T(8,128)(2,1)S(1)} all-to-all(bf16[8,16,4096]{2,1,0:T(8,128)(2,1)S(1)} %bitcast.16), channel_id=1, replica_groups=mesh['section'=2,'seq'=8,'mp'=8] {'mp'}, dimensions={0} | all-to-all | bytes 2097152 | tf_op jit(solution)/shard_map/all_to_all | solution.py:388
  (93 shorter events, 60.3 us)
Async XLA Ops:
  2.9 25.8 %all-to-all-start = ((bf16[8,16,4096]{2,1,0:T(8,128)(2,1)}), bf16[8,16,4096]{2,1,0:T(8,128)(2,1)S(1)}, u32[]{:S(2)}, u32[]{:S(2)}) async-start(bf16[8,16,4096]{2,1,0:T(8,128)(2,1)} %first_norm.1.after_ref), calls=%async_computation | async-start | bytes 2097152 | tf_op jit(solution)/shard_map/all_to_all | solution.py:388
  10.7 17.9 %collective-permute-start = (bf16[16,4096]{1,0:T(8,128)(2,1)}, bf16[16,4096]{1,0:T(8,128)(2,1)S(1)}, u32[]{:S(2)}, u32[]{:S(2)}) collective-permute-start(bf16[16,4096]{1,0:T(8,128)(2,1)} %bitcast.22), channel_id=1, source_target_pairs={{0,4},{1,5},{2,6},{3,7},{4,0},{5,1},{6,2},{7,3},{8,12},{9,13},{10,... | collective-permute-start | bytes 393224 | tf_op jit(solution)/shard_map/ppermute | solution.py:406
  28.6 2.9 %collective-permute-start.1 = (bf16[128,4096]{1,0:T(8,128)(2,1)S(1)}, bf16[128,4096]{1,0:T(8,128)(2,1)S(1)}, u32[]{:S(2)}, u32[]{:S(2)}) collective-permute-start(bf16[128,4096]{1,0:T(8,128)(2,1)S(1)} %bitcast.14), channel_id=1, source_target_pairs={{0,64},{64,0},{1,65},{65,1},{2,66},{66,2},{3,67},{67,3},{4,68},{68... | collective-permute-start | bytes 3145736 | tf_op jit(solution)/shard_map/ppermute | solution.py:384
  34.2 16.9 %all-to-all-start.1 = ((bf16[8,320,128]{2,1,0:T(8,128)(2,1)}), bf16[8,320,128]{2,1,0:T(8,128)(2,1)S(1)}, u32[]{:S(2)}, u32[]{:S(2)}) async-start(bf16[8,320,128]{2,1,0:T(8,128)(2,1)} %qkv.1), calls=%async_computation.1 | async-start | bytes 1310720 | tf_op jit(solution)/shard_map/all_to_all | solution.py:388
  38.9 19.3 %collective-permute-start.4 = (bf16[2,16,4096]{2,1,0:T(8,128)(2,1)S(1)}, bf16[2,16,4096]{2,1,0:T(8,128)(2,1)S(1)}, u32[]{:S(2)}, u32[]{:S(2)}) collective-permute-start(bf16[2,16,4096]{2,1,0:T(8,128)(2,1)S(1)} %pad_maximum_fusion.refs_0_), channel_id=1, source_target_pairs={{0,3},{1,0},{2,1},{3,2},{4,7},{5,4},{6,5},{7,6},{8,11},{9,8},{10,9... | collective-permute-start | bytes 786440 | tf_op jit(solution)/shard_map/ppermute | solution.py:412
  41.4 17.5 %collective-permute-start.3 = (bf16[2,16,4096]{2,1,0:T(8,128)(2,1)S(1)}, bf16[2,16,4096]{2,1,0:T(8,128)(2,1)S(1)}, u32[]{:S(2)}, u32[]{:S(2)}) collective-permute-start(bf16[2,16,4096]{2,1,0:T(8,128)(2,1)S(1)} %pad_maximum_fusion.refs_0_), channel_id=1, source_target_pairs={{0,2},{1,3},{2,0},{3,1},{4,6},{5,7},{6,4},{7,5},{8,10},{9,11},{10,... | collective-permute-start | bytes 786440 | tf_op jit(solution)/shard_map/ppermute | solution.py:412
  42.2 17.4 %collective-permute-start.2 = (bf16[2,16,4096]{2,1,0:T(8,128)(2,1)S(1)}, bf16[2,16,4096]{2,1,0:T(8,128)(2,1)S(1)}, u32[]{:S(2)}, u32[]{:S(2)}) collective-permute-start(bf16[2,16,4096]{2,1,0:T(8,128)(2,1)S(1)} %pad_maximum_fusion.refs_0_), channel_id=1, source_target_pairs={{0,1},{1,2},{2,3},{3,0},{4,5},{5,6},{6,7},{7,4},{8,9},{9,10},{10,1... | collective-permute-start | bytes 786440 | tf_op jit(solution)/shard_map/ppermute | solution.py:412
  53.2 10.1 %all-to-all-start.2 = ((bf16[8,64,128]{2,1,0:T(8,128)(2,1)}), bf16[8,64,128]{2,1,0:T(8,128)(2,1)S(1)}, u32[]{:S(2)}, u32[]{:S(2)}) async-start(bf16[8,64,128]{2,1,0:T(8,128)(2,1)} %get-tuple-element.56.after_ref.refs_4_.refs_1_), calls=%async_computation.2 | async-start | bytes 262144 | tf_op jit(solution)/shard_map/all_to_all | solution.py:388
  64.3 2.2 collective-permute-start.5
  64.9 7.5 %collective-permute-start.7 = (bf16[128,4096]{1,0:T(8,128)(2,1)S(1)}, bf16[128,4096]{1,0:T(8,128)(2,1)S(1)}, u32[]{:S(2)}, u32[]{:S(2)}) collective-permute-start(bf16[128,4096]{1,0:T(8,128)(2,1)S(1)} %join_cotangent.1.refs_2_.refs_0_), channel_id=1, source_target_pairs={{0,64},{64,0},{1,65},{65,1},{2,66},{66,2},{3,67},{67,3},{4,68},{68... | collective-permute-start | bytes 3145736 | tf_op jit(solution)/shard_map/ppermute | solution.py:384
  67.8 20.4 %all-to-all-start.3 = ((bf16[8,16,4096]{2,1,0:T(8,128)(2,1)}), bf16[8,16,4096]{2,1,0:T(8,128)(2,1)S(1)}, u32[]{:S(2)}, u32[]{:S(2)}) async-start(bf16[8,16,4096]{2,1,0:T(8,128)(2,1)} %bitcast.5.refs_3_), calls=%async_computation.3 | async-start | bytes 2097152 | tf_op jit(solution)/shard_map/all_to_all | solution.py:388
  110.4 3.4 %collective-permute-start.8 = (bf16[128,4096]{1,0:T(8,128)(2,1)S(1)}, bf16[128,4096]{1,0:T(8,128)(2,1)S(1)}, u32[]{:S(2)}, u32[]{:S(2)}) collective-permute-start(bf16[128,4096]{1,0:T(8,128)(2,1)S(1)} %bitcast.17), channel_id=1, source_target_pairs={{0,64},{64,0},{1,65},{65,1},{2,66},{66,2},{3,67},{67,3},{4,68},{68... | collective-permute-start | bytes 3145736 | tf_op jit(solution)/shard_map/ppermute | solution.py:384
  119.7 2.3 collective-permute-start.9
  123.3 19.6 %all-to-all-start.5 = ((bf16[8,16,4096]{2,1,0:T(8,128)(2,1)}), bf16[8,16,4096]{2,1,0:T(8,128)(2,1)S(1)}, u32[]{:S(2)}, u32[]{:S(2)}) async-start(bf16[8,16,4096]{2,1,0:T(8,128)(2,1)} %bitcast.7.refs_2_), calls=%async_computation.5 | async-start | bytes 2097152 | tf_op jit(solution)/shard_map/all_to_all | solution.py:388
  144.4 4.8 %collective-permute-start.11 = (bf16[128,4096]{1,0:T(8,128)(2,1)}, bf16[128,4096]{1,0:T(8,128)(2,1)}, u32[]{:S(2)}, u32[]{:S(2)}) collective-permute-start(bf16[128,4096]{1,0:T(8,128)(2,1)} %copy-done.14), channel_id=1, source_target_pairs={{0,64},{64,0},{1,65},{65,1},{2,66},{66,2},{3,67},{67,3},{4,68},{68... | collective-permute-start | bytes 3145736 | tf_op jit(solution)/shard_map/ppermute | solution.py:384
  144.5 20.6 %all-to-all-start.6 = ((bf16[8,16,4096]{2,1,0:T(8,128)(2,1)}), bf16[8,16,4096]{2,1,0:T(8,128)(2,1)S(1)}, u32[]{:S(2)}, u32[]{:S(2)}) async-start(bf16[8,16,4096]{2,1,0:T(8,128)(2,1)} %get-tuple-element.72.after_ref), calls=%async_computation.6 | async-start | bytes 2097152 | tf_op jit(solution)/shard_map/all_to_all | solution.py:388
  165.1 2.7 %collective-permute-start.12 = (bf16[128,4096]{1,0:T(8,128)(2,1)S(1)}, bf16[128,4096]{1,0:T(8,128)(2,1)S(1)}, u32[]{:S(2)}, u32[]{:S(2)}) collective-permute-start(bf16[128,4096]{1,0:T(8,128)(2,1)S(1)} %bitcast.12), channel_id=1, source_target_pairs={{0,64},{64,0},{1,65},{65,1},{2,66},{66,2},{3,67},{67,3},{4,68},{68... | collective-permute-start | bytes 3145736 | tf_op jit(solution)/shard_map/ppermute | solution.py:384
  184.9 18.6 %all-to-all-start.8 = ((bf16[8,320,128]{2,1,0:T(8,128)(2,1)}), bf16[8,320,128]{2,1,0:T(8,128)(2,1)S(1)}, u32[]{:S(2)}, u32[]{:S(2)}) async-start(bf16[8,320,128]{2,1,0:T(8,128)(2,1)} %attention_grad.1), calls=%async_computation.8 | async-start | bytes 1310720 | tf_op jit(solution)/shard_map/all_to_all | solution.py:388
  188.5 9.9 %collective-permute-start.13 = (bf16[2,16,4096]{2,1,0:T(8,128)(2,1)}, bf16[2,16,4096]{2,1,0:T(8,128)(2,1)S(1)}, u32[]{:S(2)}, u32[]{:S(2)}) collective-permute-start(bf16[2,16,4096]{2,1,0:T(8,128)(2,1)} %copy-done.16), channel_id=1, source_target_pairs={{0,1},{1,2},{2,3},{3,0},{4,5},{5,6},{6,7},{7,4},{8,9},{9,10},{10,1... | collective-permute-start | bytes 786440 | tf_op jit(solution)/shard_map/ppermute | solution.py:412
  189.7 13.7 %collective-permute-start.14 = (bf16[2,16,4096]{2,1,0:T(8,128)(2,1)}, bf16[2,16,4096]{2,1,0:T(8,128)(2,1)S(1)}, u32[]{:S(2)}, u32[]{:S(2)}) collective-permute-start(bf16[2,16,4096]{2,1,0:T(8,128)(2,1)} %copy-done.15), channel_id=1, source_target_pairs={{0,2},{1,3},{2,0},{3,1},{4,6},{5,7},{6,4},{7,5},{8,10},{9,11},{10,... | collective-permute-start | bytes 786440 | tf_op jit(solution)/shard_map/ppermute | solution.py:412
  192.6 10.7 %collective-permute-start.15 = (bf16[2,16,4096]{2,1,0:T(8,128)(2,1)S(1)}, bf16[2,16,4096]{2,1,0:T(8,128)(2,1)S(1)}, u32[]{:S(2)}, u32[]{:S(2)}) collective-permute-start(bf16[2,16,4096]{2,1,0:T(8,128)(2,1)S(1)} %get-tuple-element.89), channel_id=1, source_target_pairs={{0,3},{1,0},{2,1},{3,2},{4,7},{5,4},{6,5},{7,6},{8,11},{9,8},{10,9... | collective-permute-start | bytes 786440 | tf_op jit(solution)/shard_map/ppermute | solution.py:412
  206.3 10.7 %collective-permute-start.17 = (bf16[128,2048]{1,0:T(8,128)(2,1)S(1)}, bf16[128,2048]{1,0:T(8,128)(2,1)S(1)}, u32[]{:S(2)}, u32[]{:S(2)}) collective-permute-start(bf16[128,2048]{1,0:T(8,128)(2,1)S(1)} %get-tuple-element.95), channel_id=1, source_target_pairs={{0,64},{64,0},{1,65},{65,1},{2,66},{66,2},{3,67},{67,3},{4,68},{68... | collective-permute-start | bytes 1572872 | tf_op jit(solution)/shard_map/ppermute | solution.py:384
  209.4 7.6 %collective-permute-start.16 = (bf16[128,2048]{1,0:T(8,128)(2,1)S(1)}, bf16[128,2048]{1,0:T(8,128)(2,1)S(1)}, u32[]{:S(2)}, u32[]{:S(2)}) collective-permute-start(bf16[128,2048]{1,0:T(8,128)(2,1)S(1)} %get-tuple-element.91), channel_id=1, source_target_pairs={{0,64},{64,0},{1,65},{65,1},{2,66},{66,2},{3,67},{67,3},{4,68},{68... | collective-permute-start | bytes 1572872 | tf_op jit(solution)/shard_map/ppermute | solution.py:384
  210.0 7.0 %collective-permute-start.18 = (bf16[16,4096]{1,0:T(8,128)(2,1)S(1)}, bf16[16,4096]{1,0:T(8,128)(2,1)S(1)}, u32[]{:S(2)}, u32[]{:S(2)}) collective-permute-start(bf16[16,4096]{1,0:T(8,128)(2,1)S(1)} %get-tuple-element.96), channel_id=1, source_target_pairs={{0,4},{1,5},{2,6},{3,7},{4,0},{5,1},{6,2},{7,3},{8,12},{9,13},{10,... | collective-permute-start | bytes 393224 | tf_op jit(solution)/shard_map/ppermute | solution.py:406
  (19 other events, 86.5 us)

commit v4 on v3

--- a/solution.py
+++ b/solution.py
@@ -261,16 +261,38 @@
 
 
 def join_low_body(*refs):
-    out_ref = refs[-1]
-    count = len(refs) - 1
+    *block_refs, _, out_ref, sems = refs
+    count = len(block_refs)
     low = lax.rem(lax.axis_index("mp"), count)
     high = lax.axis_index("mp") // count
-    rows = refs[0].shape[1]
+    rows = block_refs[0].shape[1]
+    moves = []
     for step in range(count):
         source = lax.rem(low + count - step, count)
         for side, place in ((0, high), (1, 1 - high)):
             start = pl.multiple_of((place * count + source) * rows, rows)
-            out_ref[pl.ds(start, rows)] = refs[step][side]
+            moves.append(
+                pltpu.make_async_copy(
+                    block_refs[step].at[side], out_ref.at[pl.ds(start, rows)], sems.at[step, side]
+                )
+            )
+    for move in moves:
+        move.start()
+    for move in moves:
+        move.wait()
+
+
+def join_low(blocks, after, shape):
+    any_spec = pl.BlockSpec(memory_space=pl.ANY)
+    return pl.pallas_call(
+        join_low_body,
+        name="join_cotangent",
+        in_specs=[any_spec] * (len(blocks) + 1),
+        out_specs=any_spec,
+        out_shape=jax.ShapeDtypeStruct(shape, BF16),
+        scratch_shapes=[pltpu.SemaphoreType.DMA((len(blocks), 2))],
+        compiler_params=pltpu.CompilerParams(vmem_limit_bytes=1024 * 1024),
+    )(*[hbm(block) for block in blocks], after)
 
 
 def split_low_body(own_ref, other_ref, *out_refs):
@@ -326,11 +348,22 @@
 
 
 def pair_body(*refs):
-    out_ref = refs[-1]
-    size = refs[0].shape[1]
-    for index in range(2):
-        total = refs[2 * index][...].astype(F32) + refs[2 * index + 1][...].astype(F32)
-        out_ref[:, index * size : (index + 1) * size] = total.astype(BF16)
+    *sides, out_ref, total_ref, sems = refs
+    size = sides[0].shape[1]
+    count = sems.shape[0]
+    rows = out_ref.shape[0] // count
+    moves = []
+    for step in range(count):
+        part = pl.ds(step * rows, rows)
+        for index in range(len(sides) // 2):
+            total = sides[2 * index][part].astype(F32) + sides[2 * index + 1][part].astype(F32)
+            total_ref[part, index * size : (index + 1) * size] = total.astype(BF16)
+        moves.append(
+            pltpu.make_async_copy(total_ref.at[part], out_ref.at[part], sems.at[step])
+        )
+        moves[-1].start()
+    for move in moves:
+        move.wait()
 
 
 def down_body(rows_ref, w_ref, own_ref, other_ref):
@@ -388,13 +421,20 @@
     return lax.all_to_all(data, axis, 0, 0)
 
 
-def by_columns(partial, half, width, after=()):
+def by_columns(partial, half, width):
     sides = [partial(start) for start in (0, width // 2)]
     ins = []
     for own, other in sides:
         ins += [own, swap_section(other)]
-    (total,) = local_call(pair_body, "pair", ins, [((half, width), BF16)], after=after)
-    return total
+    return pl.pallas_call(
+        pair_body,
+        name="pair",
+        in_specs=[pl.BlockSpec(memory_space=pltpu.VMEM)] * len(ins),
+        out_specs=pl.BlockSpec(memory_space=pl.ANY),
+        out_shape=jax.ShapeDtypeStruct((half, width), BF16),
+        scratch_shapes=[pltpu.VMEM((half, width), BF16), pltpu.SemaphoreType.DMA((4,))],
+        compiler_params=pltpu.CompilerParams(vmem_limit_bytes=16 * 1024 * 1024),
+    )(*ins)
 
 
 def pair_sum(own, other):
@@ -439,7 +479,6 @@
     weight = fetch(qkv_weight, send, "fetch_qkv")
     mine, cot_far = lax.optimization_barrier((exchange(send, "mp"), cot_far))
     mine = mine.reshape(half, width)
-    cot_two = jnp.stack([cot_near, cot_far])
     (send,) = local_call(
         qkv_body,
         "qkv",
@@ -448,7 +487,8 @@
         [joined],
         flops=2 * total_rows * width * 3 * head_cols,
     )
-    send, cot_two = lax.optimization_barrier((send, cot_two))
+    send, cot_near, cot_far = lax.optimization_barrier((send, cot_near, cot_far))
+    cot_two = jnp.stack([cot_near, cot_far])
     pack = exchange(send, "seq")
     cot_shifted = [shift_low(cot_two, step) for step in range(1, group // 2)]
     att, lse = local_call(
@@ -460,13 +500,7 @@
     )
     weight = fetch(out_weight, att, "fetch_out")
     got = exchange(att, "seq")
-    (cot_mine,) = local_call(
-        join_low_body,
-        "join_cotangent",
-        [cot_two, *cot_shifted],
-        [((half, width), BF16)],
-        after=[att],
-    )
+    cot_mine = join_low([cot_two, *cot_shifted], att, (half, width))
     cots = [cot_mine, swap_section(cot_mine)]
 
     def attn_out(start):
@@ -594,7 +628,7 @@
             cost_estimate=pl.CostEstimate(flops=0, bytes_accessed=0, transcendentals=0),
         )(got, hbm(qkv_weight), *after)
 
-    parts = exchange(by_columns(qkv_grad, half, width, [sum_far]).reshape(group, rows, width), "mp")
+    parts = exchange(by_columns(qkv_grad, half, width).reshape(group, rows, width), "mp")
     grad_input, block_out = local_call(
         input_grad_body,
         "input_grad",

time: 243 us -> 237 us (0.975)
  blocking collectives: 56 us -> 30.9 us
  waiting for transfers between devices: 69.1 us -> 84.2 us
  starting transfers between devices: 50.7 us -> 57.3 us
  local copies, waits for them, and re-layouts: 10.5 us -> 6.2 us
    all_to_all x3 -> x2, blocking collectives: 56 us -> 30.9 us  [exchange(): return lax.all_to_all(data, axis, 0, 0)]
    ppermute x2, waiting for transfers between devices: 18.9 us -> 29.3 us  [shift_high(): lax.ppermute(data, 'mp', [(i, (i + size // 2) % size) for i in range(size)])]
    all_to_all x7 -> x8, starting transfers between devices: 32.6 us -> 38 us  [exchange(): return lax.all_to_all(data, axis, 0, 0)]
    pallas_call x0 -> x4, Pallas kernels: none -> 4.7 us  [the longest x3 3.33 us: by_columns(): pl.pallas_call(pair_body, name='pair', in_specs=[pl.BlockSpec(memory_spac...]
    unnamed x34 -> x24, local copies, waits for them, and re-layouts: 10.5 us -> 6.2 us
    pallas_call x19 -> x15, Pallas kernels: 25.9 us -> 23.1 us  [local_call(): pl.pallas_call(run, name=name, in_specs=[vmem] * count + [pl.BlockSpec(me...]
    all_to_all x7 -> x8, waiting for transfers between devices: 36 us -> 38.9 us  [exchange(): return lax.all_to_all(data, axis, 0, 0)]
  transfers between devices with their start and end apart: 26 -> 27, of which waited for: 13 -> 15; matrix products, arithmetic and copies ran while one was open for 0% -> 0% of each run, Pallas kernels for 13% -> 14%
where the time goes in v4:
time: 237 us; the launch traced here: 236 us
  waiting for transfers between devices  84.2 us (36%)
  starting transfers between devices  57.3 us (24%)
  Pallas kernels  55.9 us (24%)
  blocking collectives  30.9 us (13%)
  local copies, waits for them, and re-layouts  6.2 us (3%)
    all_to_all x8, waiting for transfers between devices, exchange(): return lax.all_to_all(data, axis, 0, 0)  38.9 us
    all_to_all x8, starting transfers between devices, exchange(): return lax.all_to_all(data, axis, 0, 0)  38 us
    all_to_all x2, blocking collectives, exchange(): return lax.all_to_all(data, axis, 0, 0)  30.9 us
    ppermute x2, waiting for transfers between devices, shift_high(): lax.ppermute(data, 'mp', [(i, (i + size // 2) % size) for i in range(size)])  29.3 us
    pallas_call x15, Pallas kernels, local_call(): pl.pallas_call(run, name=name, in_specs=[vmem] * count + [pl.BlockSpec(me...  23.1 us
    pallas_call x2, Pallas kernels, kernel_call(): pl.pallas_call(run, name=name, grid=grid, in_specs=in_specs, out_specs=ou...  13.2 us
    ppermute x6, starting transfers between devices, shift_low(): return lax.ppermute(data, 'mp', pairs)  9.88 us
    ppermute x6, waiting for transfers between devices, shift_low(): return lax.ppermute(data, 'mp', pairs)  9.73 us
  transfers between devices with their start and end apart: 27, of which 15 were waited for; matrix products, arithmetic and copies ran while one was open for 0% of the time, Pallas kernels for 14%

profile of v4, /device:TPU:0, one launch (start us, length us, event | category | flops | bytes accessed | tf_op | source)
XLA Modules:
  0.0 235.6 jit_solution(17304163599268102017)
XLA Ops:
  2.8 7.9 %all-to-all-start = ((bf16[8,16,4096]{2,1,0:T(8,128)(2,1)}), bf16[8,16,4096]{2,1,0:T(8,128)(2,1)S(1)}, u32[]{:S(2)}, u32[]{:S(2)}) async-start(bf16[8,16,4096]{2,1,0:T(8,128)(2,1)} %first_norm.1.after_ref), calls=%async_computation | async-start | bytes 2097152 | tf_op jit(solution)/shard_map/all_to_all | solution.py:421
  10.7 3.5 %collective-permute-start = (bf16[16,4096]{1,0:T(8,128)(2,1)}, bf16[16,4096]{1,0:T(8,128)(2,1)S(1)}, u32[]{:S(2)}, u32[]{:S(2)}) collective-permute-start(bf16[16,4096]{1,0:T(8,128)(2,1)} %bitcast.21), channel_id=1, source_target_pairs={{0,4},{1,5},{2,6},{3,7},{4,0},{5,1},{6,2},{7,3},{8,12},{9,13},{10,... | collective-permute-start | bytes 393224 | tf_op jit(solution)/shard_map/ppermute | solution.py:446
  14.2 14.4 %collective-permute-done = bf16[16,4096]{1,0:T(8,128)(2,1)S(1)} collective-permute-done((bf16[16,4096]{1,0:T(8,128)(2,1)}, bf16[16,4096]{1,0:T(8,128)(2,1)S(1)}, u32[]{:S(2)}, u32[]{:S(2)}) %collective-permute-start) | collective-permute-done | bytes 131104 | tf_op jit(solution)/shard_map/ppermute | solution.py:446
  34.1 4.8 %all-to-all-start.1 = ((bf16[8,320,128]{2,1,0:T(8,128)(2,1)}), bf16[8,320,128]{2,1,0:T(8,128)(2,1)S(1)}, u32[]{:S(2)}, u32[]{:S(2)}) async-start(bf16[8,320,128]{2,1,0:T(8,128)(2,1)} %qkv.1), calls=%async_computation.1 | async-start | bytes 1310720 | tf_op jit(solution)/shard_map/all_to_all | solution.py:421
  43.3 7.8 %all-to-all-done.1.refs_0_ = bf16[8,320,128]{2,1,0:T(8,128)(2,1)S(1)} async-done(((bf16[8,320,128]{2,1,0:T(8,128)(2,1)}), bf16[8,320,128]{2,1,0:T(8,128)(2,1)S(1)}, u32[]{:S(2)}, u32[]{:S(2)}) %all-to-all-start.1) | async-done | bytes 655392 | tf_op jit(solution)/shard_map/all_to_all | solution.py:421
  59.6 3.6 %all-to-all-done.2.refs_0_ = bf16[8,64,128]{2,1,0:T(8,128)(2,1)S(1)} async-done(((bf16[8,64,128]{2,1,0:T(8,128)(2,1)}), bf16[8,64,128]{2,1,0:T(8,128)(2,1)S(1)}, u32[]{:S(2)}, u32[]{:S(2)}) %all-to-all-start.2) | async-done | bytes 131104 | tf_op jit(solution)/shard_map/all_to_all | solution.py:421
  67.5 4.6 %all-to-all-start.3 = ((bf16[8,16,4096]{2,1,0:T(8,128)(2,1)}), bf16[8,16,4096]{2,1,0:T(8,128)(2,1)S(1)}, u32[]{:S(2)}, u32[]{:S(2)}) async-start(bf16[8,16,4096]{2,1,0:T(8,128)(2,1)} %bitcast.5.refs_3_), calls=%async_computation.3 | async-start | bytes 2097152 | tf_op jit(solution)/shard_map/all_to_all | solution.py:421
  74.3 5.7 %grad_act.1.refs_2_.refs_3_ = f32[256,1024]{1,0:T(8,128)S(1)} custom-call(bf16[128,4096]{1,0:T(8,128)(2,1)S(1)} %join_cotangent.1.refs_2_.refs_0_, bf16[128,4096]{1,0:T(8,128)(2,1)S(1)} %copy-done.5, bf16[1024,4096]{1,0:T(8,128)(2,1)} %refs_1_.1, bf16[8,16,4096]{2,1,0:T(8,128)(2,1)} %bitcast.5.refs_3_), custom_call_target="tpu_custom_call" | custom-call | flops 2147483648 | bytes 8388608 | tf_op jit(solution)/shard_map/grad_act/pallas_call | solution.py:38
  80.1 7.9 %all-to-all-done.3.refs_0_ = bf16[8,16,4096]{2,1,0:T(8,128)(2,1)S(1)} async-done(((bf16[8,16,4096]{2,1,0:T(8,128)(2,1)}), bf16[8,16,4096]{2,1,0:T(8,128)(2,1)S(1)}, u32[]{:S(2)}, u32[]{:S(2)}) %all-to-all-start.3) | async-done | bytes 1048608 | tf_op jit(solution)/shard_map/all_to_all | solution.py:421
  88.4 21.7 %all_to_all.50 = bf16[8,16,4096]{2,1,0:T(8,128)(2,1)S(1)} all-to-all(bf16[8,16,4096]{2,1,0:T(8,128)(2,1)S(1)} %get-tuple-element.65.after_ref), channel_id=1, replica_groups=mesh['section'=2,'seq'=8,'mp'=8] {'mp'}, dimensions={0} | all-to-all | bytes 2097152 | tf_op jit(solution)/shard_map/all_to_all | solution.py:421
  110.1 3.4 %fetch_up.1.refs_2_.refs_1_ = bf16[4096,1024]{1,0:T(8,128)(2,1)S(1)} custom-call(bf16[4096,1024]{1,0:T(8,128)(2,1)} %src_ref.6, bf16[8,16,4096]{2,1,0:T(8,128)(2,1)S(1)} %get-tuple-element.65.after_ref), custom_call_target="tpu_custom_call" | custom-call | bytes 8388608 | tf_op jit(solution)/shard_map/fetch_up/pallas_call | solution.py:61
  122.8 3.6 %all-to-all-start.5 = ((bf16[8,16,4096]{2,1,0:T(8,128)(2,1)}), bf16[8,16,4096]{2,1,0:T(8,128)(2,1)S(1)}, u32[]{:S(2)}, u32[]{:S(2)}) async-start(bf16[8,16,4096]{2,1,0:T(8,128)(2,1)} %bitcast.7.refs_2_), calls=%async_computation.5 | async-start | bytes 2097152 | tf_op jit(solution)/shard_map/all_to_all | solution.py:421
  126.4 7.5 %down.1 = (bf16[128,4096]{1,0:T(8,128)(2,1)S(1)}, bf16[128,4096]{1,0:T(8,128)(2,1)S(1)}) custom-call(bf16[256,1024]{1,0:T(8,128)(2,1)S(1)} %get-tuple-element.72.refs_0_, bf16[1024,4096]{1,0:T(8,128)(2,1)} %refs_1_.1, bf16[8,16,4096]{2,1,0:T(8,128)(2,1)} %bitcast.7.refs_2_), custom_call_target="tpu_custom_call" | custom-call | flops 2147483648 | bytes 8388608 | tf_op jit(solution)/shard_map/down/pallas_call | solution.py:38
  134.9 7.5 %all-to-all-done.5.refs_0_ = bf16[8,16,4096]{2,1,0:T(8,128)(2,1)S(1)} async-done(((bf16[8,16,4096]{2,1,0:T(8,128)(2,1)}), bf16[8,16,4096]{2,1,0:T(8,128)(2,1)S(1)}, u32[]{:S(2)}, u32[]{:S(2)}) %all-to-all-start.5) | async-done | bytes 1048608 | tf_op jit(solution)/shard_map/all_to_all | solution.py:421
  143.9 4.8 %all-to-all-start.6 = ((bf16[8,16,4096]{2,1,0:T(8,128)(2,1)}), bf16[8,16,4096]{2,1,0:T(8,128)(2,1)S(1)}, u32[]{:S(2)}, u32[]{:S(2)}) async-start(bf16[8,16,4096]{2,1,0:T(8,128)(2,1)} %get-tuple-element.74.after_ref), calls=%async_computation.6 | async-start | bytes 2097152 | tf_op jit(solution)/shard_map/all_to_all | solution.py:421
  152.4 12.1 %all-to-all-done.6 = bf16[8,16,4096]{2,1,0:T(8,128)(2,1)S(1)} async-done(((bf16[8,16,4096]{2,1,0:T(8,128)(2,1)}), bf16[8,16,4096]{2,1,0:T(8,128)(2,1)S(1)}, u32[]{:S(2)}, u32[]{:S(2)}) %all-to-all-start.6) | async-done | bytes 1048608 | tf_op jit(solution)/shard_map/all_to_all | solution.py:421
  167.9 9.2 %all_to_all.51.refs_3_ = bf16[8,64,128]{2,1,0:T(8,128)(2,1)S(1)} all-to-all(bf16[8,64,128]{2,1,0:T(8,128)(2,1)S(1)} %attn_out_grad.1), channel_id=1, replica_groups=mesh['section'=2,'seq'=8,'mp'=8] {'seq'}, dimensions={0} | all-to-all | bytes 262144 | tf_op jit(solution)/shard_map/all_to_all | solution.py:421
  177.1 4.2 %attention_grad.1 = bf16[8,320,128]{2,1,0:T(8,128)(2,1)} custom-call(bf16[8,320,128]{2,1,0:T(8,128)(2,1)S(1)} %copy-done.1, bf16[8,64,128]{2,1,0:T(8,128)(2,1)} %get-tuple-element.57.after_ref.refs_4_.refs_1_, f32[4,1,128]{2,1,0:T(1,128)S(1)} %get-tuple-element.58.refs_2_, bf16[8,64,128]{2,1,0:T(8,128)(2,1)S(1)} %all_to_all.51.refs_3_), custom_call_target="tpu_custom_call" | custom-call | flops 167772160 | tf_op jit(solution)/shard_map/attention_grad/pallas_call | solution.py:104
  181.4 3.5 %all-to-all-start.8 = ((bf16[8,320,128]{2,1,0:T(8,128)(2,1)}), bf16[8,320,128]{2,1,0:T(8,128)(2,1)S(1)}, u32[]{:S(2)}, u32[]{:S(2)}) async-start(bf16[8,320,128]{2,1,0:T(8,128)(2,1)} %attention_grad.1), calls=%async_computation.8 | async-start | bytes 1310720 | tf_op jit(solution)/shard_map/all_to_all | solution.py:421
  190.4 4.4 %collective-permute-done.13.refs_0_.refs_1_ = bf16[2,16,4096]{2,1,0:T(8,128)(2,1)S(1)} collective-permute-done((bf16[2,16,4096]{2,1,0:T(8,128)(2,1)}, bf16[2,16,4096]{2,1,0:T(8,128)(2,1)S(1)}, u32[]{:S(2)}, u32[]{:S(2)}) %collective-permute-start.13) | collective-permute-done | bytes 262176 | tf_op jit(solution)/shard_map/ppermute | solution.py:452
  194.8 5.3 %collective-permute-done.14.refs_1_.refs_2_ = bf16[2,16,4096]{2,1,0:T(8,128)(2,1)S(1)} collective-permute-done((bf16[2,16,4096]{2,1,0:T(8,128)(2,1)}, bf16[2,16,4096]{2,1,0:T(8,128)(2,1)S(1)}, u32[]{:S(2)}, u32[]{:S(2)}) %collective-permute-start.14) | collective-permute-done | bytes 262176 | tf_op jit(solution)/shard_map/ppermute | solution.py:452
  209.4 5.5 %all-to-all-start.9 = ((bf16[8,16,4096]{2,1,0:T(8,128)(2,1)}), bf16[8,16,4096]{2,1,0:T(8,128)(2,1)S(1)}, u32[]{:S(2)}, u32[]{:S(2)}) async-start(bf16[8,16,4096]{2,1,0:T(8,128)(2,1)} %bitcast.9), calls=%async_computation.9 | async-start | bytes 2097152 | tf_op jit(solution)/shard_map/all_to_all | solution.py:421
  215.0 3.5 %collective-permute-start.18 = (bf16[16,4096]{1,0:T(8,128)(2,1)S(1)}, bf16[16,4096]{1,0:T(8,128)(2,1)S(1)}, u32[]{:S(2)}, u32[]{:S(2)}) collective-permute-start(bf16[16,4096]{1,0:T(8,128)(2,1)S(1)} %get-tuple-element.99), channel_id=1, source_target_pairs={{0,4},{1,5},{2,6},{3,7},{4,0},{5,1},{6,2},{7,3},{8,12},{9,13},{10,... | collective-permute-start | bytes 393224 | tf_op jit(solution)/shard_map/ppermute | solution.py:446
  218.5 14.9 %collective-permute-done.18.refs_5_ = bf16[16,4096]{1,0:T(8,128)(2,1)S(1)} collective-permute-done((bf16[16,4096]{1,0:T(8,128)(2,1)S(1)}, bf16[16,4096]{1,0:T(8,128)(2,1)S(1)}, u32[]{:S(2)}, u32[]{:S(2)}) %collective-permute-start.18) | collective-permute-done | bytes 131104 | tf_op jit(solution)/shard_map/ppermute | solution.py:446
  (84 shorter events, 63.2 us)
Async XLA Ops:
  2.8 25.8 %all-to-all-start = ((bf16[8,16,4096]{2,1,0:T(8,128)(2,1)}), bf16[8,16,4096]{2,1,0:T(8,128)(2,1)S(1)}, u32[]{:S(2)}, u32[]{:S(2)}) async-start(bf16[8,16,4096]{2,1,0:T(8,128)(2,1)} %first_norm.1.after_ref), calls=%async_computation | async-start | bytes 2097152 | tf_op jit(solution)/shard_map/all_to_all | solution.py:421
  10.7 17.9 %collective-permute-start = (bf16[16,4096]{1,0:T(8,128)(2,1)}, bf16[16,4096]{1,0:T(8,128)(2,1)S(1)}, u32[]{:S(2)}, u32[]{:S(2)}) collective-permute-start(bf16[16,4096]{1,0:T(8,128)(2,1)} %bitcast.21), channel_id=1, source_target_pairs={{0,4},{1,5},{2,6},{3,7},{4,0},{5,1},{6,2},{7,3},{8,12},{9,13},{10,... | collective-permute-start | bytes 393224 | tf_op jit(solution)/shard_map/ppermute | solution.py:446
  28.6 2.8 %collective-permute-start.1 = (bf16[128,4096]{1,0:T(8,128)(2,1)S(1)}, bf16[128,4096]{1,0:T(8,128)(2,1)S(1)}, u32[]{:S(2)}, u32[]{:S(2)}) collective-permute-start(bf16[128,4096]{1,0:T(8,128)(2,1)S(1)} %bitcast.14), channel_id=1, source_target_pairs={{0,64},{64,0},{1,65},{65,1},{2,66},{66,2},{3,67},{67,3},{4,68},{68... | collective-permute-start | bytes 3145736 | tf_op jit(solution)/shard_map/ppermute | solution.py:417
  34.1 17.0 %all-to-all-start.1 = ((bf16[8,320,128]{2,1,0:T(8,128)(2,1)}), bf16[8,320,128]{2,1,0:T(8,128)(2,1)S(1)}, u32[]{:S(2)}, u32[]{:S(2)}) async-start(bf16[8,320,128]{2,1,0:T(8,128)(2,1)} %qkv.1), calls=%async_computation.1 | async-start | bytes 1310720 | tf_op jit(solution)/shard_map/all_to_all | solution.py:421
  38.9 19.3 %collective-permute-start.4 = (bf16[2,16,4096]{2,1,0:T(8,128)(2,1)S(1)}, bf16[2,16,4096]{2,1,0:T(8,128)(2,1)}, u32[]{:S(2)}, u32[]{:S(2)}) collective-permute-start(bf16[2,16,4096]{2,1,0:T(8,128)(2,1)S(1)} %pad_maximum_fusion.refs_0_), channel_id=1, source_target_pairs={{0,3},{1,0},{2,1},{3,2},{4,7},{5,4},{6,5},{7,6},{8,11},{9,8},{10,9... | collective-permute-start | bytes 786440 | tf_op jit(solution)/shard_map/ppermute | solution.py:452
  41.4 16.8 %collective-permute-start.3 = (bf16[2,16,4096]{2,1,0:T(8,128)(2,1)S(1)}, bf16[2,16,4096]{2,1,0:T(8,128)(2,1)}, u32[]{:S(2)}, u32[]{:S(2)}) collective-permute-start(bf16[2,16,4096]{2,1,0:T(8,128)(2,1)S(1)} %pad_maximum_fusion.refs_0_), channel_id=1, source_target_pairs={{0,2},{1,3},{2,0},{3,1},{4,6},{5,7},{6,4},{7,5},{8,10},{9,11},{10,... | collective-permute-start | bytes 786440 | tf_op jit(solution)/shard_map/ppermute | solution.py:452
  42.3 15.9 %collective-permute-start.2 = (bf16[2,16,4096]{2,1,0:T(8,128)(2,1)S(1)}, bf16[2,16,4096]{2,1,0:T(8,128)(2,1)}, u32[]{:S(2)}, u32[]{:S(2)}) collective-permute-start(bf16[2,16,4096]{2,1,0:T(8,128)(2,1)S(1)} %pad_maximum_fusion.refs_0_), channel_id=1, source_target_pairs={{0,1},{1,2},{2,3},{3,0},{4,5},{5,6},{6,7},{7,4},{8,9},{9,10},{10,1... | collective-permute-start | bytes 786440 | tf_op jit(solution)/shard_map/ppermute | solution.py:452
  53.2 10.0 %all-to-all-start.2 = ((bf16[8,64,128]{2,1,0:T(8,128)(2,1)}), bf16[8,64,128]{2,1,0:T(8,128)(2,1)S(1)}, u32[]{:S(2)}, u32[]{:S(2)}) async-start(bf16[8,64,128]{2,1,0:T(8,128)(2,1)} %get-tuple-element.57.after_ref.refs_4_.refs_1_), calls=%async_computation.2 | async-start | bytes 262144 | tf_op jit(solution)/shard_map/all_to_all | solution.py:421
  64.2 2.2 collective-permute-start.5
  64.8 7.3 %collective-permute-start.7 = (bf16[128,4096]{1,0:T(8,128)(2,1)S(1)}, bf16[128,4096]{1,0:T(8,128)(2,1)S(1)}, u32[]{:S(2)}, u32[]{:S(2)}) collective-permute-start(bf16[128,4096]{1,0:T(8,128)(2,1)S(1)} %join_cotangent.1.refs_2_.refs_0_), channel_id=1, source_target_pairs={{0,64},{64,0},{1,65},{65,1},{2,66},{66,2},{3,67},{67,3},{4,68},{68... | collective-permute-start | bytes 3145736 | tf_op jit(solution)/shard_map/ppermute | solution.py:417
  67.5 20.4 %all-to-all-start.3 = ((bf16[8,16,4096]{2,1,0:T(8,128)(2,1)}), bf16[8,16,4096]{2,1,0:T(8,128)(2,1)S(1)}, u32[]{:S(2)}, u32[]{:S(2)}) async-start(bf16[8,16,4096]{2,1,0:T(8,128)(2,1)} %bitcast.5.refs_3_), calls=%async_computation.3 | async-start | bytes 2097152 | tf_op jit(solution)/shard_map/all_to_all | solution.py:421
  110.1 3.4 %collective-permute-start.8 = (bf16[128,4096]{1,0:T(8,128)(2,1)S(1)}, bf16[128,4096]{1,0:T(8,128)(2,1)S(1)}, u32[]{:S(2)}, u32[]{:S(2)}) collective-permute-start(bf16[128,4096]{1,0:T(8,128)(2,1)S(1)} %bitcast.16), channel_id=1, source_target_pairs={{0,64},{64,0},{1,65},{65,1},{2,66},{66,2},{3,67},{67,3},{4,68},{68... | collective-permute-start | bytes 3145736 | tf_op jit(solution)/shard_map/ppermute | solution.py:417
  119.4 2.3 collective-permute-start.9
  122.8 19.5 %all-to-all-start.5 = ((bf16[8,16,4096]{2,1,0:T(8,128)(2,1)}), bf16[8,16,4096]{2,1,0:T(8,128)(2,1)S(1)}, u32[]{:S(2)}, u32[]{:S(2)}) async-start(bf16[8,16,4096]{2,1,0:T(8,128)(2,1)} %bitcast.7.refs_2_), calls=%async_computation.5 | async-start | bytes 2097152 | tf_op jit(solution)/shard_map/all_to_all | solution.py:421
  143.9 4.8 %collective-permute-start.11 = (bf16[128,4096]{1,0:T(8,128)(2,1)}, bf16[128,4096]{1,0:T(8,128)(2,1)}, u32[]{:S(2)}, u32[]{:S(2)}) collective-permute-start(bf16[128,4096]{1,0:T(8,128)(2,1)} %copy-done.7), channel_id=1, source_target_pairs={{0,64},{64,0},{1,65},{65,1},{2,66},{66,2},{3,67},{67,3},{4,68},{68... | collective-permute-start | bytes 3145736 | tf_op jit(solution)/shard_map/ppermute | solution.py:417
  143.9 20.6 %all-to-all-start.6 = ((bf16[8,16,4096]{2,1,0:T(8,128)(2,1)}), bf16[8,16,4096]{2,1,0:T(8,128)(2,1)S(1)}, u32[]{:S(2)}, u32[]{:S(2)}) async-start(bf16[8,16,4096]{2,1,0:T(8,128)(2,1)} %get-tuple-element.74.after_ref), calls=%async_computation.6 | async-start | bytes 2097152 | tf_op jit(solution)/shard_map/all_to_all | solution.py:421
  164.5 2.7 %collective-permute-start.12 = (bf16[128,4096]{1,0:T(8,128)(2,1)S(1)}, bf16[128,4096]{1,0:T(8,128)(2,1)S(1)}, u32[]{:S(2)}, u32[]{:S(2)}) collective-permute-start(bf16[128,4096]{1,0:T(8,128)(2,1)S(1)} %bitcast.12), channel_id=1, source_target_pairs={{0,64},{64,0},{1,65},{65,1},{2,66},{66,2},{3,67},{67,3},{4,68},{68... | collective-permute-start | bytes 3145736 | tf_op jit(solution)/shard_map/ppermute | solution.py:417
  181.4 18.9 %all-to-all-start.8 = ((bf16[8,320,128]{2,1,0:T(8,128)(2,1)}), bf16[8,320,128]{2,1,0:T(8,128)(2,1)S(1)}, u32[]{:S(2)}, u32[]{:S(2)}) async-start(bf16[8,320,128]{2,1,0:T(8,128)(2,1)} %attention_grad.1), calls=%async_computation.8 | async-start | bytes 1310720 | tf_op jit(solution)/shard_map/all_to_all | solution.py:421
  184.9 9.9 %collective-permute-start.13 = (bf16[2,16,4096]{2,1,0:T(8,128)(2,1)}, bf16[2,16,4096]{2,1,0:T(8,128)(2,1)S(1)}, u32[]{:S(2)}, u32[]{:S(2)}) collective-permute-start(bf16[2,16,4096]{2,1,0:T(8,128)(2,1)} %copy-done.10), channel_id=1, source_target_pairs={{0,1},{1,2},{2,3},{3,0},{4,5},{5,6},{6,7},{7,4},{8,9},{9,10},{10,1... | collective-permute-start | bytes 786440 | tf_op jit(solution)/shard_map/ppermute | solution.py:452
  186.3 13.9 %collective-permute-start.14 = (bf16[2,16,4096]{2,1,0:T(8,128)(2,1)}, bf16[2,16,4096]{2,1,0:T(8,128)(2,1)S(1)}, u32[]{:S(2)}, u32[]{:S(2)}) collective-permute-start(bf16[2,16,4096]{2,1,0:T(8,128)(2,1)} %copy-done.9), channel_id=1, source_target_pairs={{0,2},{1,3},{2,0},{3,1},{4,6},{5,7},{6,4},{7,5},{8,10},{9,11},{10,... | collective-permute-start | bytes 786440 | tf_op jit(solution)/shard_map/ppermute | solution.py:452
  189.1 11.1 %collective-permute-start.15 = (bf16[2,16,4096]{2,1,0:T(8,128)(2,1)}, bf16[2,16,4096]{2,1,0:T(8,128)(2,1)S(1)}, u32[]{:S(2)}, u32[]{:S(2)}) collective-permute-start(bf16[2,16,4096]{2,1,0:T(8,128)(2,1)} %copy-done.8), channel_id=1, source_target_pairs={{0,3},{1,0},{2,1},{3,2},{4,7},{5,4},{6,5},{7,6},{8,11},{9,8},{10,9... | collective-permute-start | bytes 786440 | tf_op jit(solution)/shard_map/ppermute | solution.py:452
  203.1 3.7 %collective-permute-start.17 = (bf16[128,2048]{1,0:T(8,128)(2,1)S(1)}, bf16[128,2048]{1,0:T(8,128)(2,1)S(1)}, u32[]{:S(2)}, u32[]{:S(2)}) collective-permute-start(bf16[128,2048]{1,0:T(8,128)(2,1)S(1)} %get-tuple-element.97), channel_id=1, source_target_pairs={{0,64},{64,0},{1,65},{65,1},{2,66},{66,2},{3,67},{67,3},{4,68},{68... | collective-permute-start | bytes 1572872 | tf_op jit(solution)/shard_map/ppermute | solution.py:417
  209.4 24.0 %all-to-all-start.9 = ((bf16[8,16,4096]{2,1,0:T(8,128)(2,1)}), bf16[8,16,4096]{2,1,0:T(8,128)(2,1)S(1)}, u32[]{:S(2)}, u32[]{:S(2)}) async-start(bf16[8,16,4096]{2,1,0:T(8,128)(2,1)} %bitcast.9), calls=%async_computation.9 | async-start | bytes 2097152 | tf_op jit(solution)/shard_map/all_to_all | solution.py:421
  215.0 18.5 %collective-permute-start.18 = (bf16[16,4096]{1,0:T(8,128)(2,1)S(1)}, bf16[16,4096]{1,0:T(8,128)(2,1)S(1)}, u32[]{:S(2)}, u32[]{:S(2)}) collective-permute-start(bf16[16,4096]{1,0:T(8,128)(2,1)S(1)} %get-tuple-element.99), channel_id=1, source_target_pairs={{0,4},{1,5},{2,6},{3,7},{4,0},{5,1},{6,2},{7,3},{8,12},{9,13},{10,... | collective-permute-start | bytes 393224 | tf_op jit(solution)/shard_map/ppermute | solution.py:446
  (15 other events, 85.6 us)

commit v5 on v4

--- a/solution.py
+++ b/solution.py
@@ -105,8 +105,10 @@
         run,
         name=name,
         in_specs=[vmem] * count + [pl.BlockSpec(memory_space=pl.ANY)] * (extra + len(after)),
-        out_specs=[vmem] * len(outs),
-        out_shape=[jax.ShapeDtypeStruct(shape, dtype) for shape, dtype in outs],
+        out_specs=[
+            vmem if len(out) == 2 else pl.BlockSpec(memory_space=pl.ANY) for out in outs
+        ],
+        out_shape=[jax.ShapeDtypeStruct(*out[:2]) for out in outs],
         scratch_shapes=scratch,
         input_output_aliases=aliases or {},
         compiler_params=pltpu.CompilerParams(vmem_limit_bytes=16 * 1024 * 1024),
@@ -186,22 +188,25 @@
     rows_ref[half:] = other_ref[...]
 
 
-def qkv_body(
-    mine_ref, other_ref, w_ref, pack_ref, rows_ref
-):
+def qkv_body(mine_ref, other_ref, w_ref, send_ref, rows_ref, pack_ref, sems):
     join_halves(mine_ref, other_ref, rows_ref)
     half_rows = pack_ref.shape[1] // 5
+    moves = []
     for part in range(3):
         acc = dot(rows_ref[...], w_ref[part]).astype(BF16)
+        start = half_rows * max(2 * part - 1, 0)
+        size = half_rows * min(part + 1, 2)
         for slot in range(8):
             image_row, row, col = pack_place(slot, half_rows)
-            if part == 0:
-                pack_ref[slot, :half_rows] = acc[row : row + half_rows, col : col + HD]
-            else:
-                start = half_rows * (2 * part - 1)
-                pack_ref[slot, start : start + 2 * half_rows] = acc[
-                    image_row : image_row + 2 * half_rows, col : col + HD
-                ]
+            first = row if part == 0 else image_row
+            pack_ref[slot, start : start + size] = acc[first : first + size, col : col + HD]
+        place = pl.ds(start, size)
+        moves.append(
+            pltpu.make_async_copy(pack_ref.at[:, place], send_ref.at[:, place], sems.at[part])
+        )
+        moves[-1].start()
+    for move in moves:
+        move.wait()
 
 
 def attention_body(pack_ref, att_ref, lse_ref):
@@ -220,7 +225,7 @@
         att_ref[2 * chunk : 2 * chunk + 2] = mixed.T.astype(BF16).reshape(2, half_rows, HD)
 
 
-def attention_grad_body(pack_ref, att_ref, lse_ref, grad_ref, out_ref):
+def attention_grad_body(pack_ref, att_ref, lse_ref, grad_ref, send_ref, out_ref, sems):
     half_rows = att_ref.shape[1]
     scale = 1.0 / math.sqrt(HD)
     queries = pack_ref[:, :half_rows, :].reshape(-1, HD)
@@ -229,6 +234,7 @@
     delta = jnp.sum(mix.T, axis=0, keepdims=True)
     lse = jnp.concatenate([lse_ref[chunk] for chunk in range(4)], axis=1)
     query_total = None
+    moves = []
     for slot in range(8):
         keys = pack_ref[slot, half_rows : 3 * half_rows, :]
         values = pack_ref[slot, 3 * half_rows :, :]
@@ -239,7 +245,19 @@
         out_ref[slot, 3 * half_rows :] = dot(probs.astype(BF16), grads).astype(BF16)
         term = dot(keys, grad_scores, TN)
         query_total = term if query_total is None else query_total + term
+        part = pl.ds(half_rows, 4 * half_rows)
+        moves.append(
+            pltpu.make_async_copy(
+                out_ref.at[slot, part], send_ref.at[slot, part], sems.at[slot]
+            )
+        )
+        moves[-1].start()
     out_ref[:, :half_rows] = query_total.T.astype(BF16).reshape(8, half_rows, HD)
+    part = pl.ds(0, half_rows)
+    moves.append(pltpu.make_async_copy(out_ref.at[:, part], send_ref.at[:, part], sems.at[8]))
+    moves[-1].start()
+    for move in moves:
+        move.wait()
 
 
 def put_halves(own_ref, other_ref, cols, total):
@@ -483,8 +501,8 @@
         qkv_body,
         "qkv",
         [mine, swap_section(mine), weight],
-        [pack_shape],
-        [joined],
+        [pack_shape + ("hbm",)],
+        [joined, pltpu.VMEM(*pack_shape), pltpu.SemaphoreType.DMA((3,))],
         flops=2 * total_rows * width * 3 * head_cols,
     )
     send, cot_near, cot_far = lax.optimization_barrier((send, cot_near, cot_far))
@@ -598,7 +616,8 @@
         attention_grad_body,
         "attention_grad",
         [pack, att, lse, grad_att],
-        [pack_shape],
+        [pack_shape + ("hbm",)],
+        [pltpu.VMEM(*pack_shape), pltpu.SemaphoreType.DMA((9,))],
         flops=10 * half * half * 8 * HD,
     )
     send, *sums_low = lax.optimization_barrier((send, *sums_low))

time: 237 us -> 237 us (level)
  no operation moved by 1% of the time
where the time goes in v5:
time: 237 us; the launch traced here: 236 us
  waiting for transfers between devices  84.2 us (36%)
  starting transfers between devices  57.3 us (24%)
  Pallas kernels  55.8 us (24%)
  blocking collectives  30.9 us (13%)
  local copies, waits for them, and re-layouts  6.2 us (3%)
    all_to_all x8, waiting for transfers between devices, exchange(): return lax.all_to_all(data, axis, 0, 0)  38.9 us
    all_to_all x8, starting transfers between devices, exchange(): return lax.all_to_all(data, axis, 0, 0)  38.1 us
    all_to_all x2, blocking collectives, exchange(): return lax.all_to_all(data, axis, 0, 0)  30.9 us
    ppermute x2, waiting for transfers between devices, shift_high(): lax.ppermute(data, 'mp', [(i, (i + size // 2) % size) for i in range(size)])  29.3 us
    pallas_call x15, Pallas kernels, local_call(): pl.pallas_call(run, name=name, in_specs=[vmem] * count + [pl.BlockSpec(me...  23 us
    pallas_call x2, Pallas kernels, kernel_call(): pl.pallas_call(run, name=name, grid=grid, in_specs=in_specs, out_specs=ou...  13.2 us
    ppermute x6, starting transfers between devices, shift_low(): return lax.ppermute(data, 'mp', pairs)  9.87 us
    ppermute x6, waiting for transfers between devices, shift_low(): return lax.ppermute(data, 'mp', pairs)  9.73 us
  transfers between devices with their start and end apart: 27, of which 15 were waited for; matrix products, arithmetic and copies ran while one was open for 0% of the time, Pallas kernels for 14%

profile of v5, /device:TPU:0, one launch (start us, length us, event | category | flops | bytes accessed | tf_op | source)
XLA Modules:
  0.0 235.6 jit_solution(10567009444871028272)
XLA Ops:
  2.8 7.9 %all-to-all-start = ((bf16[8,16,4096]{2,1,0:T(8,128)(2,1)}), bf16[8,16,4096]{2,1,0:T(8,128)(2,1)S(1)}, u32[]{:S(2)}, u32[]{:S(2)}) async-start(bf16[8,16,4096]{2,1,0:T(8,128)(2,1)} %first_norm.1.after_ref), calls=%async_computation | async-start | bytes 2097152 | tf_op jit(solution)/shard_map/all_to_all | solution.py:439
  10.7 3.5 %collective-permute-start = (bf16[16,4096]{1,0:T(8,128)(2,1)}, bf16[16,4096]{1,0:T(8,128)(2,1)S(1)}, u32[]{:S(2)}, u32[]{:S(2)}) collective-permute-start(bf16[16,4096]{1,0:T(8,128)(2,1)} %bitcast.21), channel_id=1, source_target_pairs={{0,4},{1,5},{2,6},{3,7},{4,0},{5,1},{6,2},{7,3},{8,12},{9,13},{10,... | collective-permute-start | bytes 393224 | tf_op jit(solution)/shard_map/ppermute | solution.py:464
  14.2 14.4 %collective-permute-done = bf16[16,4096]{1,0:T(8,128)(2,1)S(1)} collective-permute-done((bf16[16,4096]{1,0:T(8,128)(2,1)}, bf16[16,4096]{1,0:T(8,128)(2,1)S(1)}, u32[]{:S(2)}, u32[]{:S(2)}) %collective-permute-start) | collective-permute-done | bytes 131104 | tf_op jit(solution)/shard_map/ppermute | solution.py:464
  34.1 4.8 %all-to-all-start.1 = ((bf16[8,320,128]{2,1,0:T(8,128)(2,1)}), bf16[8,320,128]{2,1,0:T(8,128)(2,1)S(1)}, u32[]{:S(2)}, u32[]{:S(2)}) async-start(bf16[8,320,128]{2,1,0:T(8,128)(2,1)} %qkv.1), calls=%async_computation.1 | async-start | bytes 1310720 | tf_op jit(solution)/shard_map/all_to_all | solution.py:439
  43.3 7.8 %all-to-all-done.1.refs_0_ = bf16[8,320,128]{2,1,0:T(8,128)(2,1)S(1)} async-done(((bf16[8,320,128]{2,1,0:T(8,128)(2,1)}), bf16[8,320,128]{2,1,0:T(8,128)(2,1)S(1)}, u32[]{:S(2)}, u32[]{:S(2)}) %all-to-all-start.1) | async-done | bytes 655392 | tf_op jit(solution)/shard_map/all_to_all | solution.py:439
  59.6 3.6 %all-to-all-done.2.refs_0_ = bf16[8,64,128]{2,1,0:T(8,128)(2,1)S(1)} async-done(((bf16[8,64,128]{2,1,0:T(8,128)(2,1)}), bf16[8,64,128]{2,1,0:T(8,128)(2,1)S(1)}, u32[]{:S(2)}, u32[]{:S(2)}) %all-to-all-start.2) | async-done | bytes 131104 | tf_op jit(solution)/shard_map/all_to_all | solution.py:439
  67.5 4.6 %all-to-all-start.3 = ((bf16[8,16,4096]{2,1,0:T(8,128)(2,1)}), bf16[8,16,4096]{2,1,0:T(8,128)(2,1)S(1)}, u32[]{:S(2)}, u32[]{:S(2)}) async-start(bf16[8,16,4096]{2,1,0:T(8,128)(2,1)} %bitcast.5.refs_3_), calls=%async_computation.3 | async-start | bytes 2097152 | tf_op jit(solution)/shard_map/all_to_all | solution.py:439
  74.3 5.7 %grad_act.1.refs_2_.refs_3_ = f32[256,1024]{1,0:T(8,128)S(1)} custom-call(bf16[128,4096]{1,0:T(8,128)(2,1)S(1)} %join_cotangent.1.refs_2_.refs_0_, bf16[128,4096]{1,0:T(8,128)(2,1)S(1)} %copy-done.5, bf16[1024,4096]{1,0:T(8,128)(2,1)} %refs_1_.1, bf16[8,16,4096]{2,1,0:T(8,128)(2,1)} %bitcast.5.refs_3_), custom_call_target="tpu_custom_call" | custom-call | flops 2147483648 | bytes 8388608 | tf_op jit(solution)/shard_map/grad_act/pallas_call | solution.py:38
  80.1 7.9 %all-to-all-done.3.refs_0_ = bf16[8,16,4096]{2,1,0:T(8,128)(2,1)S(1)} async-done(((bf16[8,16,4096]{2,1,0:T(8,128)(2,1)}), bf16[8,16,4096]{2,1,0:T(8,128)(2,1)S(1)}, u32[]{:S(2)}, u32[]{:S(2)}) %all-to-all-start.3) | async-done | bytes 1048608 | tf_op jit(solution)/shard_map/all_to_all | solution.py:439
  88.4 21.7 %all_to_all.50 = bf16[8,16,4096]{2,1,0:T(8,128)(2,1)S(1)} all-to-all(bf16[8,16,4096]{2,1,0:T(8,128)(2,1)S(1)} %get-tuple-element.65.after_ref), channel_id=1, replica_groups=mesh['section'=2,'seq'=8,'mp'=8] {'mp'}, dimensions={0} | all-to-all | bytes 2097152 | tf_op jit(solution)/shard_map/all_to_all | solution.py:439
  110.1 3.4 %fetch_up.1.refs_2_.refs_1_ = bf16[4096,1024]{1,0:T(8,128)(2,1)S(1)} custom-call(bf16[4096,1024]{1,0:T(8,128)(2,1)} %src_ref.6, bf16[8,16,4096]{2,1,0:T(8,128)(2,1)S(1)} %get-tuple-element.65.after_ref), custom_call_target="tpu_custom_call" | custom-call | bytes 8388608 | tf_op jit(solution)/shard_map/fetch_up/pallas_call | solution.py:61
  122.9 3.6 %all-to-all-start.5 = ((bf16[8,16,4096]{2,1,0:T(8,128)(2,1)}), bf16[8,16,4096]{2,1,0:T(8,128)(2,1)S(1)}, u32[]{:S(2)}, u32[]{:S(2)}) async-start(bf16[8,16,4096]{2,1,0:T(8,128)(2,1)} %bitcast.7.refs_2_), calls=%async_computation.5 | async-start | bytes 2097152 | tf_op jit(solution)/shard_map/all_to_all | solution.py:439
  126.4 7.5 %down.1 = (bf16[128,4096]{1,0:T(8,128)(2,1)S(1)}, bf16[128,4096]{1,0:T(8,128)(2,1)S(1)}) custom-call(bf16[256,1024]{1,0:T(8,128)(2,1)S(1)} %get-tuple-element.72.refs_0_, bf16[1024,4096]{1,0:T(8,128)(2,1)} %refs_1_.1, bf16[8,16,4096]{2,1,0:T(8,128)(2,1)} %bitcast.7.refs_2_), custom_call_target="tpu_custom_call" | custom-call | flops 2147483648 | bytes 8388608 | tf_op jit(solution)/shard_map/down/pallas_call | solution.py:38
  134.9 7.5 %all-to-all-done.5.refs_0_ = bf16[8,16,4096]{2,1,0:T(8,128)(2,1)S(1)} async-done(((bf16[8,16,4096]{2,1,0:T(8,128)(2,1)}), bf16[8,16,4096]{2,1,0:T(8,128)(2,1)S(1)}, u32[]{:S(2)}, u32[]{:S(2)}) %all-to-all-start.5) | async-done | bytes 1048608 | tf_op jit(solution)/shard_map/all_to_all | solution.py:439
  143.9 4.8 %all-to-all-start.6 = ((bf16[8,16,4096]{2,1,0:T(8,128)(2,1)}), bf16[8,16,4096]{2,1,0:T(8,128)(2,1)S(1)}, u32[]{:S(2)}, u32[]{:S(2)}) async-start(bf16[8,16,4096]{2,1,0:T(8,128)(2,1)} %get-tuple-element.74.after_ref), calls=%async_computation.6 | async-start | bytes 2097152 | tf_op jit(solution)/shard_map/all_to_all | solution.py:439
  152.4 12.1 %all-to-all-done.6 = bf16[8,16,4096]{2,1,0:T(8,128)(2,1)S(1)} async-done(((bf16[8,16,4096]{2,1,0:T(8,128)(2,1)}), bf16[8,16,4096]{2,1,0:T(8,128)(2,1)S(1)}, u32[]{:S(2)}, u32[]{:S(2)}) %all-to-all-start.6) | async-done | bytes 1048608 | tf_op jit(solution)/shard_map/all_to_all | solution.py:439
  167.9 9.2 %all_to_all.51.refs_3_ = bf16[8,64,128]{2,1,0:T(8,128)(2,1)S(1)} all-to-all(bf16[8,64,128]{2,1,0:T(8,128)(2,1)S(1)} %attn_out_grad.1), channel_id=1, replica_groups=mesh['section'=2,'seq'=8,'mp'=8] {'seq'}, dimensions={0} | all-to-all | bytes 262144 | tf_op jit(solution)/shard_map/all_to_all | solution.py:439
  177.1 4.1 %attention_grad.1 = bf16[8,320,128]{2,1,0:T(8,128)(2,1)} custom-call(bf16[8,320,128]{2,1,0:T(8,128)(2,1)S(1)} %copy-done.1, bf16[8,64,128]{2,1,0:T(8,128)(2,1)} %get-tuple-element.57.after_ref.refs_4_.refs_1_, f32[4,1,128]{2,1,0:T(1,128)S(1)} %get-tuple-element.58.refs_2_, bf16[8,64,128]{2,1,0:T(8,128)(2,1)S(1)} %all_to_all.51.refs_3_), custom_call_target="tpu_custom_call" | custom-call | flops 167772160 | tf_op jit(solution)/shard_map/attention_grad/pallas_call | solution.py:104
  181.3 3.6 %all-to-all-start.8 = ((bf16[8,320,128]{2,1,0:T(8,128)(2,1)}), bf16[8,320,128]{2,1,0:T(8,128)(2,1)S(1)}, u32[]{:S(2)}, u32[]{:S(2)}) async-start(bf16[8,320,128]{2,1,0:T(8,128)(2,1)} %attention_grad.1), calls=%async_computation.8 | async-start | bytes 1310720 | tf_op jit(solution)/shard_map/all_to_all | solution.py:439
  190.3 4.4 %collective-permute-done.13.refs_0_.refs_1_ = bf16[2,16,4096]{2,1,0:T(8,128)(2,1)S(1)} collective-permute-done((bf16[2,16,4096]{2,1,0:T(8,128)(2,1)}, bf16[2,16,4096]{2,1,0:T(8,128)(2,1)S(1)}, u32[]{:S(2)}, u32[]{:S(2)}) %collective-permute-start.13) | collective-permute-done | bytes 262176 | tf_op jit(solution)/shard_map/ppermute | solution.py:470
  194.7 5.3 %collective-permute-done.14.refs_1_.refs_2_ = bf16[2,16,4096]{2,1,0:T(8,128)(2,1)S(1)} collective-permute-done((bf16[2,16,4096]{2,1,0:T(8,128)(2,1)}, bf16[2,16,4096]{2,1,0:T(8,128)(2,1)S(1)}, u32[]{:S(2)}, u32[]{:S(2)}) %collective-permute-start.14) | collective-permute-done | bytes 262176 | tf_op jit(solution)/shard_map/ppermute | solution.py:470
  209.3 5.5 %all-to-all-start.9 = ((bf16[8,16,4096]{2,1,0:T(8,128)(2,1)}), bf16[8,16,4096]{2,1,0:T(8,128)(2,1)S(1)}, u32[]{:S(2)}, u32[]{:S(2)}) async-start(bf16[8,16,4096]{2,1,0:T(8,128)(2,1)} %bitcast.9), calls=%async_computation.9 | async-start | bytes 2097152 | tf_op jit(solution)/shard_map/all_to_all | solution.py:439
  214.9 3.5 %collective-permute-start.18 = (bf16[16,4096]{1,0:T(8,128)(2,1)S(1)}, bf16[16,4096]{1,0:T(8,128)(2,1)S(1)}, u32[]{:S(2)}, u32[]{:S(2)}) collective-permute-start(bf16[16,4096]{1,0:T(8,128)(2,1)S(1)} %get-tuple-element.99), channel_id=1, source_target_pairs={{0,4},{1,5},{2,6},{3,7},{4,0},{5,1},{6,2},{7,3},{8,12},{9,13},{10,... | collective-permute-start | bytes 393224 | tf_op jit(solution)/shard_map/ppermute | solution.py:464
  218.4 14.9 %collective-permute-done.18.refs_5_ = bf16[16,4096]{1,0:T(8,128)(2,1)S(1)} collective-permute-done((bf16[16,4096]{1,0:T(8,128)(2,1)S(1)}, bf16[16,4096]{1,0:T(8,128)(2,1)S(1)}, u32[]{:S(2)}, u32[]{:S(2)}) %collective-permute-start.18) | collective-permute-done | bytes 131104 | tf_op jit(solution)/shard_map/ppermute | solution.py:464
  (84 shorter events, 63.2 us)
Async XLA Ops:
  2.8 25.8 %all-to-all-start = ((bf16[8,16,4096]{2,1,0:T(8,128)(2,1)}), bf16[8,16,4096]{2,1,0:T(8,128)(2,1)S(1)}, u32[]{:S(2)}, u32[]{:S(2)}) async-start(bf16[8,16,4096]{2,1,0:T(8,128)(2,1)} %first_norm.1.after_ref), calls=%async_computation | async-start | bytes 2097152 | tf_op jit(solution)/shard_map/all_to_all | solution.py:439
  10.7 17.9 %collective-permute-start = (bf16[16,4096]{1,0:T(8,128)(2,1)}, bf16[16,4096]{1,0:T(8,128)(2,1)S(1)}, u32[]{:S(2)}, u32[]{:S(2)}) collective-permute-start(bf16[16,4096]{1,0:T(8,128)(2,1)} %bitcast.21), channel_id=1, source_target_pairs={{0,4},{1,5},{2,6},{3,7},{4,0},{5,1},{6,2},{7,3},{8,12},{9,13},{10,... | collective-permute-start | bytes 393224 | tf_op jit(solution)/shard_map/ppermute | solution.py:464
  28.6 2.8 %collective-permute-start.1 = (bf16[128,4096]{1,0:T(8,128)(2,1)S(1)}, bf16[128,4096]{1,0:T(8,128)(2,1)S(1)}, u32[]{:S(2)}, u32[]{:S(2)}) collective-permute-start(bf16[128,4096]{1,0:T(8,128)(2,1)S(1)} %bitcast.14), channel_id=1, source_target_pairs={{0,64},{64,0},{1,65},{65,1},{2,66},{66,2},{3,67},{67,3},{4,68},{68... | collective-permute-start | bytes 3145736 | tf_op jit(solution)/shard_map/ppermute | solution.py:435
  34.1 17.0 %all-to-all-start.1 = ((bf16[8,320,128]{2,1,0:T(8,128)(2,1)}), bf16[8,320,128]{2,1,0:T(8,128)(2,1)S(1)}, u32[]{:S(2)}, u32[]{:S(2)}) async-start(bf16[8,320,128]{2,1,0:T(8,128)(2,1)} %qkv.1), calls=%async_computation.1 | async-start | bytes 1310720 | tf_op jit(solution)/shard_map/all_to_all | solution.py:439
  38.9 19.3 %collective-permute-start.4 = (bf16[2,16,4096]{2,1,0:T(8,128)(2,1)S(1)}, bf16[2,16,4096]{2,1,0:T(8,128)(2,1)}, u32[]{:S(2)}, u32[]{:S(2)}) collective-permute-start(bf16[2,16,4096]{2,1,0:T(8,128)(2,1)S(1)} %pad_maximum_fusion.refs_0_), channel_id=1, source_target_pairs={{0,3},{1,0},{2,1},{3,2},{4,7},{5,4},{6,5},{7,6},{8,11},{9,8},{10,9... | collective-permute-start | bytes 786440 | tf_op jit(solution)/shard_map/ppermute | solution.py:470
  41.4 16.8 %collective-permute-start.3 = (bf16[2,16,4096]{2,1,0:T(8,128)(2,1)S(1)}, bf16[2,16,4096]{2,1,0:T(8,128)(2,1)}, u32[]{:S(2)}, u32[]{:S(2)}) collective-permute-start(bf16[2,16,4096]{2,1,0:T(8,128)(2,1)S(1)} %pad_maximum_fusion.refs_0_), channel_id=1, source_target_pairs={{0,2},{1,3},{2,0},{3,1},{4,6},{5,7},{6,4},{7,5},{8,10},{9,11},{10,... | collective-permute-start | bytes 786440 | tf_op jit(solution)/shard_map/ppermute | solution.py:470
  42.3 15.9 %collective-permute-start.2 = (bf16[2,16,4096]{2,1,0:T(8,128)(2,1)S(1)}, bf16[2,16,4096]{2,1,0:T(8,128)(2,1)}, u32[]{:S(2)}, u32[]{:S(2)}) collective-permute-start(bf16[2,16,4096]{2,1,0:T(8,128)(2,1)S(1)} %pad_maximum_fusion.refs_0_), channel_id=1, source_target_pairs={{0,1},{1,2},{2,3},{3,0},{4,5},{5,6},{6,7},{7,4},{8,9},{9,10},{10,1... | collective-permute-start | bytes 786440 | tf_op jit(solution)/shard_map/ppermute | solution.py:470
  53.2 10.0 %all-to-all-start.2 = ((bf16[8,64,128]{2,1,0:T(8,128)(2,1)}), bf16[8,64,128]{2,1,0:T(8,128)(2,1)S(1)}, u32[]{:S(2)}, u32[]{:S(2)}) async-start(bf16[8,64,128]{2,1,0:T(8,128)(2,1)} %get-tuple-element.57.after_ref.refs_4_.refs_1_), calls=%async_computation.2 | async-start | bytes 262144 | tf_op jit(solution)/shard_map/all_to_all | solution.py:439
  64.2 2.2 collective-permute-start.5
  64.8 7.4 %collective-permute-start.7 = (bf16[128,4096]{1,0:T(8,128)(2,1)S(1)}, bf16[128,4096]{1,0:T(8,128)(2,1)S(1)}, u32[]{:S(2)}, u32[]{:S(2)}) collective-permute-start(bf16[128,4096]{1,0:T(8,128)(2,1)S(1)} %join_cotangent.1.refs_2_.refs_0_), channel_id=1, source_target_pairs={{0,64},{64,0},{1,65},{65,1},{2,66},{66,2},{3,67},{67,3},{4,68},{68... | collective-permute-start | bytes 3145736 | tf_op jit(solution)/shard_map/ppermute | solution.py:435
  67.5 20.4 %all-to-all-start.3 = ((bf16[8,16,4096]{2,1,0:T(8,128)(2,1)}), bf16[8,16,4096]{2,1,0:T(8,128)(2,1)S(1)}, u32[]{:S(2)}, u32[]{:S(2)}) async-start(bf16[8,16,4096]{2,1,0:T(8,128)(2,1)} %bitcast.5.refs_3_), calls=%async_computation.3 | async-start | bytes 2097152 | tf_op jit(solution)/shard_map/all_to_all | solution.py:439
  110.1 3.4 %collective-permute-start.8 = (bf16[128,4096]{1,0:T(8,128)(2,1)S(1)}, bf16[128,4096]{1,0:T(8,128)(2,1)S(1)}, u32[]{:S(2)}, u32[]{:S(2)}) collective-permute-start(bf16[128,4096]{1,0:T(8,128)(2,1)S(1)} %bitcast.16), channel_id=1, source_target_pairs={{0,64},{64,0},{1,65},{65,1},{2,66},{66,2},{3,67},{67,3},{4,68},{68... | collective-permute-start | bytes 3145736 | tf_op jit(solution)/shard_map/ppermute | solution.py:435
  119.5 2.3 collective-permute-start.9
  122.9 19.5 %all-to-all-start.5 = ((bf16[8,16,4096]{2,1,0:T(8,128)(2,1)}), bf16[8,16,4096]{2,1,0:T(8,128)(2,1)S(1)}, u32[]{:S(2)}, u32[]{:S(2)}) async-start(bf16[8,16,4096]{2,1,0:T(8,128)(2,1)} %bitcast.7.refs_2_), calls=%async_computation.5 | async-start | bytes 2097152 | tf_op jit(solution)/shard_map/all_to_all | solution.py:439
  143.9 4.8 %collective-permute-start.11 = (bf16[128,4096]{1,0:T(8,128)(2,1)}, bf16[128,4096]{1,0:T(8,128)(2,1)}, u32[]{:S(2)}, u32[]{:S(2)}) collective-permute-start(bf16[128,4096]{1,0:T(8,128)(2,1)} %copy-done.7), channel_id=1, source_target_pairs={{0,64},{64,0},{1,65},{65,1},{2,66},{66,2},{3,67},{67,3},{4,68},{68... | collective-permute-start | bytes 3145736 | tf_op jit(solution)/shard_map/ppermute | solution.py:435
  143.9 20.6 %all-to-all-start.6 = ((bf16[8,16,4096]{2,1,0:T(8,128)(2,1)}), bf16[8,16,4096]{2,1,0:T(8,128)(2,1)S(1)}, u32[]{:S(2)}, u32[]{:S(2)}) async-start(bf16[8,16,4096]{2,1,0:T(8,128)(2,1)} %get-tuple-element.74.after_ref), calls=%async_computation.6 | async-start | bytes 2097152 | tf_op jit(solution)/shard_map/all_to_all | solution.py:439
  164.5 2.7 %collective-permute-start.12 = (bf16[128,4096]{1,0:T(8,128)(2,1)S(1)}, bf16[128,4096]{1,0:T(8,128)(2,1)S(1)}, u32[]{:S(2)}, u32[]{:S(2)}) collective-permute-start(bf16[128,4096]{1,0:T(8,128)(2,1)S(1)} %bitcast.12), channel_id=1, source_target_pairs={{0,64},{64,0},{1,65},{65,1},{2,66},{66,2},{3,67},{67,3},{4,68},{68... | collective-permute-start | bytes 3145736 | tf_op jit(solution)/shard_map/ppermute | solution.py:435
  181.3 18.9 %all-to-all-start.8 = ((bf16[8,320,128]{2,1,0:T(8,128)(2,1)}), bf16[8,320,128]{2,1,0:T(8,128)(2,1)S(1)}, u32[]{:S(2)}, u32[]{:S(2)}) async-start(bf16[8,320,128]{2,1,0:T(8,128)(2,1)} %attention_grad.1), calls=%async_computation.8 | async-start | bytes 1310720 | tf_op jit(solution)/shard_map/all_to_all | solution.py:439
  184.9 9.9 %collective-permute-start.13 = (bf16[2,16,4096]{2,1,0:T(8,128)(2,1)}, bf16[2,16,4096]{2,1,0:T(8,128)(2,1)S(1)}, u32[]{:S(2)}, u32[]{:S(2)}) collective-permute-start(bf16[2,16,4096]{2,1,0:T(8,128)(2,1)} %copy-done.10), channel_id=1, source_target_pairs={{0,1},{1,2},{2,3},{3,0},{4,5},{5,6},{6,7},{7,4},{8,9},{9,10},{10,1... | collective-permute-start | bytes 786440 | tf_op jit(solution)/shard_map/ppermute | solution.py:470
  186.2 13.9 %collective-permute-start.14 = (bf16[2,16,4096]{2,1,0:T(8,128)(2,1)}, bf16[2,16,4096]{2,1,0:T(8,128)(2,1)S(1)}, u32[]{:S(2)}, u32[]{:S(2)}) collective-permute-start(bf16[2,16,4096]{2,1,0:T(8,128)(2,1)} %copy-done.9), channel_id=1, source_target_pairs={{0,2},{1,3},{2,0},{3,1},{4,6},{5,7},{6,4},{7,5},{8,10},{9,11},{10,... | collective-permute-start | bytes 786440 | tf_op jit(solution)/shard_map/ppermute | solution.py:470
  189.0 11.1 %collective-permute-start.15 = (bf16[2,16,4096]{2,1,0:T(8,128)(2,1)}, bf16[2,16,4096]{2,1,0:T(8,128)(2,1)S(1)}, u32[]{:S(2)}, u32[]{:S(2)}) collective-permute-start(bf16[2,16,4096]{2,1,0:T(8,128)(2,1)} %copy-done.8), channel_id=1, source_target_pairs={{0,3},{1,0},{2,1},{3,2},{4,7},{5,4},{6,5},{7,6},{8,11},{9,8},{10,9... | collective-permute-start | bytes 786440 | tf_op jit(solution)/shard_map/ppermute | solution.py:470
  203.0 3.7 %collective-permute-start.17 = (bf16[128,2048]{1,0:T(8,128)(2,1)S(1)}, bf16[128,2048]{1,0:T(8,128)(2,1)S(1)}, u32[]{:S(2)}, u32[]{:S(2)}) collective-permute-start(bf16[128,2048]{1,0:T(8,128)(2,1)S(1)} %get-tuple-element.97), channel_id=1, source_target_pairs={{0,64},{64,0},{1,65},{65,1},{2,66},{66,2},{3,67},{67,3},{4,68},{68... | collective-permute-start | bytes 1572872 | tf_op jit(solution)/shard_map/ppermute | solution.py:435
  209.3 24.0 %all-to-all-start.9 = ((bf16[8,16,4096]{2,1,0:T(8,128)(2,1)}), bf16[8,16,4096]{2,1,0:T(8,128)(2,1)S(1)}, u32[]{:S(2)}, u32[]{:S(2)}) async-start(bf16[8,16,4096]{2,1,0:T(8,128)(2,1)} %bitcast.9), calls=%async_computation.9 | async-start | bytes 2097152 | tf_op jit(solution)/shard_map/all_to_all | solution.py:439
  214.9 18.5 %collective-permute-start.18 = (bf16[16,4096]{1,0:T(8,128)(2,1)S(1)}, bf16[16,4096]{1,0:T(8,128)(2,1)S(1)}, u32[]{:S(2)}, u32[]{:S(2)}) collective-permute-start(bf16[16,4096]{1,0:T(8,128)(2,1)S(1)} %get-tuple-element.99), channel_id=1, source_target_pairs={{0,4},{1,5},{2,6},{3,7},{4,0},{5,1},{6,2},{7,3},{8,12},{9,13},{10,... | collective-permute-start | bytes 393224 | tf_op jit(solution)/shard_map/ppermute | solution.py:464
  (15 other events, 85.6 us)

commit v6 on v5

--- a/solution.py
+++ b/solution.py
@@ -439,8 +439,12 @@
     return lax.all_to_all(data, axis, 0, 0)
 
 
-def by_columns(partial, half, width):
+def by_columns(partial, half, width, hold=None):
     sides = [partial(start) for start in (0, width // 2)]
+    if hold is not None:
+        own, other = sides[0]
+        other, hold[0] = lax.optimization_barrier((other, hold[0]))
+        sides[0] = own, other
     ins = []
     for own, other in sides:
         ins += [own, swap_section(other)]
@@ -628,6 +632,7 @@
     sum_far = shift_high(sum_far)
     got = exchange(send, "seq")
     vmem = pl.BlockSpec(memory_space=pltpu.VMEM)
+    hold = [sum_far]
 
     def qkv_grad(start):
         after = shifted if start == 0 else [sum_near]
@@ -647,13 +652,13 @@
             cost_estimate=pl.CostEstimate(flops=0, bytes_accessed=0, transcendentals=0),
         )(got, hbm(qkv_weight), *after)
 
-    parts = exchange(by_columns(qkv_grad, half, width).reshape(group, rows, width), "mp")
+    parts = exchange(by_columns(qkv_grad, half, width, hold).reshape(group, rows, width), "mp")
     grad_input, block_out = local_call(
         input_grad_body,
         "input_grad",
         [parts],
         [row_out, row_out],
-        late=[hbm(own_in), grad_resid, resid, sum_near, sum_far],
+        late=[hbm(own_in), grad_resid, resid, sum_near, hold[0]],
     )
     return (block_out[None], grad_input[None])
 

time: 237 us -> 239 us (level)
  blocking collectives: 30.9 us -> 54.1 us
  waiting for transfers between devices: 84.2 us -> 71.5 us
  starting transfers between devices: 57.3 us -> 50.4 us
    all_to_all x2 -> x3, blocking collectives: 30.9 us -> 54.1 us  [exchange(): return lax.all_to_all(data, axis, 0, 0)]
    ppermute x2, waiting for transfers between devices: 29.3 us -> 15.9 us  [shift_high(): lax.ppermute(data, 'mp', [(i, (i + size // 2) % size) for i in range(size)])]
    all_to_all x8 -> x7, starting transfers between devices: 38.1 us -> 32.5 us  [exchange(): return lax.all_to_all(data, axis, 0, 0)]
    all_to_all x8 -> x7, waiting for transfers between devices: 38.9 us -> 38.9 us  [exchange(): return lax.all_to_all(data, axis, 0, 0)]
  transfers between devices with their start and end apart: 27 -> 26, of which waited for: 15 -> 16; matrix products, arithmetic and copies ran while one was open for 0% -> 0% of each run, Pallas kernels for 14% -> 13%
where the time goes in v6:
time: 239 us; the launch traced here: 238 us
  waiting for transfers between devices  71.5 us (30%)
  Pallas kernels  55.1 us (23%)
  blocking collectives  54.1 us (23%)
  starting transfers between devices  50.4 us (21%)
  local copies, waits for them, and re-layouts  6.19 us (3%)
    all_to_all x3, blocking collectives, exchange(): return lax.all_to_all(data, axis, 0, 0)  54.1 us
    all_to_all x7, waiting for transfers between devices, exchange(): return lax.all_to_all(data, axis, 0, 0)  38.9 us
    all_to_all x7, starting transfers between devices, exchange(): return lax.all_to_all(data, axis, 0, 0)  32.5 us
    pallas_call x15, Pallas kernels, local_call(): pl.pallas_call(run, name=name, in_specs=[vmem] * count + [pl.BlockSpec(me...  23 us
    ppermute x2, waiting for transfers between devices, shift_high(): lax.ppermute(data, 'mp', [(i, (i + size // 2) % size) for i in range(size)])  15.9 us
    pallas_call x2, Pallas kernels, kernel_call(): pl.pallas_call(run, name=name, grid=grid, in_specs=in_specs, out_specs=ou...  13.2 us
    ppermute x6, starting transfers between devices, shift_low(): return lax.ppermute(data, 'mp', pairs)  9.88 us
    ppermute x6, waiting for transfers between devices, shift_low(): return lax.ppermute(data, 'mp', pairs)  9.73 us
  transfers between devices with their start and end apart: 26, of which 16 were waited for; matrix products, arithmetic and copies ran while one was open for 0% of the time, Pallas kernels for 13%

profile of v6, /device:TPU:0, one launch (start us, length us, event | category | flops | bytes accessed | tf_op | source)
XLA Modules:
  0.0 238.3 jit_solution(16819250141808274451)
XLA Ops:
  2.9 7.9 %all-to-all-start = ((bf16[8,16,4096]{2,1,0:T(8,128)(2,1)}), bf16[8,16,4096]{2,1,0:T(8,128)(2,1)S(1)}, u32[]{:S(2)}, u32[]{:S(2)}) async-start(bf16[8,16,4096]{2,1,0:T(8,128)(2,1)} %first_norm.1.after_ref), calls=%async_computation | async-start | bytes 2097152 | tf_op jit(solution)/shard_map/all_to_all | solution.py:439
  10.7 3.5 %collective-permute-start = (bf16[16,4096]{1,0:T(8,128)(2,1)}, bf16[16,4096]{1,0:T(8,128)(2,1)S(1)}, u32[]{:S(2)}, u32[]{:S(2)}) collective-permute-start(bf16[16,4096]{1,0:T(8,128)(2,1)} %bitcast.22), channel_id=1, source_target_pairs={{0,4},{1,5},{2,6},{3,7},{4,0},{5,1},{6,2},{7,3},{8,12},{9,13},{10,... | collective-permute-start | bytes 393224 | tf_op jit(solution)/shard_map/ppermute | solution.py:468
  14.2 14.4 %collective-permute-done = bf16[16,4096]{1,0:T(8,128)(2,1)S(1)} collective-permute-done((bf16[16,4096]{1,0:T(8,128)(2,1)}, bf16[16,4096]{1,0:T(8,128)(2,1)S(1)}, u32[]{:S(2)}, u32[]{:S(2)}) %collective-permute-start) | collective-permute-done | bytes 131104 | tf_op jit(solution)/shard_map/ppermute | solution.py:468
  28.6 2.8 %fetch_qkv.1.refs_2_ = bf16[3,4096,256]{2,1,0:T(8,128)(2,1)S(1)} custom-call(bf16[3,4096,256]{2,1,0:T(8,128)(2,1)} %w_ref.3, bf16[8,16,4096]{2,1,0:T(8,128)(2,1)} %first_norm.1.after_ref), custom_call_target="tpu_custom_call" | custom-call | bytes 6291456 | tf_op jit(solution)/shard_map/fetch_qkv/pallas_call | solution.py:61
  34.1 4.8 %all-to-all-start.1 = ((bf16[8,320,128]{2,1,0:T(8,128)(2,1)}), bf16[8,320,128]{2,1,0:T(8,128)(2,1)S(1)}, u32[]{:S(2)}, u32[]{:S(2)}) async-start(bf16[8,320,128]{2,1,0:T(8,128)(2,1)} %qkv.1), calls=%async_computation.1 | async-start | bytes 1310720 | tf_op jit(solution)/shard_map/all_to_all | solution.py:439
  43.3 7.8 %all-to-all-done.1.refs_0_ = bf16[8,320,128]{2,1,0:T(8,128)(2,1)S(1)} async-done(((bf16[8,320,128]{2,1,0:T(8,128)(2,1)}), bf16[8,320,128]{2,1,0:T(8,128)(2,1)S(1)}, u32[]{:S(2)}, u32[]{:S(2)}) %all-to-all-start.1) | async-done | bytes 655392 | tf_op jit(solution)/shard_map/all_to_all | solution.py:439
  53.2 3.4 %all-to-all-start.2 = ((bf16[8,64,128]{2,1,0:T(8,128)(2,1)}), bf16[8,64,128]{2,1,0:T(8,128)(2,1)S(1)}, u32[]{:S(2)}, u32[]{:S(2)}) async-start(bf16[8,64,128]{2,1,0:T(8,128)(2,1)} %get-tuple-element.59.after_ref.refs_4_.refs_1_), calls=%async_computation.2 | async-start | bytes 262144 | tf_op jit(solution)/shard_map/all_to_all | solution.py:439
  59.6 3.6 %all-to-all-done.2.refs_0_ = bf16[8,64,128]{2,1,0:T(8,128)(2,1)S(1)} async-done(((bf16[8,64,128]{2,1,0:T(8,128)(2,1)}), bf16[8,64,128]{2,1,0:T(8,128)(2,1)S(1)}, u32[]{:S(2)}, u32[]{:S(2)}) %all-to-all-start.2) | async-done | bytes 131104 | tf_op jit(solution)/shard_map/all_to_all | solution.py:439
  67.5 4.6 %all-to-all-start.3 = ((bf16[8,16,4096]{2,1,0:T(8,128)(2,1)}), bf16[8,16,4096]{2,1,0:T(8,128)(2,1)S(1)}, u32[]{:S(2)}, u32[]{:S(2)}) async-start(bf16[8,16,4096]{2,1,0:T(8,128)(2,1)} %bitcast.5.refs_3_), calls=%async_computation.3 | async-start | bytes 2097152 | tf_op jit(solution)/shard_map/all_to_all | solution.py:439
  74.4 5.7 %grad_act.1.refs_2_.refs_3_ = f32[256,1024]{1,0:T(8,128)S(1)} custom-call(bf16[128,4096]{1,0:T(8,128)(2,1)S(1)} %join_cotangent.1.refs_2_.refs_0_, bf16[128,4096]{1,0:T(8,128)(2,1)S(1)} %copy-done.5, bf16[1024,4096]{1,0:T(8,128)(2,1)} %refs_1_.1, bf16[8,16,4096]{2,1,0:T(8,128)(2,1)} %bitcast.5.refs_3_), custom_call_target="tpu_custom_call" | custom-call | flops 2147483648 | bytes 8388608 | tf_op jit(solution)/shard_map/grad_act/pallas_call | solution.py:38
  80.1 7.9 %all-to-all-done.3.refs_0_ = bf16[8,16,4096]{2,1,0:T(8,128)(2,1)S(1)} async-done(((bf16[8,16,4096]{2,1,0:T(8,128)(2,1)}), bf16[8,16,4096]{2,1,0:T(8,128)(2,1)S(1)}, u32[]{:S(2)}, u32[]{:S(2)}) %all-to-all-start.3) | async-done | bytes 1048608 | tf_op jit(solution)/shard_map/all_to_all | solution.py:439
  88.5 21.7 %all_to_all.50 = bf16[8,16,4096]{2,1,0:T(8,128)(2,1)S(1)} all-to-all(bf16[8,16,4096]{2,1,0:T(8,128)(2,1)S(1)} %get-tuple-element.67.after_ref), channel_id=1, replica_groups=mesh['section'=2,'seq'=8,'mp'=8] {'mp'}, dimensions={0} | all-to-all | bytes 2097152 | tf_op jit(solution)/shard_map/all_to_all | solution.py:439
  110.2 3.4 %fetch_up.1.refs_2_.refs_1_ = bf16[4096,1024]{1,0:T(8,128)(2,1)S(1)} custom-call(bf16[4096,1024]{1,0:T(8,128)(2,1)} %src_ref.6, bf16[8,16,4096]{2,1,0:T(8,128)(2,1)S(1)} %get-tuple-element.67.after_ref), custom_call_target="tpu_custom_call" | custom-call | bytes 8388608 | tf_op jit(solution)/shard_map/fetch_up/pallas_call | solution.py:61
  122.9 3.6 %all-to-all-start.5 = ((bf16[8,16,4096]{2,1,0:T(8,128)(2,1)}), bf16[8,16,4096]{2,1,0:T(8,128)(2,1)S(1)}, u32[]{:S(2)}, u32[]{:S(2)}) async-start(bf16[8,16,4096]{2,1,0:T(8,128)(2,1)} %bitcast.7.refs_2_), calls=%async_computation.5 | async-start | bytes 2097152 | tf_op jit(solution)/shard_map/all_to_all | solution.py:439
  126.5 7.4 %down.1 = (bf16[128,4096]{1,0:T(8,128)(2,1)S(1)}, bf16[128,4096]{1,0:T(8,128)(2,1)S(1)}) custom-call(bf16[256,1024]{1,0:T(8,128)(2,1)S(1)} %get-tuple-element.74.refs_0_, bf16[1024,4096]{1,0:T(8,128)(2,1)} %refs_1_.1, bf16[8,16,4096]{2,1,0:T(8,128)(2,1)} %bitcast.7.refs_2_), custom_call_target="tpu_custom_call" | custom-call | flops 2147483648 | bytes 8388608 | tf_op jit(solution)/shard_map/down/pallas_call | solution.py:38
  134.9 7.5 %all-to-all-done.5.refs_0_ = bf16[8,16,4096]{2,1,0:T(8,128)(2,1)S(1)} async-done(((bf16[8,16,4096]{2,1,0:T(8,128)(2,1)}), bf16[8,16,4096]{2,1,0:T(8,128)(2,1)S(1)}, u32[]{:S(2)}, u32[]{:S(2)}) %all-to-all-start.5) | async-done | bytes 1048608 | tf_op jit(solution)/shard_map/all_to_all | solution.py:439
  144.0 4.8 %all-to-all-start.6 = ((bf16[8,16,4096]{2,1,0:T(8,128)(2,1)}), bf16[8,16,4096]{2,1,0:T(8,128)(2,1)S(1)}, u32[]{:S(2)}, u32[]{:S(2)}) async-start(bf16[8,16,4096]{2,1,0:T(8,128)(2,1)} %get-tuple-element.76.after_ref), calls=%async_computation.6 | async-start | bytes 2097152 | tf_op jit(solution)/shard_map/all_to_all | solution.py:439
  152.4 12.1 %all-to-all-done.6 = bf16[8,16,4096]{2,1,0:T(8,128)(2,1)S(1)} async-done(((bf16[8,16,4096]{2,1,0:T(8,128)(2,1)}), bf16[8,16,4096]{2,1,0:T(8,128)(2,1)S(1)}, u32[]{:S(2)}, u32[]{:S(2)}) %all-to-all-start.6) | async-done | bytes 1048608 | tf_op jit(solution)/shard_map/all_to_all | solution.py:439
  168.0 9.2 %all_to_all.51.refs_3_ = bf16[8,64,128]{2,1,0:T(8,128)(2,1)S(1)} all-to-all(bf16[8,64,128]{2,1,0:T(8,128)(2,1)S(1)} %attn_out_grad.1), channel_id=1, replica_groups=mesh['section'=2,'seq'=8,'mp'=8] {'seq'}, dimensions={0} | all-to-all | bytes 262144 | tf_op jit(solution)/shard_map/all_to_all | solution.py:439
  177.2 4.1 %attention_grad.1 = bf16[8,320,128]{2,1,0:T(8,128)(2,1)} custom-call(bf16[8,320,128]{2,1,0:T(8,128)(2,1)S(1)} %copy-done.1, bf16[8,64,128]{2,1,0:T(8,128)(2,1)} %get-tuple-element.59.after_ref.refs_4_.refs_1_, f32[4,1,128]{2,1,0:T(1,128)S(1)} %get-tuple-element.60.refs_2_, bf16[8,64,128]{2,1,0:T(8,128)(2,1)S(1)} %all_to_all.51.refs_3_), custom_call_target="tpu_custom_call" | custom-call | flops 167772160 | tf_op jit(solution)/shard_map/attention_grad/pallas_call | solution.py:104
  181.3 3.6 %all-to-all-start.8 = ((bf16[8,320,128]{2,1,0:T(8,128)(2,1)}), bf16[8,320,128]{2,1,0:T(8,128)(2,1)S(1)}, u32[]{:S(2)}, u32[]{:S(2)}) async-start(bf16[8,320,128]{2,1,0:T(8,128)(2,1)} %attention_grad.1), calls=%async_computation.8 | async-start | bytes 1310720 | tf_op jit(solution)/shard_map/all_to_all | solution.py:439
  190.4 4.4 %collective-permute-done.13.refs_0_.refs_1_ = bf16[2,16,4096]{2,1,0:T(8,128)(2,1)S(1)} collective-permute-done((bf16[2,16,4096]{2,1,0:T(8,128)(2,1)}, bf16[2,16,4096]{2,1,0:T(8,128)(2,1)S(1)}, u32[]{:S(2)}, u32[]{:S(2)}) %collective-permute-start.13) | collective-permute-done | bytes 262176 | tf_op jit(solution)/shard_map/ppermute | solution.py:474
  194.8 5.3 %collective-permute-done.14.refs_1_.refs_2_ = bf16[2,16,4096]{2,1,0:T(8,128)(2,1)S(1)} collective-permute-done((bf16[2,16,4096]{2,1,0:T(8,128)(2,1)}, bf16[2,16,4096]{2,1,0:T(8,128)(2,1)S(1)}, u32[]{:S(2)}, u32[]{:S(2)}) %collective-permute-start.14) | collective-permute-done | bytes 262176 | tf_op jit(solution)/shard_map/ppermute | solution.py:474
  212.9 23.2 %all_to_all.52.refs_0_ = bf16[8,16,4096]{2,1,0:T(8,128)(2,1)S(1)} all-to-all(bf16[8,16,4096]{2,1,0:T(8,128)(2,1)S(1)} %bitcast.16), channel_id=1, replica_groups=mesh['section'=2,'seq'=8,'mp'=8] {'mp'}, dimensions={0} | all-to-all | bytes 2097152 | tf_op jit(solution)/shard_map/all_to_all | solution.py:439
  (83 shorter events, 60.6 us)
Async XLA Ops:
  2.9 25.8 %all-to-all-start = ((bf16[8,16,4096]{2,1,0:T(8,128)(2,1)}), bf16[8,16,4096]{2,1,0:T(8,128)(2,1)S(1)}, u32[]{:S(2)}, u32[]{:S(2)}) async-start(bf16[8,16,4096]{2,1,0:T(8,128)(2,1)} %first_norm.1.after_ref), calls=%async_computation | async-start | bytes 2097152 | tf_op jit(solution)/shard_map/all_to_all | solution.py:439
  10.7 17.9 %collective-permute-start = (bf16[16,4096]{1,0:T(8,128)(2,1)}, bf16[16,4096]{1,0:T(8,128)(2,1)S(1)}, u32[]{:S(2)}, u32[]{:S(2)}) collective-permute-start(bf16[16,4096]{1,0:T(8,128)(2,1)} %bitcast.22), channel_id=1, source_target_pairs={{0,4},{1,5},{2,6},{3,7},{4,0},{5,1},{6,2},{7,3},{8,12},{9,13},{10,... | collective-permute-start | bytes 393224 | tf_op jit(solution)/shard_map/ppermute | solution.py:468
  28.6 2.8 %collective-permute-start.1 = (bf16[128,4096]{1,0:T(8,128)(2,1)S(1)}, bf16[128,4096]{1,0:T(8,128)(2,1)S(1)}, u32[]{:S(2)}, u32[]{:S(2)}) collective-permute-start(bf16[128,4096]{1,0:T(8,128)(2,1)S(1)} %bitcast.14), channel_id=1, source_target_pairs={{0,64},{64,0},{1,65},{65,1},{2,66},{66,2},{3,67},{67,3},{4,68},{68... | collective-permute-start | bytes 3145736 | tf_op jit(solution)/shard_map/ppermute | solution.py:435
  34.1 17.0 %all-to-all-start.1 = ((bf16[8,320,128]{2,1,0:T(8,128)(2,1)}), bf16[8,320,128]{2,1,0:T(8,128)(2,1)S(1)}, u32[]{:S(2)}, u32[]{:S(2)}) async-start(bf16[8,320,128]{2,1,0:T(8,128)(2,1)} %qkv.1), calls=%async_computation.1 | async-start | bytes 1310720 | tf_op jit(solution)/shard_map/all_to_all | solution.py:439
  38.9 19.3 %collective-permute-start.4 = (bf16[2,16,4096]{2,1,0:T(8,128)(2,1)S(1)}, bf16[2,16,4096]{2,1,0:T(8,128)(2,1)}, u32[]{:S(2)}, u32[]{:S(2)}) collective-permute-start(bf16[2,16,4096]{2,1,0:T(8,128)(2,1)S(1)} %pad_maximum_fusion.refs_0_), channel_id=1, source_target_pairs={{0,3},{1,0},{2,1},{3,2},{4,7},{5,4},{6,5},{7,6},{8,11},{9,8},{10,9... | collective-permute-start | bytes 786440 | tf_op jit(solution)/shard_map/ppermute | solution.py:474
  41.4 16.8 %collective-permute-start.3 = (bf16[2,16,4096]{2,1,0:T(8,128)(2,1)S(1)}, bf16[2,16,4096]{2,1,0:T(8,128)(2,1)}, u32[]{:S(2)}, u32[]{:S(2)}) collective-permute-start(bf16[2,16,4096]{2,1,0:T(8,128)(2,1)S(1)} %pad_maximum_fusion.refs_0_), channel_id=1, source_target_pairs={{0,2},{1,3},{2,0},{3,1},{4,6},{5,7},{6,4},{7,5},{8,10},{9,11},{10,... | collective-permute-start | bytes 786440 | tf_op jit(solution)/shard_map/ppermute | solution.py:474
  42.3 15.9 %collective-permute-start.2 = (bf16[2,16,4096]{2,1,0:T(8,128)(2,1)S(1)}, bf16[2,16,4096]{2,1,0:T(8,128)(2,1)}, u32[]{:S(2)}, u32[]{:S(2)}) collective-permute-start(bf16[2,16,4096]{2,1,0:T(8,128)(2,1)S(1)} %pad_maximum_fusion.refs_0_), channel_id=1, source_target_pairs={{0,1},{1,2},{2,3},{3,0},{4,5},{5,6},{6,7},{7,4},{8,9},{9,10},{10,1... | collective-permute-start | bytes 786440 | tf_op jit(solution)/shard_map/ppermute | solution.py:474
  53.2 10.0 %all-to-all-start.2 = ((bf16[8,64,128]{2,1,0:T(8,128)(2,1)}), bf16[8,64,128]{2,1,0:T(8,128)(2,1)S(1)}, u32[]{:S(2)}, u32[]{:S(2)}) async-start(bf16[8,64,128]{2,1,0:T(8,128)(2,1)} %get-tuple-element.59.after_ref.refs_4_.refs_1_), calls=%async_computation.2 | async-start | bytes 262144 | tf_op jit(solution)/shard_map/all_to_all | solution.py:439
  64.2 2.2 collective-permute-start.5
  64.8 7.4 %collective-permute-start.7 = (bf16[128,4096]{1,0:T(8,128)(2,1)S(1)}, bf16[128,4096]{1,0:T(8,128)(2,1)S(1)}, u32[]{:S(2)}, u32[]{:S(2)}) collective-permute-start(bf16[128,4096]{1,0:T(8,128)(2,1)S(1)} %join_cotangent.1.refs_2_.refs_0_), channel_id=1, source_target_pairs={{0,64},{64,0},{1,65},{65,1},{2,66},{66,2},{3,67},{67,3},{4,68},{68... | collective-permute-start | bytes 3145736 | tf_op jit(solution)/shard_map/ppermute | solution.py:435
  67.5 20.5 %all-to-all-start.3 = ((bf16[8,16,4096]{2,1,0:T(8,128)(2,1)}), bf16[8,16,4096]{2,1,0:T(8,128)(2,1)S(1)}, u32[]{:S(2)}, u32[]{:S(2)}) async-start(bf16[8,16,4096]{2,1,0:T(8,128)(2,1)} %bitcast.5.refs_3_), calls=%async_computation.3 | async-start | bytes 2097152 | tf_op jit(solution)/shard_map/all_to_all | solution.py:439
  110.2 3.4 %collective-permute-start.8 = (bf16[128,4096]{1,0:T(8,128)(2,1)S(1)}, bf16[128,4096]{1,0:T(8,128)(2,1)S(1)}, u32[]{:S(2)}, u32[]{:S(2)}) collective-permute-start(bf16[128,4096]{1,0:T(8,128)(2,1)S(1)} %bitcast.17), channel_id=1, source_target_pairs={{0,64},{64,0},{1,65},{65,1},{2,66},{66,2},{3,67},{67,3},{4,68},{68... | collective-permute-start | bytes 3145736 | tf_op jit(solution)/shard_map/ppermute | solution.py:435
  118.9 2.1 collective-permute-start.10
  119.5 2.3 collective-permute-start.9
  122.9 19.5 %all-to-all-start.5 = ((bf16[8,16,4096]{2,1,0:T(8,128)(2,1)}), bf16[8,16,4096]{2,1,0:T(8,128)(2,1)S(1)}, u32[]{:S(2)}, u32[]{:S(2)}) async-start(bf16[8,16,4096]{2,1,0:T(8,128)(2,1)} %bitcast.7.refs_2_), calls=%async_computation.5 | async-start | bytes 2097152 | tf_op jit(solution)/shard_map/all_to_all | solution.py:439
  144.0 4.8 %collective-permute-start.11 = (bf16[128,4096]{1,0:T(8,128)(2,1)}, bf16[128,4096]{1,0:T(8,128)(2,1)}, u32[]{:S(2)}, u32[]{:S(2)}) collective-permute-start(bf16[128,4096]{1,0:T(8,128)(2,1)} %copy-done.7), channel_id=1, source_target_pairs={{0,64},{64,0},{1,65},{65,1},{2,66},{66,2},{3,67},{67,3},{4,68},{68... | collective-permute-start | bytes 3145736 | tf_op jit(solution)/shard_map/ppermute | solution.py:435
  144.0 20.6 %all-to-all-start.6 = ((bf16[8,16,4096]{2,1,0:T(8,128)(2,1)}), bf16[8,16,4096]{2,1,0:T(8,128)(2,1)S(1)}, u32[]{:S(2)}, u32[]{:S(2)}) async-start(bf16[8,16,4096]{2,1,0:T(8,128)(2,1)} %get-tuple-element.76.after_ref), calls=%async_computation.6 | async-start | bytes 2097152 | tf_op jit(solution)/shard_map/all_to_all | solution.py:439
  164.6 2.7 %collective-permute-start.12 = (bf16[128,4096]{1,0:T(8,128)(2,1)S(1)}, bf16[128,4096]{1,0:T(8,128)(2,1)S(1)}, u32[]{:S(2)}, u32[]{:S(2)}) collective-permute-start(bf16[128,4096]{1,0:T(8,128)(2,1)S(1)} %bitcast.12), channel_id=1, source_target_pairs={{0,64},{64,0},{1,65},{65,1},{2,66},{66,2},{3,67},{67,3},{4,68},{68... | collective-permute-start | bytes 3145736 | tf_op jit(solution)/shard_map/ppermute | solution.py:435
  181.3 21.4 %all-to-all-start.8 = ((bf16[8,320,128]{2,1,0:T(8,128)(2,1)}), bf16[8,320,128]{2,1,0:T(8,128)(2,1)S(1)}, u32[]{:S(2)}, u32[]{:S(2)}) async-start(bf16[8,320,128]{2,1,0:T(8,128)(2,1)} %attention_grad.1), calls=%async_computation.8 | async-start | bytes 1310720 | tf_op jit(solution)/shard_map/all_to_all | solution.py:439
  184.9 9.9 %collective-permute-start.13 = (bf16[2,16,4096]{2,1,0:T(8,128)(2,1)}, bf16[2,16,4096]{2,1,0:T(8,128)(2,1)S(1)}, u32[]{:S(2)}, u32[]{:S(2)}) collective-permute-start(bf16[2,16,4096]{2,1,0:T(8,128)(2,1)} %copy-done.10), channel_id=1, source_target_pairs={{0,1},{1,2},{2,3},{3,0},{4,5},{5,6},{6,7},{7,4},{8,9},{9,10},{10,1... | collective-permute-start | bytes 786440 | tf_op jit(solution)/shard_map/ppermute | solution.py:474
  186.3 13.9 %collective-permute-start.14 = (bf16[2,16,4096]{2,1,0:T(8,128)(2,1)}, bf16[2,16,4096]{2,1,0:T(8,128)(2,1)S(1)}, u32[]{:S(2)}, u32[]{:S(2)}) collective-permute-start(bf16[2,16,4096]{2,1,0:T(8,128)(2,1)} %copy-done.9), channel_id=1, source_target_pairs={{0,2},{1,3},{2,0},{3,1},{4,6},{5,7},{6,4},{7,5},{8,10},{9,11},{10,... | collective-permute-start | bytes 786440 | tf_op jit(solution)/shard_map/ppermute | solution.py:474
  189.0 11.1 %collective-permute-start.15 = (bf16[2,16,4096]{2,1,0:T(8,128)(2,1)}, bf16[2,16,4096]{2,1,0:T(8,128)(2,1)S(1)}, u32[]{:S(2)}, u32[]{:S(2)}) collective-permute-start(bf16[2,16,4096]{2,1,0:T(8,128)(2,1)} %copy-done.8), channel_id=1, source_target_pairs={{0,3},{1,0},{2,1},{3,2},{4,7},{5,4},{6,5},{7,6},{8,11},{9,8},{10,9... | collective-permute-start | bytes 786440 | tf_op jit(solution)/shard_map/ppermute | solution.py:474
  200.2 6.8 %collective-permute-start.16 = (bf16[16,4096]{1,0:T(8,128)(2,1)S(1)}, bf16[16,4096]{1,0:T(8,128)(2,1)S(1)}, u32[]{:S(2)}, u32[]{:S(2)}) collective-permute-start(bf16[16,4096]{1,0:T(8,128)(2,1)S(1)} %get-tuple-element.97), channel_id=1, source_target_pairs={{0,4},{1,5},{2,6},{3,7},{4,0},{5,1},{6,2},{7,3},{8,12},{9,13},{10,... | collective-permute-start | bytes 393224 | tf_op jit(solution)/shard_map/ppermute | solution.py:468
  209.9 2.6 %collective-permute-start.17 = (bf16[128,2048]{1,0:T(8,128)(2,1)S(1)}, bf16[128,2048]{1,0:T(8,128)(2,1)S(1)}, u32[]{:S(2)}, u32[]{:S(2)}) collective-permute-start(bf16[128,2048]{1,0:T(8,128)(2,1)S(1)} %get-tuple-element.98), channel_id=1, source_target_pairs={{0,64},{64,0},{1,65},{65,1},{2,66},{66,2},{3,67},{67,3},{4,68},{68... | collective-permute-start | bytes 1572872 | tf_op jit(solution)/shard_map/ppermute | solution.py:435
  (14 other events, 83.4 us)
